TPU v7x, 128 devices: a whole 4x4x4 slice. The times are simulated.
128 devices in a mesh: tm: 32 (over x, z_lo, y), fsdp: 4 (over z_hi, core).
Axes of the slice: x: 4, y: 4, z: 4 (z_hi: 2, z_lo: 2; z = z_hi * 2 + z_lo), core: 2. Of those that a mesh axis runs over, the one named last changes fastest.
Arguments:
- latents: bfloat16 [24576, 4096], P('tm'), may hold values from -64 to 64
- out_grads: bfloat16 [24576, 8192], P('tm', 'fsdp'), may hold values from -0.64 to 0.64
- eig_in: float32 [8, 512, 512], replicated, may hold values from -0.25 to 0.25
- eig_out: float32 [16, 512, 512], P('fsdp'), may hold values from -0.25 to 0.25
- owner_table: int32 [32], replicated, may hold values from 0 to 31, each once
Outputs:
- update: float32 [4, 32, 512, 512], P(None, 'tm')
Inputs may be any that keep to these rules, and one draw needn't show every extreme that they name: `owner_table`: every block number 0 to 31 stands exactly once.
All inputs are finite; a program needn't handle non-finite values.
Results may differ from a plain program's by a relative error of at most 0.0003.
Values sent between devices are 32-bit elements; how exact they have to be, the bound alone decides.
No kernel may reach another device: no remote copies, remote signals or barrier semaphores. Data moves between devices by JAX's collectives and lax.ppermute only.
A program may use at most 256 MiB of HBM per device.

v0:
```python
import jax
import jax.numpy as jnp
from jax import lax
from jax.sharding import PartitionSpec as P

DAMPING = 0.0001
HIGH_ACCURACY = lax.Precision.HIGHEST


def on_device(latents, out_grads, eig_in, eig_out, owner_table):
    tok_rows = latents.shape[0]
    block_size = eig_in.shape[1]
    in_blocks = eig_in.shape[0]
    col_blocks = eig_out.shape[0]
    tokens_all = tok_rows * lax.axis_size("tm")
    per_owner = owner_table.shape[0] // lax.axis_size("tm")
    input_partition = latents.reshape(tok_rows, in_blocks, block_size)
    output_partition = out_grads.reshape(tok_rows, col_blocks, block_size)
    left = jnp.take(input_partition, owner_table // col_blocks, axis=1)
    right = jnp.take(output_partition, owner_table % col_blocks, axis=1)
    grad_owned = (
        lax.psum_scatter(
            jnp.einsum("tcb,tce->cbe", left, right, preferred_element_type=jnp.float32),
            "tm",
            scatter_dimension=0,
            tiled=True,
        )
        / tokens_all
    )
    proj_in = jnp.einsum(
        "tab,abk->tak",
        input_partition,
        eig_in,
        precision=HIGH_ACCURACY,
        preferred_element_type=jnp.float32,
    )
    proj_out = jnp.einsum(
        "tab,abk->tak",
        output_partition,
        eig_out,
        precision=HIGH_ACCURACY,
        preferred_element_type=jnp.float32,
    )
    sums_in, sums_out = lax.psum(
        (jnp.sum(proj_in * proj_in, axis=0), jnp.sum(proj_out * proj_out, axis=0)), "tm"
    )
    eigen_in = sums_in / tokens_all
    eigen_out = sums_out / tokens_all
    my_slots = lax.dynamic_slice_in_dim(owner_table, lax.axis_index("tm") * per_owner, per_owner)
    row_ids = my_slots // col_blocks
    col_ids = my_slots % col_blocks
    basis_in = jnp.take(eig_in, row_ids, axis=0)
    basis_out = jnp.take(eig_out, col_ids, axis=0)
    values_in = jnp.take(eigen_in, row_ids, axis=0)
    values_out = jnp.take(eigen_out, col_ids, axis=0)
    rotated = jnp.einsum("cba,cbe->cae", basis_in, grad_owned, precision=HIGH_ACCURACY)
    rotated = jnp.einsum("cae,cek->cak", rotated, basis_out, precision=HIGH_ACCURACY)
    scaled = rotated / (values_in[:, :, None] * values_out[:, None, :] + DAMPING)
    back = jnp.einsum("cab,cbk->cak", basis_in, scaled, precision=HIGH_ACCURACY)
    result = jnp.einsum("cak,cek->cae", back, basis_out, precision=HIGH_ACCURACY)
    return lax.all_gather(result[None], "fsdp", axis=0, tiled=True)


def solution(mesh):
    in_specs = (P("tm", None), P("tm", "fsdp"), P(), P("fsdp", None, None), P())
    out_specs = P(None, "tm", None, None)
    return jax.shard_map(
        on_device, mesh=mesh, in_specs=in_specs, out_specs=out_specs, check_vma=False
    )
```

profile of v0, /device:TPU:1, one launch (start us, length us, event | category | flops | bytes accessed | tf_op | source)
XLA Modules:
  0.0 516.1 jit_solution(9151039081616112342)
XLA Ops:
  6.5 0.0 reduce-scatter.2.cloned.1.call-start
  6.5 0.7 compare_and_fusion.1
  7.2 4.6 copy.18
  11.8 3.2 copy.19
  15.0 8.7 %copy.16 = bf16[768,4096]{0,1:T(8,128)(2,1)} copy(bf16[768,4096]{1,0:T(8,128)(2,1)} %param.5) | data formatting | bytes 12582912 | tf_op args[0]
  23.7 8.7 %copy.17 = bf16[768,8,512]{2,0,1:T(8,128)(2,1)} copy(bf16[768,8,512]{0,2,1:T(8,128)(2,1)} %bitcast.37) | data formatting | bytes 12582912 | tf_op jit(solution)/shard_map/reshape | solution.py:17
  32.4 13.0 %gather_fusion = bf16[32,768,512]{2,1,0:T(8,128)(2,1)} fusion(bf16[768,8,512]{2,0,1:T(8,128)(2,1)} %copy.17, s32[1024]{0:T(1024)S(1)} %get-tuple-element.58), kind=kCustom, calls=%fused_computation | custom fusion | bytes 50331776 | tf_op jit(solution)/shard_map/jit(_take)/gather | solution.py:19
  45.4 10.0 %gather_fusion.1 = bf16[32,768,512]{2,1,0:T(8,128)(2,1)} fusion(bf16[768,4,512]{2,0,1:T(8,128)(2,1)S(1)} %copy.19, s32[1024]{0:T(1024)S(1)} %get-tuple-element.57), kind=kCustom, calls=%fused_computation.1 | custom fusion | bytes 50331776 | tf_op jit(solution)/shard_map/jit(_take)/gather | solution.py:20
  55.4 29.2 %fusion = f32[32,512,512]{2,1,0:T(8,128)} fusion(bf16[32,768,512]{2,1,0:T(8,128)(2,1)} %gather_fusion.1, bf16[32,768,512]{2,1,0:T(8,128)(2,1)} %gather_fusion, pred[32]{0:T(512)(128)(4,1)S(1)} %get-tuple-element.55, pred[32]{0:T(512)(128)(4,1)S(1)} %get-tuple-element.51), kind=kOutput, calls=%fused_computation.2 | convolution fusion | flops 12910067712 | bytes 83886144 | tf_op jit(solution)/shard_map/tcb,tce->cbe/dot_general | solution.py:23
  84.5 0.0 copy-start.1
  84.5 0.0 copy-start
  84.5 0.0 reduce-scatter.2.cloned.1.call-update
  84.6 0.2 all-gather.3.cloned.1.call-start
  84.8 0.4 copy-done.1
  85.2 0.6 dynamic_slice.3
  88.4 0.0 copy-done
  88.4 13.1 %multiply_reduce_fusion.1 = f32[4,512]{1,0:T(4,128)S(1)} fusion(f32[4,512,512]{2,1,0:T(8,128)} %param.8, bf16[768,4,512]{0,2,1:T(8,128)(2,1)S(1)} %bitcast.40), kind=kOutput, calls=%fused_computation.11 | convolution fusion | flops 9666820096 | bytes 7348224 | tf_op jit(solution)/shard_map/tab,abk->tak/dot_general | solution.py:37
  101.5 14.6 %multiply_reduce_fusion = f32[8,512]{1,0:T(8,128)S(1)} fusion(f32[8,512,512]{2,1,0:T(8,128)} %param.7, bf16[768,8,512]{0,2,1:T(8,128)(2,1)} %bitcast.38), kind=kOutput, calls=%fused_computation.10 | convolution fusion | flops 19333640192 | bytes 14696448 | tf_op jit(solution)/shard_map/tab,abk->tak/dot_general | solution.py:30
  116.1 152.4 %all-reduce = (f32[4,512]{1,0:T(4,128)S(1)}, f32[8,512]{1,0:T(8,128)S(1)}) all-reduce(f32[4,512]{1,0:T(4,128)S(1)} %multiply_reduce_fusion.1, f32[8,512]{1,0:T(8,128)S(1)} %multiply_reduce_fusion), channel_id=1, replica_groups=mesh['tm'=32,'fsdp'=4] {'tm'}, use_global_device_ids=true, to_apply=%region_4.5 | all-reduce | flops 6144 | bytes 49152 | tf_op jit(solution)/shard_map/psum | solution.py:44
  268.5 186.8 %reduce-scatter.2.cloned.1.call-done = f32[1,512,512]{2,1,0:T(8,128)} async-done(((f32[32,512,512]{2,1,0:T(8,128)}), f32[1,512,512]{2,1,0:T(8,128)}) %reduce-scatter.2.cloned.1.call-update) | async-done | bytes 1048592 | tf_op jit(solution)/shard_map/reduce_scatter | solution.py:22
  455.3 3.4 fusion.11
  458.8 3.1 convolution_divide_fusion
  461.9 3.1 fusion.13
  465.0 4.1 fusion.8
  469.0 0.0 all-gather.3.cloned.1.call-update
  469.0 35.6 %all-gather.3.cloned.1.call-done = f32[2048,512]{1,0:T(8,128)} async-done(((f32[512,512]{1,0:T(8,128)}), f32[2048,512]{1,0:T(8,128)}) %all-gather.3.cloned.1.call-update) | async-done | bytes 4194320 | tf_op jit(solution)/shard_map/all_gather | solution.py:61
  504.6 4.6 copy.32
  (2 shorter events, 0.0 us)
Async XLA Ops:
  6.5 448.8 %reduce-scatter.2.cloned.1.call-start = ((), (), s32[]{:S(2)}) async-start(), calls=%async_computation.1 | async-start | bytes 34603008 | tf_op jit(solution)/shard_map/reduce_scatter | solution.py:22
  84.5 0.7 copy-start.1
  84.5 3.8 copy-start
  84.6 420.1 %all-gather.3.cloned.1.call-start = ((), (), s32[]{:S(2)}) async-start(), calls=%async_computation.2 | async-start | bytes 5242880 | tf_op jit(solution)/shard_map/all_gather | solution.py:61
Sparse Core Ops, SparseCore 0:
  84.7 370.6 reduce-scatter.1
  469.2 35.4 all-gather.2
where the time goes:
time: 517 us; the launch traced here: 516 us
  waiting for transfers between devices  222 us (43%)
  blocking collectives  152 us (29%)
  matrix products  70.6 us (14%)
  local copies, waits for them, and re-layouts  53.8 us (10%)
  between operations  16.1 us (3%)
    reduce_scatter x1, waiting for transfers between devices, on_device(): lax.psum_scatter(jnp.einsum('tcb,tce->cbe', left, right, preferred_elemen...  187 us
    psum x1, blocking collectives, on_device(): lax.psum((jnp.sum(proj_in * proj_in, axis=0), jnp.sum(proj_out * proj_out...  152 us
    all_gather x1, waiting for transfers between devices, on_device(): return lax.all_gather(result[None], 'fsdp', axis=0, tiled=True)  35.6 us
    dot_general x1, matrix products, on_device(): jnp.einsum('tcb,tce->cbe', left, right, preferred_element_type=jnp.float32)  29.2 us
    unnamed x7, local copies, waits for them, and re-layouts  18.4 us
    dot_general x1, matrix products, on_device(): jnp.einsum('tab,abk->tak', input_partition, eig_in, precision=HIGH_ACCURA...  14.6 us
    dot_general x1, matrix products, on_device(): jnp.einsum('tab,abk->tak', output_partition, eig_out, precision=HIGH_ACCU...  13.1 us
    gather x1, local copies, waits for them, and re-layouts, on_device(): left = jnp.take(input_partition, owner_table // col_blocks, axis=1)  13 us
  transfers between devices with their start and end apart: 2, of which 2 were waited for; matrix products, arithmetic and copies ran while one was open for 5% of the time, Pallas kernels for 0%

commit v1 on v0

v1 whole, which is shorter than its diff:
```python
import functools

import jax
import jax.numpy as jnp
from jax import lax
from jax.experimental import pallas as pl
from jax.experimental.pallas import tpu as pltpu
from jax.sharding import PartitionSpec as P

DAMPING = 0.0001
AXES = ("tm", "fsdp")
NX, NZ, NY = 4, 2, 4
N_TM, N_FSDP = 32, 4
BLK = 512
ROWS_A = 192
ROWS_C = (BLK - 2 * ROWS_A) // 2
EXTRA = 8
SMALL, LARGE = 16 * 1024 * 1024, 56 * 1024 * 1024


def flat(x, zl, y, zh, core):
    return ((x % NX) * 8 + zl * 4 + (y % NY)) * N_FSDP + zh * 2 + core


def coords():
    for x in range(NX):
        for zl in range(NZ):
            for y in range(NY):
                for zh in range(2):
                    for core in range(2):
                        yield x, zl, y, zh, core


def pairs_far(axis, d):
    return [
        (flat(x, zl, y, zh, c), flat(x + d * (axis == "x"), zl, y + d * (axis == "y"), zh, c))
        for x, zl, y, zh, c in coords()
    ]


def pairs_z(step):
    out = []
    for x, zl, y, zh, c in coords():
        z = (zh * 2 + zl + (step if zl == 0 else -step)) % 4
        out.append((flat(x, zl, y, zh, c), flat(x, z % 2, y, z // 2, c)))
    return out


def pairs_core():
    return [
        (flat(x, zl, y, zh, c), flat(x, zl, y, zh, 1 - c))
        for x, zl, y, zh, c in coords()
    ]


def split(value):
    high = value.astype(jnp.bfloat16)
    low = (value - high.astype(jnp.float32)).astype(jnp.bfloat16)
    return high, low


def dot3(a, b, dims):
    (ah, al), (bh, bl) = a, b
    dot = functools.partial(
        lax.dot_general,
        dimension_numbers=(dims, ((), ())),
        preferred_element_type=jnp.float32,
    )
    return dot(ah, bh) + (dot(ah, bl) + dot(al, bh))


def spot(where, stream, r, sub, i):
    z = where[1] if sub == 0 else 1 - where[1]
    if stream == "x":
        return ((where[0] + r) & 3) * 8 + z * 4 + i
    if stream == "y":
        return i * 8 + z * 4 + ((where[2] + r) & 3)
    return (i >> 2) * 8 + z * 4 + (i & 3)


def spec(shape, index, **more):
    return pl.BlockSpec(shape, index, **more)


def resident(array):
    zeros = (0,) * array.ndim
    return pl.BlockSpec(array.shape, lambda *_: zeros, pipeline_mode=pl.Buffered(1))


class Order:
    def __init__(self, table, where):
        self.table, self.where, self.last = table, where, None

    def gate(self, held, behind):
        anywhere = pl.BlockSpec(memory_space=pl.ANY)
        made = pl.pallas_call(
            lambda *refs: None,
            out_shape=[jax.ShapeDtypeStruct(a.shape, a.dtype) for a in held],
            in_specs=[anywhere] * (len(held) + len(behind) + 1),
            out_specs=[anywhere] * len(held),
            input_output_aliases={i: i for i in range(len(held))},
            cost_estimate=pl.CostEstimate(flops=0, bytes_accessed=1, transcendentals=0),
        )(*held, *behind, self.last)
        self.last = made[-1]
        return made

    def __call__(self, body, grid, ins, outs, cost=1.0, vmem=SMALL):
        shapes = [
            jax.ShapeDtypeStruct(o[0], o[2] if len(o) > 2 else jnp.float32) for o in outs
        ]
        inner = body
        if self.last is not None:
            ins = [(self.last, pl.BlockSpec(memory_space=pl.ANY))] + ins
            inner = lambda table, where, after, *refs: body(table, where, *refs)
        made = pl.pallas_call(
            inner,
            out_shape=shapes,
            grid_spec=pltpu.PrefetchScalarGridSpec(
                num_scalar_prefetch=2,
                grid=(grid,),
                in_specs=[s for _, s in ins],
                out_specs=[o[1] for o in outs],
            ),
            cost_estimate=pl.CostEstimate(
                flops=0, bytes_accessed=int(cost * 3.69e6), transcendentals=0
            ),
            compiler_params=pltpu.CompilerParams(vmem_limit_bytes=vmem),
        )(self.table, self.where, *[a for a, _ in ins])
        self.last = made[-1]
        return made


def piece(turned, latents, block, row, rows):
    left = turned[pl.ds(pl.multiple_of((block & 3) * BLK + row, 16), rows), :]
    right = latents[:, pl.ds(pl.multiple_of((block >> 2) * BLK, BLK), BLK)]
    return jnp.dot(left, right, preferred_element_type=jnp.float32)


SETS_A = (("x", 0, 2), ("x", 1, 2), ("y", 0, 2), ("y", 1, 2))
SETS_B = (("x", 1, 1), ("x", 0, 3), ("y", 1, 1), ("y", 0, 3))
SETS_T = (("x", 0, 1), ("x", 1, 3), ("y", 0, 1), ("y", 1, 3))
SETS_OWN = (("x", 0, 0), ("x", 1, 0), ("y", 0, 0), ("y", 1, 0))
SETS_AWAY, SETS_KEEP = (("c", 0, 0),), (("c", 1, 0),)
ROW = {"x": 0, "y": ROWS_A, "c": 2 * ROWS_A}


def first_body(table, where, grads, *refs):
    rights, turned, outs = refs[:4], refs[4], refs[5:]
    i = pl.program_id(0)

    @pl.when(i == 0)
    def _():
        for c in range(grads.shape[1] // BLK):
            turned[c * BLK : (c + 1) * BLK, :] = grads[:, c * BLK : (c + 1) * BLK].T

    for right, out, (stream, sub, r) in zip(rights, outs, SETS_A):
        block = table[spot(where, stream, r, sub, i)]
        row = (block & 3) * BLK + ROW[stream]
        left = turned[pl.ds(pl.multiple_of(row, 16), ROWS_A), :]
        out[0] = jnp.dot(left, right[...], preferred_element_type=jnp.float32)


def first_products(order, latents, out_grads):
    tok, wide = out_grads.shape
    ins = [(out_grads, resident(out_grads))]
    for job in SETS_A:
        at = lambda i, t, w, job=job: (0, t[spot(w, job[0], job[2], job[1], i)] >> 2)
        ins.append((latents, spec((tok, BLK), at)))
    outs = [((wide, tok), spec((wide, tok), lambda i, t, w: (0, 0)), out_grads.dtype)]
    for _ in SETS_A:
        outs.append(((4, ROWS_A, BLK), spec((1, ROWS_A, BLK), lambda i, t, w: (i, 0, 0))))
    return order(first_body, 4, ins, outs, vmem=LARGE)


def products_body(jobs, table, where, turned, latents, *refs):
    outs, got = refs[-len(jobs) :], refs[: -len(jobs)]
    i = pl.program_id(0)
    for m, ((stream, sub, r), out) in enumerate(zip(jobs, outs)):
        n, rows = out.shape[:2]
        for u in range(n):
            at = spot(where, stream, r, sub, n * i + u)
            value = piece(turned, latents, table[at], ROW[stream], rows)
            if m < len(got):
                value = value + got[m][u]
            out[u] = value


def products(order, turned, latents, jobs, got=()):
    outs = []
    for stream, sub, r in jobs:
        n, rows = (4, ROWS_A) if stream in "xy" else (16, 2 * ROWS_C)
        outs.append(((n, rows, BLK), spec((n // 4, rows, BLK), lambda i, t, w: (i, 0, 0))))
    return order(
        functools.partial(products_body, jobs),
        4,
        [(turned, resident(turned)), (latents, resident(latents))]
        + [(g, spec((1, ROWS_A, BLK), lambda i, t, w: (i, 0, 0))) for g in got],
        outs,
        vmem=LARGE,
    )


def whole(array):
    zeros = (0,) * array.ndim
    return spec(array.shape, lambda i, t, w: zeros)


def full(*shape):
    zeros = (0,) * len(shape)
    return (shape, spec(shape, lambda i, t, w: zeros))


def relay_body(table, where, *refs):
    for got, term, out in zip(refs[:4], refs[4:8], refs[8:]):
        out[...] = got[...] + term[...]


def relay(order, got, terms):
    here = spec((1, ROWS_A, BLK), lambda i, t, w: (i, 0, 0))
    ins = [(a, here) for a in (*got, *terms)]
    return order(relay_body, 4, ins, [(got[0].shape, here)] * 4, vmem=LARGE)


def half_rows(stream):
    return ROWS_A + 2 * (ROWS_C + (EXTRA if stream == "x" else 0))


MESSAGES = ((2, 0, (0, 0)), (1, 1, (0, 1)), (2, 1, (1, 0)), (3, 0, (1, 1)))
TERMS = ((1, 0, (0,)), (3, 1, (1,)), (0, 0, (2, 0)), (0, 1, (2, 1)))


def turn_body(stream, jobs, table, where, *refs):
    sums = refs[16:19] if stream == "x" else ()
    outs = refs[16 + len(sums) :]
    rows = (half_rows(stream) - ROWS_A) // 2
    for n, (r, half, place) in enumerate(jobs):
        base, more, got, term = refs[4 * n : 4 * n + 4]
        out = outs[place[0]].at[place[1]] if len(place) == 2 else outs[place[0]]
        out[:ROWS_A, :] = base[0] + more[0]
        for v in range(2):
            at = (0, v) if stream == "y" else (v, 0)
            low = ROWS_A + v * rows
            out[low : low + ROWS_C, :] = got[at] + term[at]
            if stream == "y":
                continue
            first_in, second_in, sums_out = sums
            parts = []
            for sub in (1, 0):
                block = table[spot(where, "y", r, sub, 2 * half + v)]
                a = block >> 2
                parts.append(jnp.where(a < 4, first_in[a & 3], second_in[a & 3]))
                parts.append(sums_out[block & 3])
            parts.append(jnp.zeros((EXTRA - 4, BLK), jnp.float32))
            out[low + ROWS_C : low + rows, :] = jnp.concatenate(parts, axis=0)


def turn(order, stream, jobs, halves, got, terms, sums):
    ins = []
    for r, half, _ in jobs:
        if stream == "x":
            here = lambda i, t, w, r=r: ((w[2] + r) & 3, 0, 0)
            side = spec((2, 1, ROWS_C, BLK), lambda i, t, w, r=r, h=half: (h, (w[2] + r) & 3, 1, 0))
        else:
            here = lambda i, t, w, r=r: ((w[0] + r) & 3, 0, 0)
            side = spec((1, 2, ROWS_C, BLK), lambda i, t, w, r=r, h=half: ((w[0] + r) & 3, h, 0, 0))
        ins += [(a, spec((1, ROWS_A, BLK), here)) for a in halves[half]]
        ins += [(a.reshape(4, 4, 2 * ROWS_C, BLK), side) for a in (got, terms)]
    if stream == "x":
        ins += [(s, whole(s)) for s in sums]
    rows = half_rows(stream)
    outs = [full(2, rows, BLK)] * 2
    if jobs is TERMS:
        outs = [full(rows, BLK)] * 2 + [full(2, rows, BLK)]
    return order(functools.partial(turn_body, stream, jobs), 1, ins, outs, vmem=LARGE)


def relay_half_body(table, where, message, term, out):
    out[...] = message[0] + term[...]


def relay_half(order, message, term):
    rows = message.shape[1]
    ins = [(message, spec((1, rows, BLK), lambda i, t, w: (0, 0, 0))), (term, whole(term))]
    return order(relay_half_body, 1, ins, [full(rows, BLK)])[0]


def end_body(stream, table, where, own, forth, back, more_forth, more_back, *outs):
    halves = (
        lambda a, b: own[0, a:b] + back[1, a:b] + more_forth[a:b, :],
        lambda a, b: own[1, a:b] + forth[1, a:b] + more_back[a:b, :],
    )
    outs[0][...] = halves[0](0, ROWS_A)
    outs[1][...] = halves[1](0, ROWS_A)
    rows = (half_rows(stream) - ROWS_A) // 2
    for u in range(4):
        base = ROWS_A + (u % 2) * rows
        slot = halves[u // 2](base, base + rows)
        for d in range(4):

            @pl.when(((where[0 if stream == "x" else 2] + d) & 3) == u)
            def _():
                outs[2 + d][...] = slot


def end(order, stream, own, forth, back, more_forth, more_back):
    rows = (half_rows(stream) - ROWS_A) // 2
    outs = [full(ROWS_A, BLK)] * 2 + [full(rows, BLK)] * 4
    ins = [(a, whole(a)) for a in (own, forth, back, more_forth, more_back)]
    return order(functools.partial(end_body, stream), 1, ins, outs)


def sums_body(table, where, rows, basis, out):
    high, low = split(basis[0])
    tokens = rows[...]
    moved = jnp.dot(
        jnp.concatenate([tokens, tokens], axis=1),
        jnp.concatenate([high, low], axis=0),
        preferred_element_type=jnp.float32,
    )
    out[0] = jnp.sum(moved * moved, axis=0, keepdims=True)


def square_sums(order, rows, basis, first, n):
    tok = rows.shape[0]
    ins = [
        (rows, spec((tok, BLK), lambda i, t, w: (0, first + i))),
        (basis, spec((1, BLK, BLK), lambda i, t, w: (first + i, 0, 0))),
    ]
    out = ((n, 1, BLK), spec((1, 1, BLK), lambda i, t, w: (i, 0, 0)))
    return order(sums_body, n, ins, [out], vmem=LARGE)[0]


def total_body(table, where, *refs):
    value = (refs[0][...] + refs[1][...]) + (refs[2][...] + refs[3][...])
    refs[4][...] = value[:ROWS_C]
    if len(refs) == 6:
        refs[5][...] = value[ROWS_C:]


def total(order, parts):
    rows = parts[0].shape[0]
    outs = [full(ROWS_C, BLK)] + ([full(EXTRA, BLK)] if rows > ROWS_C else [])
    return order(total_body, 1, [(p, whole(p)) for p in parts], outs)


def join_body(table, where, a, b, out):
    out[...] = a[...] + b[...]


def join(order, a, b):
    return order(join_body, 1, [(a, whole(a)), (b, whole(b))], [full(*a.shape)])[0]


def precondition_body(tokens_all, table, where, *refs):
    x, y0, y1, cx, cy, ours, theirs = (r[...] for r in refs[:7])
    basis_in, basis_out, out = refs[7:]
    scale = 1.0 / tokens_all
    grad = jnp.concatenate([x, y0 + y1, cx, cy], axis=0) * scale
    values_in = (ours[0:1] + theirs[2:3]) * scale
    values_out = (ours[1:2] + theirs[3:4]) * scale
    a = split(basis_in[0])
    b = split(basis_out[0])
    rotated = dot3(split(grad), a, ((1,), (0,)))
    rotated = dot3(b, split(rotated), ((0,), (0,)))
    scaled = rotated / (values_out.reshape(BLK, 1) * values_in + DAMPING)
    back = dot3(b, split(scaled), ((1,), (0,)))
    out[...] = dot3(a, split(back), ((1,), (1,)))


def precondition(tokens_all, order, parts, eig_in, eig_out):
    mine = lambda w: w[0] * 8 + (1 - w[1]) * 4 + w[2]
    ins = [(q, whole(q)) for q in parts]
    ins.append((eig_in, spec((1, BLK, BLK), lambda i, t, w: (t[mine(w)] >> 2, 0, 0))))
    ins.append((eig_out, spec((1, BLK, BLK), lambda i, t, w: (t[mine(w)] & 3, 0, 0))))
    return order(
        functools.partial(precondition_body, tokens_all),
        1,
        ins,
        [full(BLK, BLK)],
        cost=3.0,
        vmem=LARGE,
    )[0]


def on_device(latents, out_grads, eig_in, eig_out, table):
    tokens_all = latents.shape[0] * N_TM
    tm = lax.axis_index("tm")
    fsdp = lax.axis_index("fsdp")
    x, zl, y = tm // 8, (tm // 4) % 2, tm % 4
    zh, core = fsdp // 2, fsdp % 2
    where = jnp.stack([x, zl, y]).astype(jnp.int32)
    near, cross = pairs_z(1), pairs_z(-1)
    send = lambda value, pairs: lax.ppermute(value, AXES, pairs)
    hop = lambda value, axis, d: send(value, pairs_far(axis, d))
    both = lambda forth, back, axis: [hop(forth, axis, 1), hop(back, axis, 3)]
    order = Order(table, where)
    far = lambda parts, axis: [parts[0]] + [hop(parts[d], axis, d) for d in (1, 2, 3)]

    turned, *sets_a = first_products(order, latents, out_grads)
    got_a = both(*sets_a[:2], "x") + both(*sets_a[2:], "y")
    got_c = send(products(order, turned, latents, SETS_AWAY)[0], near)
    made = products(order, turned, latents, SETS_B + SETS_T)
    got_b = both(*made[:2], "x") + both(*made[2:4], "y")
    sets_t = relay(order, got_a, made[4:])
    sums = [square_sums(order, latents, eig_in, 0, 4)]
    got_t = both(*order.gate(sets_t[:2], got_b[:2]), "x")
    got_t += both(*order.gate(sets_t[2:], got_b[2:]), "y")
    got_b = [got_b[n] for n in (1, 0, 3, 2)]
    *own, terms_c = products(order, turned, latents, SETS_OWN + SETS_KEEP, got_b)
    sums.append(square_sums(order, latents, eig_in, 4, 4))
    sums.append(square_sums(order, out_grads, eig_out, 0, 4))

    def pieces(stream, jobs):
        n = 0 if stream == "x" else 2
        halves = ((own[n], got_t[n]), (own[n + 1], got_t[n + 1]))
        return turn(order, stream, jobs, halves, got_c, terms_c, sums)

    msgs_x = both(*pieces("x", MESSAGES), "y")
    msgs_y = both(*pieces("y", MESSAGES), "x")
    *parts_x, mine_x = pieces("x", TERMS)
    *parts_y, mine_y = pieces("y", TERMS)

    def follow(stream, messages, parts):
        more = [relay_half(order, m, p) for m, p in zip(messages, parts)]
        return both(*more, "y" if stream == "x" else "x")

    more_x = follow("x", msgs_x, parts_x)
    more_y = follow("y", msgs_y, parts_y)

    away_x, keep_x, *parts_cy = end(order, "x", mine_x, *msgs_x, *more_x)
    got_x = send(away_x, near)
    away_y, keep_y, *parts_cx = end(order, "y", mine_y, *msgs_y, *more_y)
    got_y = send(away_y, near)
    done_cy, ours = total(order, far(parts_cy, "x"))
    theirs = send(ours, near)
    (done_cx,) = total(order, far(parts_cx, "y"))
    done_x = join(order, keep_x, got_x)
    update = precondition(
        tokens_all,
        order,
        [done_x, keep_y, got_y, done_cx, done_cy, ours, theirs],
        eig_in,
        eig_out,
    )
    same = send(update, near)
    other = send(update, cross)
    same_core = send(same, pairs_core())
    other_core = send(other, pairs_core())
    result = jnp.zeros((N_FSDP, BLK, BLK), jnp.float32)
    for block, at in (
        (same, zh * 2 + core),
        (other, (1 - zh) * 2 + core),
        (same_core, zh * 2 + 1 - core),
        (other_core, (1 - zh) * 2 + 1 - core),
    ):
        result = lax.dynamic_update_index_in_dim(result, block, at, 0)
    return result[:, None]


def solution(mesh):
    in_specs = (P("tm", None), P("tm", "fsdp"), P(), P("fsdp", None, None), P())
    out_specs = P(None, "tm", None, None)
    return jax.shard_map(
        on_device, mesh=mesh, in_specs=in_specs, out_specs=out_specs, check_vma=False
    )
```

time: 517 us -> 242 us (0.47)
  waiting for transfers between devices: 222 us -> 64.8 us
  blocking collectives: 152 us -> 0 us
  Pallas kernels: 0 us -> 107 us
  matrix products: 70.6 us -> 0 us
  starting transfers between devices: 0.22 us -> 58.4 us
  local copies, waits for them, and re-layouts: 53.8 us -> 10.1 us
  between operations: 16.1 us -> 0.3 us
    reduce_scatter x1 -> x0, waiting for transfers between devices: 187 us -> none  [on_device(): lax.psum_scatter(jnp.einsum('tcb,tce->cbe', left, right, preferred_elemen...]
    psum x1 -> x0, blocking collectives: 152 us -> none  [on_device(): lax.psum((jnp.sum(proj_in * proj_in, axis=0), jnp.sum(proj_out * proj_out...]
    pallas_call x0 -> x24, Pallas kernels: none -> 107 us  [the longest x22 107 us: __call__(): pl.pallas_call(inner, out_shape=shapes, grid_spec=pltpu.PrefetchScalarGri...]
    dot_general x7 -> x0, matrix products: 70.6 us -> none  [the longest x1 29.2 us: on_device(): jnp.einsum('tcb,tce->cbe', left, right, preferred_element_type=jnp.float32)]
    ppermute x0 -> x34, waiting for transfers between devices: none -> 64.8 us  [on_device(): send = lambda value, pairs: lax.ppermute(value, AXES, pairs)]
    ppermute x0 -> x34, starting transfers between devices: none -> 58.4 us  [on_device(): send = lambda value, pairs: lax.ppermute(value, AXES, pairs)]
    all_gather x1 -> x0, waiting for transfers between devices: 35.6 us -> none  [on_device(): return lax.all_gather(result[None], 'fsdp', axis=0, tiled=True)]
    gather x2 -> x0, local copies, waits for them, and re-layouts: 23 us -> none  [the longest x1 13 us: on_device(): left = jnp.take(input_partition, owner_table // col_blocks, axis=1)]
  transfers between devices with their start and end apart: 2 -> 34, of which waited for: 2 -> 15; matrix products, arithmetic and copies ran while one was open for 5% -> 0% of each run, Pallas kernels for 0% -> 36%
where the time goes in v1:
time: 242 us; the launch traced here: 241 us
  Pallas kernels  107 us (44%)
  waiting for transfers between devices  64.8 us (27%)
  starting transfers between devices  58.4 us (24%)
  local copies, waits for them, and re-layouts  10.1 us (4%)
    pallas_call x22, Pallas kernels, __call__(): pl.pallas_call(inner, out_shape=shapes, grid_spec=pltpu.PrefetchScalarGri...  107 us
    ppermute x34, waiting for transfers between devices, on_device(): send = lambda value, pairs: lax.ppermute(value, AXES, pairs)  64.8 us
    ppermute x34, starting transfers between devices, on_device(): send = lambda value, pairs: lax.ppermute(value, AXES, pairs)  58.4 us
    unnamed x48, local copies, waits for them, and re-layouts  7.08 us
  transfers between devices with their start and end apart: 34, of which 15 were waited for; matrix products, arithmetic and copies ran while one was open for 0% of the time, Pallas kernels for 36%

profile of v1, /device:TPU:1, one launch (start us, length us, event | category | flops | bytes accessed | tf_op | source)
XLA Modules:
  0.0 241.5 jit_solution(8060563036463210011)
XLA Ops:
  0.6 11.9 %shard_map.55 = (bf16[2048,768]{1,0:T(8,128)(2,1)}, f32[4,192,512]{2,1,0:T(8,128)}, f32[4,192,512]{2,1,0:T(8,128)}, f32[4,192,512]{2,1,0:T(8,128)}, f32[4,192,512]{2,1,0:T(8,128)}) custom-call(s32[32]{0:T(128)} %table.43, s32[3]{0:T(128)} %pad_add_fusion.where, bf16[768,2048]{1,0:T(8,128)(2,1)} %refs_0_.7, bf16[768,4096]{1,0:T(8,128)(2,1)} %refs_0_.6, ...), custom_call_target="tpu_custom_call" | custom-call | bytes 3690000 | tf_op jit(solution)/shard_map/pallas_call | solution.py:115
  12.5 2.1 collective-permute-start
  14.6 1.1 collective-permute-start.1
  15.7 1.7 collective-permute-start.2
  17.3 1.2 collective-permute-start.3
  18.5 8.2 %shard_map.56.after = f32[16,128,512]{2,1,0:T(8,128)} custom-call(s32[32]{0:T(128)} %table.43, s32[3]{0:T(128)} %pad_add_fusion.where, f32[4,192,512]{2,1,0:T(8,128)} %get-tuple-element.55.after, bf16[2048,768]{1,0:T(8,128)(2,1)} %get-tuple-element.56.refs_0_, bf16[768,4096]{1,0:T(8,128)(2,1)} %refs_0_.6), custom_call_target="tpu_custom_call" | custom-call | bytes 3690000 | tf_op jit(solution)/shard_map/pallas_call | solution.py:115
  26.8 1.8 collective-permute-start.9
  28.5 11.9 %shard_map.57 = (f32[4,192,512]{2,1,0:T(8,128)}, f32[4,192,512]{2,1,0:T(8,128)}, f32[4,192,512]{2,1,0:T(8,128)}, f32[4,192,512]{2,1,0:T(8,128)}, f32[4,192,512]{...) custom-call(s32[32]{0:T(128)} %table.43, s32[3]{0:T(128)} %pad_add_fusion.where, ...), custom_call_target="tpu_custom_call" | custom-call | bytes 3690000 | tf_op jit(solution)/shard_map/pallas_call | solution.py:115
  40.4 8.8 %collective-permute-done.refs_0_ = f32[4,192,512]{2,1,0:T(8,128)S(1)} collective-permute-done((f32[4,192,512]{2,1,0:T(8,128)}, f32[4,192,512]{2,1,0:T(8,128)S(1)}, u32[]{:S(2)}, u32[]{:S(2)}) %collective-permute-start) | collective-permute-done | bytes 1572896 | tf_op jit(solution)/shard_map/ppermute | solution.py:393
  49.2 0.9 collective-permute-start.6
  50.2 1.8 collective-permute-start.7
  51.9 2.1 collective-permute-start.4
  54.0 1.3 collective-permute-start.5
  55.3 8.0 %shard_map.58 = (f32[4,192,512]{2,1,0:T(8,128)}, f32[4,192,512]{2,1,0:T(8,128)}, f32[4,192,512]{2,1,0:T(8,128)}, f32[4,192,512]{2,1,0:T(8,128)}) custom-call(s32[32]{0:T(128)} %table.43, s32[3]{0:T(128)} %pad_add_fusion.where, f32[4,192,512]{2,1,0:T(8,128)} %get-tuple-element.57.after.refs_7_, f32[4,192,512]{2,1,0:T(8,128)} %copy-done.18, ...), custom_call_target="tpu_custom_call" | custom-call | bytes 3690000 | tf_op jit(solution)/shard_map/pallas_call | solution.py:115
  63.3 7.3 %shard_map.59.refs_4_.refs_16_ = f32[4,1,512]{2,1,0:T(1,128)} custom-call(s32[32]{0:T(128)} %table.43, s32[3]{0:T(128)} %pad_add_fusion.where, f32[4,192,512]{2,1,0:T(8,128)} %get-tuple-element.65.after.refs_1_, bf16[768,4096]{1,0:T(8,128)(2,1)} %refs_0_.6, f32[8,512,512]{2,1,0:T(8,128)} %refs_7_.1), custom_call_target="tpu_custom_call" | custom-call | bytes 3690000 | tf_op jit(solution)/shard_map/pallas_call | solution.py:115
  70.6 14.1 %collective-permute-done.6.refs_2_.refs_3_ = f32[4,192,512]{2,1,0:T(8,128)S(1)} collective-permute-done((f32[4,192,512]{2,1,0:T(8,128)}, f32[4,192,512]{2,1,0:T(8,128)S(1)}, u32[]{:S(2)}, u32[]{:S(2)}) %collective-permute-start.6) | collective-permute-done | bytes 1572896 | tf_op jit(solution)/shard_map/ppermute | solution.py:393
  84.7 1.1 copy-done.16
  85.9 1.3 collective-permute-start.10
  87.3 0.8 collective-permute-done.4.refs_2_.refs_5_
  88.1 1.7 collective-permute-start.11
  89.8 1.5 collective-permute-start.12
  91.3 12.6 %shard_map.62 = (f32[4,192,512]{2,1,0:T(8,128)}, f32[4,192,512]{2,1,0:T(8,128)}, f32[4,192,512]{2,1,0:T(8,128)}, f32[4,192,512]{2,1,0:T(8,128)}, f32[16,128,512]{2,1,0:T(8,128)}) custom-call(s32[32]{0:T(128)} %table.43, s32[3]{0:T(128)} %pad_add_fusion.where, f32[4,192,512]{2,1,0:T(8,128)} %get-tuple-element.73.after, ...), custom_call_target="tpu_custom_call" | custom-call | bytes 3690000 | tf_op jit(solution)/shard_map/pallas_call | solution.py:115
  103.8 7.3 %shard_map.63.after.refs_17_ = f32[4,1,512]{2,1,0:T(1,128)} custom-call(s32[32]{0:T(128)} %table.43, s32[3]{0:T(128)} %pad_add_fusion.where, f32[16,128,512]{2,1,0:T(8,128)} %get-tuple-element.74.after, bf16[768,4096]{1,0:T(8,128)(2,1)} %refs_0_.6, f32[8,512,512]{2,1,0:T(8,128)} %refs_7_.1), custom_call_target="tpu_custom_call" | custom-call | bytes 3690000 | tf_op jit(solution)/shard_map/pallas_call | solution.py:115
  111.2 7.3 %shard_map.64.after.refs_18_ = f32[4,1,512]{2,1,0:T(1,128)} custom-call(s32[32]{0:T(128)} %table.43, s32[3]{0:T(128)} %pad_add_fusion.where, f32[4,1,512]{2,1,0:T(1,128)} %shard_map.63.after.refs_17_, bf16[768,2048]{1,0:T(8,128)(2,1)} %refs_0_.7, f32[4,512,512]{2,1,0:T(8,128)} %refs_8_.1), custom_call_target="tpu_custom_call" | custom-call | bytes 3690000 | tf_op jit(solution)/shard_map/pallas_call | solution.py:115
  118.5 0.8 collective-permute-done.10.refs_5_.refs_9_.refs_13_
  119.3 1.8 collective-permute-done.8.refs_1_.refs_13_.refs_9_
  121.1 4.9 %shard_map.65 = (f32[2,336,512]{2,1,0:T(8,128)}, f32[2,336,512]{2,1,0:T(8,128)}) custom-call(s32[32]{0:T(128)} %table.43, s32[3]{0:T(128)} %pad_add_fusion.where, f32[4,1,512]{2,1,0:T(1,128)} %shard_map.64.after.refs_18_, f32[4,192,512]{2,1,0:T(8,128)} %get-tuple-element.75.refs_0_.refs_12_.refs_8_, ...), custom_call_target="tpu_custom_call" | custom-call | bytes 3690000 | tf_op jit(solution)/shard_map/pallas_call | solution.py:115
  126.0 2.9 %collective-permute-start.13 = (f32[2,336,512]{2,1,0:T(8,128)}, f32[2,336,512]{2,1,0:T(8,128)S(1)}, u32[]{:S(2)}, u32[]{:S(2)}) collective-permute-start(f32[2,336,512]{2,1,0:T(8,128)} %get-tuple-element.85), channel_id=1, source_target_pairs={{0,4},{1,5},{2,6},{3,7},{4,8},{5,9},{6,10},{7,11},{8,12},{9,13},{1... | collective-permute-start | bytes 4128776 | tf_op jit(solution)/shard_map/ppermute | solution.py:393
  128.9 1.2 collective-permute-start.14
  130.2 1.1 copy-done.14
  131.9 4.8 %shard_map.66 = (f32[2,320,512]{2,1,0:T(8,128)}, f32[2,320,512]{2,1,0:T(8,128)}) custom-call(s32[32]{0:T(128)} %table.43, s32[3]{0:T(128)} %pad_add_fusion.where, f32[2,336,512]{2,1,0:T(8,128)} %get-tuple-element.78.after, f32[4,192,512]{2,1,0:T(8,128)} %get-tuple-element.79.refs_0_.refs_12_.refs_8_, f32[4,192,512]{2,1,0:T(8,128)} %copy-done.14, ...), custom_call_target="tpu_custom_call" | custom-call | bytes 3690000 | tf_op jit(solution)/shard_map/pallas_call | solution.py:115
  136.7 2.7 %collective-permute-start.16 = (f32[2,320,512]{2,1,0:T(8,128)}, f32[2,320,512]{2,1,0:T(8,128)S(1)}, u32[]{:S(2)}, u32[]{:S(2)}) collective-permute-start(f32[2,320,512]{2,1,0:T(8,128)} %get-tuple-element.82.after), channel_id=1, source_target_pairs={{0,96},{1,97},{2,98},{3,99},{4,100},{5,101},{6,102},{7,103},{8,104... | collective-permute-start | bytes 3932168 | tf_op jit(solution)/shard_map/ppermute | solution.py:393
  139.4 4.9 %shard_map.67 = (f32[336,512]{1,0:T(8,128)}, f32[336,512]{1,0:T(8,128)}, f32[2,336,512]{2,1,0:T(8,128)}) custom-call(s32[32]{0:T(128)} %table.43, s32[3]{0:T(128)} %pad_add_fusion.where, f32[2,320,512]{2,1,0:T(8,128)} %get-tuple-element.82.after, f32[4,192,512]{2,1,0:T(8,128)} %get-tuple-element.75.refs_0_.refs_12_.refs_8_, ...), custom_call_target="tpu_custom_call" | custom-call | bytes 3690000 | tf_op jit(solution)/shard_map/pallas_call | solution.py:115
  144.3 4.8 %shard_map.68 = (f32[320,512]{1,0:T(8,128)}, f32[320,512]{1,0:T(8,128)}, f32[2,320,512]{2,1,0:T(8,128)}) custom-call(s32[32]{0:T(128)} %table.43, s32[3]{0:T(128)} %pad_add_fusion.where, f32[2,336,512]{2,1,0:T(8,128)} %get-tuple-element.83.after.refs_0_, f32[4,192,512]{2,1,0:T(8,128)} %get-tuple-element.79.refs_0_.refs_12_.refs_8_, ...), custom_call_target="tpu_custom_call" | custom-call | bytes 3690000 | tf_op jit(solution)/shard_map/pallas_call | solution.py:115
  149.1 7.7 %collective-permute-done.13.refs_0_.refs_1_ = f32[2,336,512]{2,1,0:T(8,128)S(1)} collective-permute-done((f32[2,336,512]{2,1,0:T(8,128)}, f32[2,336,512]{2,1,0:T(8,128)S(1)}, u32[]{:S(2)}, u32[]{:S(2)}) %collective-permute-start.13) | collective-permute-done | bytes 1376288 | tf_op jit(solution)/shard_map/ppermute | solution.py:393
  156.8 1.3 copy-done.1
  159.2 0.6 shard_map.70.after
  159.9 1.3 collective-permute-start.18
  161.4 2.8 %collective-permute-done.15.refs_0_.refs_1_ = f32[2,320,512]{2,1,0:T(8,128)S(1)} collective-permute-done((f32[2,320,512]{2,1,0:T(8,128)}, f32[2,320,512]{2,1,0:T(8,128)S(1)}, u32[]{:S(2)}, u32[]{:S(2)}) %collective-permute-start.15) | collective-permute-done | bytes 1310752 | tf_op jit(solution)/shard_map/ppermute | solution.py:393
  164.2 0.6 shard_map.71.after
  165.3 0.6 shard_map.72.after
  165.9 1.4 collective-permute-start.20
  167.5 4.8 %collective-permute-done.18.refs_4_ = f32[336,512]{1,0:T(8,128)S(1)} collective-permute-done((f32[336,512]{1,0:T(8,128)S(1)}, f32[336,512]{1,0:T(8,128)S(1)}, u32[]{:S(2)}, u32[]{:S(2)}) %collective-permute-start.18) | collective-permute-done | bytes 688160 | tf_op jit(solution)/shard_map/ppermute | solution.py:393
  172.3 1.8 collective-permute-done.17.refs_3_
  174.1 0.9 shard_map.73
  175.0 1.7 collective-permute-start.27
  177.1 1.6 collective-permute-done.19.refs_3_
  178.7 0.9 shard_map.74
  179.6 1.2 collective-permute-start.28
  180.7 2.7 %collective-permute-start.22 = (f32[72,512]{1,0:T(8,128)S(1)}, f32[72,512]{1,0:T(8,128)S(1)}, u32[]{:S(2)}, u32[]{:S(2)}) collective-permute-start(f32[72,512]{1,0:T(8,128)S(1)} %get-tuple-element.95), channel_id=1, source_target_pairs={{0,64},{1,65},{2,66},{3,67},{4,68},{5,69},{6,70},{7,71},{8,72},{9,... | collective-permute-start | bytes 442376 | tf_op jit(solution)/shard_map/ppermute | solution.py:393
  183.5 4.7 %collective-permute-done.21.refs_1_ = f32[72,512]{1,0:T(8,128)S(1)} collective-permute-done((f32[72,512]{1,0:T(8,128)S(1)}, f32[72,512]{1,0:T(8,128)S(1)}, u32[]{:S(2)}, u32[]{:S(2)}) %collective-permute-start.21) | collective-permute-done | bytes 147488 | tf_op jit(solution)/shard_map/ppermute | solution.py:393
  188.1 2.4 collective-permute-start.25
  190.5 1.1 collective-permute-start.26
  192.2 2.4 collective-permute-done.24.refs_1_
  194.6 2.0 collective-permute-start.29
  197.8 0.8 copy-done.3
  199.3 7.4 %shard_map.78 = f32[512,512]{1,0:T(8,128)} custom-call(s32[32]{0:T(128)} %table.43, s32[3]{0:T(128)} %pad_add_fusion.where, f32[192,512]{1,0:T(8,128)} %copy-done.3, f32[192,512]{1,0:T(8,128)} %copy-done.3, f32[192,512]{1,0:T(8,128)} %copy-done.9, f32[192,512]{1,0:T(8,128)} %copy-done.22, f32[64,512]{1,0:T(8,128)} %copy-done.4, f32[64,512]{1,0:T(8,128)} %copy-done.12, ...), custom_call_target="tpu_custom_call" | custom-call | bytes 11070000 | tf_op jit(solution)/shard_map/pallas_call | solution.py:115
  206.7 0.9 collective-permute-start.30
  207.6 2.4 collective-permute-start.31
  210.0 10.7 %collective-permute-done.30 = f32[512,512]{1,0:T(8,128)S(1)} collective-permute-done((f32[512,512]{1,0:T(8,128)}, f32[512,512]{1,0:T(8,128)S(1)}, u32[]{:S(2)}, u32[]{:S(2)}) %collective-permute-start.30) | collective-permute-done | bytes 1048608 | tf_op jit(solution)/shard_map/ppermute | solution.py:393
  220.8 13.4 %collective-permute-start.32 = (f32[512,512]{1,0:T(8,128)S(1)}, f32[512,512]{1,0:T(8,128)S(1)}, u32[]{:S(2)}, u32[]{:S(2)}) collective-permute-start(f32[512,512]{1,0:T(8,128)S(1)} %collective-permute-done.30), channel_id=1, source_target_pairs={{0,1},{1,0},{2,3},{3,2},{4,5},{5,4},{6,7},{7,6},{8,9},{9,8},{10,11... | collective-permute-start | bytes 3145736 | tf_op jit(solution)/shard_map/ppermute | solution.py:393
  234.2 2.2 collective-permute-start.33
  237.2 1.6 collective-permute-done.33
  239.2 2.3 bitcast_dynamic-update-slice_fusion
  (82 shorter events, 7.5 us)
Async XLA Ops:
  12.5 36.7 %collective-permute-start = (f32[4,192,512]{2,1,0:T(8,128)}, f32[4,192,512]{2,1,0:T(8,128)S(1)}, u32[]{:S(2)}, u32[]{:S(2)}) collective-permute-start(f32[4,192,512]{2,1,0:T(8,128)} %get-tuple-element.58), channel_id=1, source_target_pairs={{0,32},{1,33},{2,34},{3,35},{4,36},{5,37},{6,38},{7,39},{8,40},{9,... | collective-permute-start | bytes 4718600 | tf_op jit(solution)/shard_map/ppermute | solution.py:393
  14.6 35.6 %collective-permute-start.1 = (f32[4,192,512]{2,1,0:T(8,128)}, f32[4,192,512]{2,1,0:T(8,128)S(1)}, u32[]{:S(2)}, u32[]{:S(2)}) collective-permute-start(f32[4,192,512]{2,1,0:T(8,128)} %get-tuple-element.59), channel_id=1, source_target_pairs={{0,96},{1,97},{2,98},{3,99},{4,100},{5,101},{6,102},{7,103},{8,104... | collective-permute-start | bytes 4718600 | tf_op jit(solution)/shard_map/ppermute | solution.py:393
  15.7 36.2 %collective-permute-start.2 = (f32[4,192,512]{2,1,0:T(8,128)}, f32[4,192,512]{2,1,0:T(8,128)S(1)}, u32[]{:S(2)}, u32[]{:S(2)}) collective-permute-start(f32[4,192,512]{2,1,0:T(8,128)} %get-tuple-element.60), channel_id=1, source_target_pairs={{0,4},{1,5},{2,6},{3,7},{4,8},{5,9},{6,10},{7,11},{8,12},{9,13},{1... | collective-permute-start | bytes 4718600 | tf_op jit(solution)/shard_map/ppermute | solution.py:393
  17.3 36.7 %collective-permute-start.3 = (f32[4,192,512]{2,1,0:T(8,128)}, f32[4,192,512]{2,1,0:T(8,128)S(1)}, u32[]{:S(2)}, u32[]{:S(2)}) collective-permute-start(f32[4,192,512]{2,1,0:T(8,128)} %get-tuple-element.55.after), channel_id=1, source_target_pairs={{0,12},{1,13},{2,14},{3,15},{4,0},{5,1},{6,2},{7,3},{8,4},{9,5},{1... | collective-permute-start | bytes 4718600 | tf_op jit(solution)/shard_map/ppermute | solution.py:393
  26.8 94.4 %collective-permute-start.9 = (f32[16,128,512]{2,1,0:T(8,128)}, f32[16,128,512]{2,1,0:T(8,128)}, u32[]{:S(2)}, u32[]{:S(2)}) collective-permute-start(f32[16,128,512]{2,1,0:T(8,128)} %shard_map.56.after), channel_id=1, source_target_pairs={{0,16},{1,17},{2,18},{3,19},{4,20},{5,21},{6,22},{7,23},{8,24},{9,... | collective-permute-start | bytes 12582920 | tf_op jit(solution)/shard_map/ppermute | solution.py:393
  49.2 6.1 %copy-start.18 = (f32[4,192,512]{2,1,0:T(8,128)}, f32[4,192,512]{2,1,0:T(8,128)S(1)}, u32[]{:S(2)}) copy-start(f32[4,192,512]{2,1,0:T(8,128)S(1)} %collective-permute-done.refs_0_) | copy-start | bytes 4718596
  49.2 35.5 %collective-permute-start.6 = (f32[4,192,512]{2,1,0:T(8,128)}, f32[4,192,512]{2,1,0:T(8,128)S(1)}, u32[]{:S(2)}, u32[]{:S(2)}) collective-permute-start(f32[4,192,512]{2,1,0:T(8,128)} %get-tuple-element.70), channel_id=1, source_target_pairs={{0,32},{1,33},{2,34},{3,35},{4,36},{5,37},{6,38},{7,39},{8,40},{9,... | collective-permute-start | bytes 4718600 | tf_op jit(solution)/shard_map/ppermute | solution.py:393
  50.2 5.2 %copy-start.19 = (f32[4,192,512]{2,1,0:T(8,128)}, f32[4,192,512]{2,1,0:T(8,128)S(1)}, u32[]{:S(2)}) copy-start(f32[4,192,512]{2,1,0:T(8,128)S(1)} %collective-permute-done.1.refs_1_) | copy-start | bytes 4718596
  50.2 34.6 %collective-permute-start.7 = (f32[4,192,512]{2,1,0:T(8,128)}, f32[4,192,512]{2,1,0:T(8,128)}, u32[]{:S(2)}, u32[]{:S(2)}) collective-permute-start(f32[4,192,512]{2,1,0:T(8,128)} %get-tuple-element.71), channel_id=1, source_target_pairs={{0,96},{1,97},{2,98},{3,99},{4,100},{5,101},{6,102},{7,103},{8,104... | collective-permute-start | bytes 4718600 | tf_op jit(solution)/shard_map/ppermute | solution.py:393
  51.9 3.4 %copy-start.20 = (f32[4,192,512]{2,1,0:T(8,128)}, f32[4,192,512]{2,1,0:T(8,128)S(1)}, u32[]{:S(2)}) copy-start(f32[4,192,512]{2,1,0:T(8,128)S(1)} %collective-permute-done.2.refs_2_) | copy-start | bytes 4718596
  51.9 36.2 %collective-permute-start.4 = (f32[4,192,512]{2,1,0:T(8,128)}, f32[4,192,512]{2,1,0:T(8,128)}, u32[]{:S(2)}, u32[]{:S(2)}) collective-permute-start(f32[4,192,512]{2,1,0:T(8,128)} %get-tuple-element.66), channel_id=1, source_target_pairs={{0,4},{1,5},{2,6},{3,7},{4,8},{5,9},{6,10},{7,11},{8,12},{9,13},{1... | collective-permute-start | bytes 4718600 | tf_op jit(solution)/shard_map/ppermute | solution.py:393
  54.0 1.3 copy-start.21
  54.0 34.0 %collective-permute-start.5 = (f32[4,192,512]{2,1,0:T(8,128)}, f32[4,192,512]{2,1,0:T(8,128)}, u32[]{:S(2)}, u32[]{:S(2)}) collective-permute-start(f32[4,192,512]{2,1,0:T(8,128)} %get-tuple-element.67), channel_id=1, source_target_pairs={{0,12},{1,13},{2,14},{3,15},{4,0},{5,1},{6,2},{7,3},{8,4},{9,5},{1... | collective-permute-start | bytes 4718600 | tf_op jit(solution)/shard_map/ppermute | solution.py:393
  84.7 1.1 copy-start.16
  85.9 33.5 %collective-permute-start.10 = (f32[4,192,512]{2,1,0:T(8,128)}, f32[4,192,512]{2,1,0:T(8,128)}, u32[]{:S(2)}, u32[]{:S(2)}) collective-permute-start(f32[4,192,512]{2,1,0:T(8,128)} %get-tuple-element.72.refs_4_), channel_id=1, source_target_pairs={{0,96},{1,97},{2,98},{3,99},{4,100},{5,101},{6,102},{7,103},{8,104... | collective-permute-start | bytes 4718600 | tf_op jit(solution)/shard_map/ppermute | solution.py:393
  87.1 34.0 %collective-permute-start.8 = (f32[4,192,512]{2,1,0:T(8,128)}, f32[4,192,512]{2,1,0:T(8,128)}, u32[]{:S(2)}, u32[]{:S(2)}) collective-permute-start(f32[4,192,512]{2,1,0:T(8,128)} %get-tuple-element.76), channel_id=1, source_target_pairs={{0,32},{1,33},{2,34},{3,35},{4,36},{5,37},{6,38},{7,39},{8,40},{9,... | collective-permute-start | bytes 4718600 | tf_op jit(solution)/shard_map/ppermute | solution.py:393
  88.1 42.1 %collective-permute-start.11 = (f32[4,192,512]{2,1,0:T(8,128)}, f32[4,192,512]{2,1,0:T(8,128)S(1)}, u32[]{:S(2)}, u32[]{:S(2)}) collective-permute-start(f32[4,192,512]{2,1,0:T(8,128)} %get-tuple-element.80), channel_id=1, source_target_pairs={{0,4},{1,5},{2,6},{3,7},{4,8},{5,9},{6,10},{7,11},{8,12},{9,13},{1... | collective-permute-start | bytes 4718600 | tf_op jit(solution)/shard_map/ppermute | solution.py:393
  89.8 40.4 %collective-permute-start.12 = (f32[4,192,512]{2,1,0:T(8,128)}, f32[4,192,512]{2,1,0:T(8,128)S(1)}, u32[]{:S(2)}, u32[]{:S(2)}) collective-permute-start(f32[4,192,512]{2,1,0:T(8,128)} %get-tuple-element.73.after), channel_id=1, source_target_pairs={{0,12},{1,13},{2,14},{3,15},{4,0},{5,1},{6,2},{7,3},{8,4},{9,5},{1... | collective-permute-start | bytes 4718600 | tf_op jit(solution)/shard_map/ppermute | solution.py:393
  126.0 30.8 %collective-permute-start.13 = (f32[2,336,512]{2,1,0:T(8,128)}, f32[2,336,512]{2,1,0:T(8,128)S(1)}, u32[]{:S(2)}, u32[]{:S(2)}) collective-permute-start(f32[2,336,512]{2,1,0:T(8,128)} %get-tuple-element.85), channel_id=1, source_target_pairs={{0,4},{1,5},{2,6},{3,7},{4,8},{5,9},{6,10},{7,11},{8,12},{9,13},{1... | collective-permute-start | bytes 4128776 | tf_op jit(solution)/shard_map/ppermute | solution.py:393
  128.9 29.9 %collective-permute-start.14 = (f32[2,336,512]{2,1,0:T(8,128)}, f32[2,336,512]{2,1,0:T(8,128)S(1)}, u32[]{:S(2)}, u32[]{:S(2)}) collective-permute-start(f32[2,336,512]{2,1,0:T(8,128)} %get-tuple-element.78.after), channel_id=1, source_target_pairs={{0,12},{1,13},{2,14},{3,15},{4,0},{5,1},{6,2},{7,3},{8,4},{9,5},{1... | collective-permute-start | bytes 4128776 | tf_op jit(solution)/shard_map/ppermute | solution.py:393
  130.1 1.1 copy-start.14
  130.2 1.8 copy-start.15
  136.7 27.5 %collective-permute-start.15 = (f32[2,320,512]{2,1,0:T(8,128)}, f32[2,320,512]{2,1,0:T(8,128)S(1)}, u32[]{:S(2)}, u32[]{:S(2)}) collective-permute-start(f32[2,320,512]{2,1,0:T(8,128)} %get-tuple-element.88), channel_id=1, source_target_pairs={{0,32},{1,33},{2,34},{3,35},{4,36},{5,37},{6,38},{7,39},{8,40},{9,... | collective-permute-start | bytes 3932168 | tf_op jit(solution)/shard_map/ppermute | solution.py:393
  136.7 28.1 %collective-permute-start.16 = (f32[2,320,512]{2,1,0:T(8,128)}, f32[2,320,512]{2,1,0:T(8,128)S(1)}, u32[]{:S(2)}, u32[]{:S(2)}) collective-permute-start(f32[2,320,512]{2,1,0:T(8,128)} %get-tuple-element.82.after), channel_id=1, source_target_pairs={{0,96},{1,97},{2,98},{3,99},{4,100},{5,101},{6,102},{7,103},{8,104... | collective-permute-start | bytes 3932168 | tf_op jit(solution)/shard_map/ppermute | solution.py:393
  144.3 12.5 %copy-start.6 = (f32[336,512]{1,0:T(8,128)S(1)}, f32[336,512]{1,0:T(8,128)}, u32[]{:S(2)}) copy-start(f32[336,512]{1,0:T(8,128)} %get-tuple-element.86.refs_1_) | copy-start | bytes 2064388
  144.3 12.5 %copy-start.10 = (s32[3]{0:T(128)S(1)}, s32[3]{0:T(128)}, u32[]{:S(2)}) copy-start(s32[3]{0:T(128)} %pad_add_fusion.where) | copy-start | bytes 40
  144.3 12.5 %copy-start.11 = (s32[32]{0:T(128)S(1)}, s32[32]{0:T(128)}, u32[]{:S(2)}) copy-start(s32[32]{0:T(128)} %table.43) | copy-start | bytes 388
  156.8 1.3 copy-start.1
  158.1 1.1 copy-start.5
  159.2 5.0 %copy-start.8 = (f32[320,512]{1,0:T(8,128)S(1)}, f32[320,512]{1,0:T(8,128)}, u32[]{:S(2)}) copy-start(f32[320,512]{1,0:T(8,128)} %get-tuple-element.89.refs_1_) | copy-start | bytes 1966084
  159.9 12.4 %collective-permute-start.18 = (f32[336,512]{1,0:T(8,128)S(1)}, f32[336,512]{1,0:T(8,128)S(1)}, u32[]{:S(2)}, u32[]{:S(2)}) collective-permute-start(f32[336,512]{1,0:T(8,128)S(1)} %shard_map.70.after), channel_id=1, source_target_pairs={{0,12},{1,13},{2,14},{3,15},{4,0},{5,1},{6,2},{7,3},{8,4},{9,5},{1... | collective-permute-start | bytes 2064392 | tf_op jit(solution)/shard_map/ppermute | solution.py:393
  161.1 13.0 %collective-permute-start.17 = (f32[336,512]{1,0:T(8,128)S(1)}, f32[336,512]{1,0:T(8,128)S(1)}, u32[]{:S(2)}, u32[]{:S(2)}) collective-permute-start(f32[336,512]{1,0:T(8,128)S(1)} %shard_map.69.after), channel_id=1, source_target_pairs={{0,4},{1,5},{2,6},{3,7},{4,8},{5,9},{6,10},{7,11},{8,12},{9,13},{1... | collective-permute-start | bytes 2064392 | tf_op jit(solution)/shard_map/ppermute | solution.py:393
  164.2 1.1 copy-start.7
  165.3 8.8 %copy-start = (f32[2,336,512]{2,1,0:T(8,128)S(1)}, f32[2,336,512]{2,1,0:T(8,128)}, u32[]{:S(2)}) copy-start(f32[2,336,512]{2,1,0:T(8,128)} %get-tuple-element.83.after.refs_0_) | copy-start | bytes 4128772
  165.9 12.8 %copy-start.2 = (f32[2,320,512]{2,1,0:T(8,128)S(1)}, f32[2,320,512]{2,1,0:T(8,128)}, u32[]{:S(2)}) copy-start(f32[2,320,512]{2,1,0:T(8,128)} %get-tuple-element.84.after.refs_0_) | copy-start | bytes 3932164
  165.9 11.1 %collective-permute-start.20 = (f32[320,512]{1,0:T(8,128)S(1)}, f32[320,512]{1,0:T(8,128)S(1)}, u32[]{:S(2)}, u32[]{:S(2)}) collective-permute-start(f32[320,512]{1,0:T(8,128)S(1)} %shard_map.72.after), channel_id=1, source_target_pairs={{0,96},{1,97},{2,98},{3,99},{4,100},{5,101},{6,102},{7,103},{8,104... | collective-permute-start | bytes 1966088 | tf_op jit(solution)/shard_map/ppermute | solution.py:393
  167.3 11.4 %collective-permute-start.19 = (f32[320,512]{1,0:T(8,128)S(1)}, f32[320,512]{1,0:T(8,128)S(1)}, u32[]{:S(2)}, u32[]{:S(2)}) collective-permute-start(f32[320,512]{1,0:T(8,128)S(1)} %shard_map.71.after), channel_id=1, source_target_pairs={{0,32},{1,33},{2,34},{3,35},{4,36},{5,37},{6,38},{7,39},{8,40},{9,... | collective-permute-start | bytes 1966088 | tf_op jit(solution)/shard_map/ppermute | solution.py:393
  175.0 22.2 %collective-permute-start.27 = (f32[192,512]{1,0:T(8,128)S(1)}, f32[192,512]{1,0:T(8,128)S(1)}, u32[]{:S(2)}, u32[]{:S(2)}) collective-permute-start(f32[192,512]{1,0:T(8,128)S(1)} %get-tuple-element.101), channel_id=1, source_target_pairs={{0,16},{1,17},{2,18},{3,19},{4,20},{5,21},{6,22},{7,23},{8,24},{9,... | collective-permute-start | bytes 1179656 | tf_op jit(solution)/shard_map/ppermute | solution.py:393
  179.6 18.2 %copy-start.9 = (f32[192,512]{1,0:T(8,128)}, f32[192,512]{1,0:T(8,128)S(1)}, u32[]{:S(2)}) copy-start(f32[192,512]{1,0:T(8,128)S(1)} %get-tuple-element.102.refs_1_) | copy-start | bytes 1179652
  179.6 19.0 %collective-permute-start.28 = (f32[192,512]{1,0:T(8,128)S(1)}, f32[192,512]{1,0:T(8,128)S(1)}, u32[]{:S(2)}, u32[]{:S(2)}) collective-permute-start(f32[192,512]{1,0:T(8,128)S(1)} %get-tuple-element.103), channel_id=1, source_target_pairs={{0,16},{1,17},{2,18},{3,19},{4,20},{5,21},{6,22},{7,23},{8,24},{9,... | collective-permute-start | bytes 1179656 | tf_op jit(solution)/shard_map/ppermute | solution.py:393
  180.7 7.4 %collective-permute-start.21 = (f32[72,512]{1,0:T(8,128)S(1)}, f32[72,512]{1,0:T(8,128)S(1)}, u32[]{:S(2)}, u32[]{:S(2)}) collective-permute-start(f32[72,512]{1,0:T(8,128)S(1)} %get-tuple-element.94), channel_id=1, source_target_pairs={{0,32},{1,33},{2,34},{3,35},{4,36},{5,37},{6,38},{7,39},{8,40},{9,... | collective-permute-start | bytes 442376 | tf_op jit(solution)/shard_map/ppermute | solution.py:393
  180.7 7.4 %collective-permute-start.22 = (f32[72,512]{1,0:T(8,128)S(1)}, f32[72,512]{1,0:T(8,128)S(1)}, u32[]{:S(2)}, u32[]{:S(2)}) collective-permute-start(f32[72,512]{1,0:T(8,128)S(1)} %get-tuple-element.95), channel_id=1, source_target_pairs={{0,64},{1,65},{2,66},{3,67},{4,68},{5,69},{6,70},{7,71},{8,72},{9,... | collective-permute-start | bytes 442376 | tf_op jit(solution)/shard_map/ppermute | solution.py:393
  183.5 7.0 %collective-permute-start.23 = (f32[72,512]{1,0:T(8,128)S(1)}, f32[72,512]{1,0:T(8,128)S(1)}, u32[]{:S(2)}, u32[]{:S(2)}) collective-permute-start(f32[72,512]{1,0:T(8,128)S(1)} %get-tuple-element.91.after), channel_id=1, source_target_pairs={{0,96},{1,97},{2,98},{3,99},{4,100},{5,101},{6,102},{7,103},{8,104... | collective-permute-start | bytes 442376 | tf_op jit(solution)/shard_map/ppermute | solution.py:393
  188.1 6.4 %collective-permute-start.24 = (f32[64,512]{1,0:T(8,128)S(1)}, f32[64,512]{1,0:T(8,128)S(1)}, u32[]{:S(2)}, u32[]{:S(2)}) collective-permute-start(f32[64,512]{1,0:T(8,128)S(1)} %get-tuple-element.98), channel_id=1, source_target_pairs={{0,4},{1,5},{2,6},{3,7},{4,8},{5,9},{6,10},{7,11},{8,12},{9,13},{1... | collective-permute-start | bytes 393224 | tf_op jit(solution)/shard_map/ppermute | solution.py:393
  188.1 8.4 %collective-permute-start.25 = (f32[64,512]{1,0:T(8,128)S(1)}, f32[64,512]{1,0:T(8,128)S(1)}, u32[]{:S(2)}, u32[]{:S(2)}) collective-permute-start(f32[64,512]{1,0:T(8,128)S(1)} %get-tuple-element.99), channel_id=1, source_target_pairs={{0,8},{1,9},{2,10},{3,11},{4,12},{5,13},{6,14},{7,15},{8,0},{9,1},... | collective-permute-start | bytes 393224 | tf_op jit(solution)/shard_map/ppermute | solution.py:393
  190.5 6.1 %collective-permute-start.26 = (f32[64,512]{1,0:T(8,128)S(1)}, f32[64,512]{1,0:T(8,128)S(1)}, u32[]{:S(2)}, u32[]{:S(2)}) collective-permute-start(f32[64,512]{1,0:T(8,128)S(1)} %get-tuple-element.92.after), channel_id=1, source_target_pairs={{0,12},{1,13},{2,14},{3,15},{4,0},{5,1},{6,2},{7,3},{8,4},{9,5},{1... | collective-permute-start | bytes 393224 | tf_op jit(solution)/shard_map/ppermute | solution.py:393
  192.1 6.4 %copy-start.12 = (f32[64,512]{1,0:T(8,128)}, f32[64,512]{1,0:T(8,128)S(1)}, u32[]{:S(2)}) copy-start(f32[64,512]{1,0:T(8,128)S(1)} %get-tuple-element.104.refs_4_) | copy-start | bytes 393220
  192.2 6.4 %copy-start.13 = (f32[8,512]{1,0:T(8,128)}, f32[8,512]{1,0:T(8,128)S(1)}, u32[]{:S(2)}) copy-start(f32[8,512]{1,0:T(8,128)S(1)} %get-tuple-element.96.after.refs_5_) | copy-start | bytes 49156
  194.6 4.0 %collective-permute-start.29 = (f32[8,512]{1,0:T(8,128)S(1)}, f32[8,512]{1,0:T(8,128)S(1)}, u32[]{:S(2)}, u32[]{:S(2)}) collective-permute-start(f32[8,512]{1,0:T(8,128)S(1)} %get-tuple-element.96.after.refs_5_), channel_id=1, source_target_pairs={{0,16},{1,17},{2,18},{3,19},{4,20},{5,21},{6,22},{7,23},{8,24},{9,... | collective-permute-start | bytes 49160 | tf_op jit(solution)/shard_map/ppermute | solution.py:393
  197.2 1.4 copy-start.4
  197.8 0.8 copy-start.3
  198.6 0.6 copy-start.23
  198.6 0.8 copy-start.22
  206.7 14.0 %collective-permute-start.30 = (f32[512,512]{1,0:T(8,128)}, f32[512,512]{1,0:T(8,128)S(1)}, u32[]{:S(2)}, u32[]{:S(2)}) collective-permute-start(f32[512,512]{1,0:T(8,128)} %shard_map.78), channel_id=1, source_target_pairs={{0,16},{1,17},{2,18},{3,19},{4,20},{5,21},{6,22},{7,23},{8,24},{9,... | collective-permute-start | bytes 3145736 | tf_op jit(solution)/shard_map/ppermute | solution.py:393
  207.6 26.6 %collective-permute-start.31 = (f32[512,512]{1,0:T(8,128)}, f32[512,512]{1,0:T(8,128)S(1)}, u32[]{:S(2)}, u32[]{:S(2)}) collective-permute-start(f32[512,512]{1,0:T(8,128)} %shard_map.78), channel_id=1, source_target_pairs={{0,18},{1,19},{2,16},{3,17},{4,22},{5,23},{6,20},{7,21},{8,26},{9,... | collective-permute-start | bytes 3145736 | tf_op jit(solution)/shard_map/ppermute | solution.py:393
  220.8 16.3 %collective-permute-start.32 = (f32[512,512]{1,0:T(8,128)S(1)}, f32[512,512]{1,0:T(8,128)S(1)}, u32[]{:S(2)}, u32[]{:S(2)}) collective-permute-start(f32[512,512]{1,0:T(8,128)S(1)} %collective-permute-done.30), channel_id=1, source_target_pairs={{0,1},{1,0},{2,3},{3,2},{4,5},{5,4},{6,7},{7,6},{8,9},{9,8},{10,11... | collective-permute-start | bytes 3145736 | tf_op jit(solution)/shard_map/ppermute | solution.py:393
  234.2 4.6 %collective-permute-start.33 = (f32[512,512]{1,0:T(8,128)S(1)}, f32[512,512]{1,0:T(8,128)}, u32[]{:S(2)}, u32[]{:S(2)}) collective-permute-start(f32[512,512]{1,0:T(8,128)S(1)} %collective-permute-done.31), channel_id=1, source_target_pairs={{0,1},{1,0},{2,3},{3,2},{4,5},{5,4},{6,7},{7,6},{8,9},{9,8},{10,11... | collective-permute-start | bytes 3145736 | tf_op jit(solution)/shard_map/ppermute | solution.py:393
  237.2 2.0 copy-start.17

commit v2 on v1

--- a/solution.py
+++ b/solution.py
@@ -12,10 +12,10 @@
 NX, NZ, NY = 4, 2, 4
 N_TM, N_FSDP = 32, 4
 BLK = 512
-ROWS_A = 192
-ROWS_C = (BLK - 2 * ROWS_A) // 2
+ROWS_A = 208
+ROWS_C = BLK - 2 * ROWS_A
 EXTRA = 8
-SMALL, LARGE = 16 * 1024 * 1024, 56 * 1024 * 1024
+SMALL, TURN, LARGE = 16 * 1024 * 1024, 30 * 1024 * 1024, 56 * 1024 * 1024
 
 
 def flat(x, zl, y, zh, core):
@@ -188,7 +188,7 @@
 def products(order, turned, latents, jobs, got=()):
     outs = []
     for stream, sub, r in jobs:
-        n, rows = (4, ROWS_A) if stream in "xy" else (16, 2 * ROWS_C)
+        n, rows = (4, ROWS_A) if stream in "xy" else (16, ROWS_C)
         outs.append(((n, rows, BLK), spec((n // 4, rows, BLK), lambda i, t, w: (i, 0, 0))))
     return order(
         functools.partial(products_body, jobs),
@@ -221,92 +221,74 @@
     return order(relay_body, 4, ins, [(got[0].shape, here)] * 4, vmem=LARGE)
 
 
-def half_rows(stream):
-    return ROWS_A + 2 * (ROWS_C + (EXTRA if stream == "x" else 0))
-
-
 MESSAGES = ((2, 0, (0, 0)), (1, 1, (0, 1)), (2, 1, (1, 0)), (3, 0, (1, 1)))
 TERMS = ((1, 0, (0,)), (3, 1, (1,)), (0, 0, (2, 0)), (0, 1, (2, 1)))
 
 
-def turn_body(stream, jobs, table, where, *refs):
-    sums = refs[16:19] if stream == "x" else ()
-    outs = refs[16 + len(sums) :]
-    rows = (half_rows(stream) - ROWS_A) // 2
-    for n, (r, half, place) in enumerate(jobs):
-        base, more, got, term = refs[4 * n : 4 * n + 4]
+def turn_body(jobs, table, where, *refs):
+    ins, outs = refs[: 2 * len(jobs)], refs[2 * len(jobs) :]
+    for n, place in enumerate(jobs):
         out = outs[place[0]].at[place[1]] if len(place) == 2 else outs[place[0]]
-        out[:ROWS_A, :] = base[0] + more[0]
-        for v in range(2):
-            at = (0, v) if stream == "y" else (v, 0)
-            low = ROWS_A + v * rows
-            out[low : low + ROWS_C, :] = got[at] + term[at]
-            if stream == "y":
-                continue
-            first_in, second_in, sums_out = sums
-            parts = []
-            for sub in (1, 0):
-                block = table[spot(where, "y", r, sub, 2 * half + v)]
-                a = block >> 2
-                parts.append(jnp.where(a < 4, first_in[a & 3], second_in[a & 3]))
-                parts.append(sums_out[block & 3])
-            parts.append(jnp.zeros((EXTRA - 4, BLK), jnp.float32))
-            out[low + ROWS_C : low + rows, :] = jnp.concatenate(parts, axis=0)
-
-
-def turn(order, stream, jobs, halves, got, terms, sums):
-    ins = []
-    for r, half, _ in jobs:
-        if stream == "x":
-            here = lambda i, t, w, r=r: ((w[2] + r) & 3, 0, 0)
-            side = spec((2, 1, ROWS_C, BLK), lambda i, t, w, r=r, h=half: (h, (w[2] + r) & 3, 1, 0))
+        out[...] = ins[2 * n][0] + ins[2 * n + 1][0]
+
+
+def turn(order, streams, pieces, halves):
+    once = dict(pipeline_mode=pl.Buffered(1))
+    ins, jobs, outs = [], [], []
+    for stream in streams:
+        at = 2 if stream == "x" else 0
+        for r, half, place in pieces:
+            jobs.append((place[0] + len(outs), *place[1:]))
+            here = lambda i, t, w, at=at, r=r: ((w[at] + r) & 3, 0, 0)
+            ins += [(a, spec((1, ROWS_A, BLK), here, **once)) for a in halves[stream][half]]
+        if pieces is TERMS:
+            outs += [full(ROWS_A, BLK)] * 2 + [full(2, ROWS_A, BLK)]
         else:
-            here = lambda i, t, w, r=r: ((w[0] + r) & 3, 0, 0)
-            side = spec((1, 2, ROWS_C, BLK), lambda i, t, w, r=r, h=half: ((w[0] + r) & 3, h, 0, 0))
-        ins += [(a, spec((1, ROWS_A, BLK), here)) for a in halves[half]]
-        ins += [(a.reshape(4, 4, 2 * ROWS_C, BLK), side) for a in (got, terms)]
-    if stream == "x":
-        ins += [(s, whole(s)) for s in sums]
-    rows = half_rows(stream)
-    outs = [full(2, rows, BLK)] * 2
-    if jobs is TERMS:
-        outs = [full(rows, BLK)] * 2 + [full(2, rows, BLK)]
-    return order(functools.partial(turn_body, stream, jobs), 1, ins, outs, vmem=LARGE)
-
-
-def relay_half_body(table, where, message, term, out):
-    out[...] = message[0] + term[...]
-
-
-def relay_half(order, message, term):
-    rows = message.shape[1]
-    ins = [(message, spec((1, rows, BLK), lambda i, t, w: (0, 0, 0))), (term, whole(term))]
-    return order(relay_half_body, 1, ins, [full(rows, BLK)])[0]
-
-
-def end_body(stream, table, where, own, forth, back, more_forth, more_back, *outs):
-    halves = (
-        lambda a, b: own[0, a:b] + back[1, a:b] + more_forth[a:b, :],
-        lambda a, b: own[1, a:b] + forth[1, a:b] + more_back[a:b, :],
-    )
-    outs[0][...] = halves[0](0, ROWS_A)
-    outs[1][...] = halves[1](0, ROWS_A)
-    rows = (half_rows(stream) - ROWS_A) // 2
+            outs += [full(2, ROWS_A, BLK)] * 2
+    return order(functools.partial(turn_body, jobs), 1, ins, outs, vmem=TURN)
+
+
+def relay_half_body(table, where, *refs):
+    for message, term, out in zip(refs[:2], refs[2:4], refs[4:]):
+        out[...] = message[0] + term[...]
+
+
+def relay_half(order, messages, terms):
+    half = spec((1, ROWS_A, BLK), lambda i, t, w: (0, 0, 0))
+    ins = [(m, half) for m in messages] + [(a, whole(a)) for a in terms]
+    return order(relay_half_body, 1, ins, [full(ROWS_A, BLK)] * 2, cost=1.0)
+
+
+def end_body(table, where, own, forth, back, more_forth, more_back, away, keep):
+    away[...] = own[0] + back[0] + more_forth[...]
+    keep[...] = own[1] + forth[0] + more_back[...]
+
+
+def end(order, own, forth, back, more_forth, more_back):
+    half = spec((1, ROWS_A, BLK), lambda i, t, w: (1, 0, 0))
+    ins = [(own, whole(own)), (forth, half), (back, half)]
+    ins += [(a, whole(a)) for a in (more_forth, more_back)]
+    return order(end_body, 1, ins, [full(ROWS_A, BLK)] * 2, cost=1.0)
+
+
+def kept_body(table, where, got, term, ours, theirs, out):
+    i = pl.program_id(0)
     for u in range(4):
-        base = ROWS_A + (u % 2) * rows
-        slot = halves[u // 2](base, base + rows)
-        for d in range(4):
-
-            @pl.when(((where[0 if stream == "x" else 2] + d) & 3) == u)
-            def _():
-                outs[2 + d][...] = slot
-
-
-def end(order, stream, own, forth, back, more_forth, more_back):
-    rows = (half_rows(stream) - ROWS_A) // 2
-    outs = [full(ROWS_A, BLK)] * 2 + [full(rows, BLK)] * 4
-    ins = [(a, whole(a)) for a in (own, forth, back, more_forth, more_back)]
-    return order(functools.partial(end_body, stream), 1, ins, outs)
+        block = table[spot(where, "c", 0, 1, 4 * i + u)]
+        a, c = block >> 2, 8 + (block & 3)
+        out[u, :ROWS_C, :] = got[u] + term[u]
+        out[u, ROWS_C:, :] = jnp.concatenate(
+            [ours[a] + theirs[a], ours[c] + theirs[c], jnp.zeros((EXTRA - 2, BLK), jnp.float32)],
+            axis=0,
+        )
+
+
+def kept(order, got, terms, ours, theirs):
+    here = spec((4, ROWS_C, BLK), lambda i, t, w: (i, 0, 0))
+    ins = [(got, here), (terms, here), (ours, whole(ours)), (theirs, whole(theirs))]
+    rows = ROWS_C + EXTRA
+    out = ((16, rows, BLK), spec((4, rows, BLK), lambda i, t, w: (i, 0, 0)))
+    return order(kept_body, 4, ins, [out], vmem=TURN)[0]
 
 
 def sums_body(table, where, rows, basis, out):
@@ -330,37 +312,28 @@
     return order(sums_body, n, ins, [out], vmem=LARGE)[0]
 
 
-def total_body(table, where, *refs):
-    value = (refs[0][...] + refs[1][...]) + (refs[2][...] + refs[3][...])
-    refs[4][...] = value[:ROWS_C]
-    if len(refs) == 6:
-        refs[5][...] = value[ROWS_C:]
-
-
-def total(order, parts):
-    rows = parts[0].shape[0]
-    outs = [full(ROWS_C, BLK)] + ([full(EXTRA, BLK)] if rows > ROWS_C else [])
-    return order(total_body, 1, [(p, whole(p)) for p in parts], outs)
-
-
-def join_body(table, where, a, b, out):
-    out[...] = a[...] + b[...]
-
-
-def join(order, a, b):
-    return order(join_body, 1, [(a, whole(a)), (b, whole(b))], [full(*a.shape)])[0]
-
-
-def precondition_body(tokens_all, table, where, *refs):
-    x, y0, y1, cx, cy, ours, theirs = (r[...] for r in refs[:7])
-    basis_in, basis_out, out = refs[7:]
+def mine(w):
+    return w[0] * 8 + (1 - w[1]) * 4 + w[2]
+
+
+def rotate_body(table, where, first, second, basis, out):
+    out[...] = dot3(split(first[...] + second[...]), split(basis[0]), ((1,), (0,)))
+
+
+def rotate(order, first, second, eig_in):
+    ins = [(a, whole(a)) for a in (first, second)]
+    ins.append((eig_in, spec((1, BLK, BLK), lambda i, t, w: (t[mine(w)] >> 2, 0, 0))))
+    return order(rotate_body, 1, ins, [full(*first.shape)], vmem=LARGE)[0]
+
+
+def precondition_body(tokens_all, table, where, x, y0, y1, rest, basis_in, basis_out, out):
     scale = 1.0 / tokens_all
-    grad = jnp.concatenate([x, y0 + y1, cx, cy], axis=0) * scale
-    values_in = (ours[0:1] + theirs[2:3]) * scale
-    values_out = (ours[1:2] + theirs[3:4]) * scale
+    sums = rest[0, ROWS_C:, :] * scale
+    values_in, values_out = sums[0:1], sums[1:2]
     a = split(basis_in[0])
     b = split(basis_out[0])
-    rotated = dot3(split(grad), a, ((1,), (0,)))
+    late = jnp.concatenate([y0[...] + y1[...], rest[0, :ROWS_C, :]], axis=0)
+    rotated = jnp.concatenate([x[...], dot3(split(late), a, ((1,), (0,)))], axis=0) * scale
     rotated = dot3(b, split(rotated), ((0,), (0,)))
     scaled = rotated / (values_out.reshape(BLK, 1) * values_in + DAMPING)
     back = dot3(b, split(scaled), ((1,), (0,)))
@@ -368,7 +341,6 @@
 
 
 def precondition(tokens_all, order, parts, eig_in, eig_out):
-    mine = lambda w: w[0] * 8 + (1 - w[1]) * 4 + w[2]
     ins = [(q, whole(q)) for q in parts]
     ins.append((eig_in, spec((1, BLK, BLK), lambda i, t, w: (t[mine(w)] >> 2, 0, 0))))
     ins.append((eig_out, spec((1, BLK, BLK), lambda i, t, w: (t[mine(w)] & 3, 0, 0))))
@@ -377,7 +349,6 @@
         1,
         ins,
         [full(BLK, BLK)],
-        cost=3.0,
         vmem=LARGE,
     )[0]
 
@@ -394,7 +365,6 @@
     hop = lambda value, axis, d: send(value, pairs_far(axis, d))
     both = lambda forth, back, axis: [hop(forth, axis, 1), hop(back, axis, 3)]
     order = Order(table, where)
-    far = lambda parts, axis: [parts[0]] + [hop(parts[d], axis, d) for d in (1, 2, 3)]
 
     turned, *sets_a = first_products(order, latents, out_grads)
     got_a = both(*sets_a[:2], "x") + both(*sets_a[2:], "y")
@@ -402,45 +372,40 @@
     made = products(order, turned, latents, SETS_B + SETS_T)
     got_b = both(*made[:2], "x") + both(*made[2:4], "y")
     sets_t = relay(order, got_a, made[4:])
-    sums = [square_sums(order, latents, eig_in, 0, 4)]
+    sums = jnp.concatenate(
+        [
+            square_sums(order, latents, eig_in, 0, 4),
+            square_sums(order, latents, eig_in, 4, 4),
+            square_sums(order, out_grads, eig_out, 0, 4),
+        ]
+    )
+    got_sums = send(sums, near)
     got_t = both(*order.gate(sets_t[:2], got_b[:2]), "x")
     got_t += both(*order.gate(sets_t[2:], got_b[2:]), "y")
     got_b = [got_b[n] for n in (1, 0, 3, 2)]
     *own, terms_c = products(order, turned, latents, SETS_OWN + SETS_KEEP, got_b)
-    sums.append(square_sums(order, latents, eig_in, 4, 4))
-    sums.append(square_sums(order, out_grads, eig_out, 0, 4))
-
-    def pieces(stream, jobs):
-        n = 0 if stream == "x" else 2
-        halves = ((own[n], got_t[n]), (own[n + 1], got_t[n + 1]))
-        return turn(order, stream, jobs, halves, got_c, terms_c, sums)
-
-    msgs_x = both(*pieces("x", MESSAGES), "y")
-    msgs_y = both(*pieces("y", MESSAGES), "x")
-    *parts_x, mine_x = pieces("x", TERMS)
-    *parts_y, mine_y = pieces("y", TERMS)
-
-    def follow(stream, messages, parts):
-        more = [relay_half(order, m, p) for m, p in zip(messages, parts)]
-        return both(*more, "y" if stream == "x" else "x")
-
-    more_x = follow("x", msgs_x, parts_x)
-    more_y = follow("y", msgs_y, parts_y)
-
-    away_x, keep_x, *parts_cy = end(order, "x", mine_x, *msgs_x, *more_x)
+
+    rest = kept(order, got_c, terms_c, sums, got_sums)
+    planes = [[x * 8 + z * 4 + y for x in range(NX) for y in range(NY)] for z in range(NZ)]
+    rest = lax.psum_scatter(rest, "tm", axis_index_groups=planes, tiled=True)
+    halves = {
+        stream: ((own[n], got_t[n]), (own[n + 1], got_t[n + 1]))
+        for n, stream in ((0, "x"), (2, "y"))
+    }
+    messages = turn(order, "xy", MESSAGES, halves)
+    msgs_x, msgs_y = both(*messages[:2], "y"), both(*messages[2:], "x")
+    *parts_x, mine_x = turn(order, "x", TERMS, halves)
+    *parts_y, mine_y = turn(order, "y", TERMS, halves)
+    more_x = both(*relay_half(order, msgs_x, parts_x), "y")
+    more_y = both(*relay_half(order, msgs_y, parts_y), "x")
+
+    away_x, keep_x = end(order, mine_x, *msgs_x, *more_x)
     got_x = send(away_x, near)
-    away_y, keep_y, *parts_cx = end(order, "y", mine_y, *msgs_y, *more_y)
+    away_y, keep_y = end(order, mine_y, *msgs_y, *more_y)
     got_y = send(away_y, near)
-    done_cy, ours = total(order, far(parts_cy, "x"))
-    theirs = send(ours, near)
-    (done_cx,) = total(order, far(parts_cx, "y"))
-    done_x = join(order, keep_x, got_x)
+    turned_x = rotate(order, keep_x, got_x, eig_in)
     update = precondition(
-        tokens_all,
-        order,
-        [done_x, keep_y, got_y, done_cx, done_cy, ours, theirs],
-        eig_in,
-        eig_out,
+        tokens_all, order, [turned_x, keep_y, got_y, rest], eig_in, eig_out
     )
     same = send(update, near)
     other = send(update, cross)

time: 242 us -> 265 us (1.095)
  waiting for transfers between devices: 64.8 us -> 94.7 us
  between operations: 0.3 us -> 13.6 us
  Pallas kernels: 107 us -> 94.2 us
  starting transfers between devices: 58.4 us -> 50.6 us
    ppermute x34 -> x28, waiting for transfers between devices: 64.8 us -> 94.6 us  [on_device(): send = lambda value, pairs: lax.ppermute(value, AXES, pairs)]
    pallas_call x22 -> x18, Pallas kernels: 107 us -> 94.2 us  [__call__(): pl.pallas_call(inner, out_shape=shapes, grid_spec=pltpu.PrefetchScalarGri...]
    ppermute x34 -> x28, starting transfers between devices: 58.4 us -> 50.6 us  [on_device(): send = lambda value, pairs: lax.ppermute(value, AXES, pairs)]
    unnamed x48 -> x32, local copies, waits for them, and re-layouts: 7.08 us -> 7.56 us
  transfers between devices with their start and end apart: 34 -> 29, of which waited for: 15 -> 11; matrix products, arithmetic and copies ran while one was open for 0% -> 1% of each run, Pallas kernels for 36% -> 27%
where the time goes in v2:
time: 265 us
  waiting for transfers between devices  94.7 us (36%)
  Pallas kernels  94.2 us (36%)
  starting transfers between devices  50.6 us (19%)
  between operations  13.6 us (5%)
  local copies, waits for them, and re-layouts  10.6 us (4%)
    ppermute x28, waiting for transfers between devices, on_device(): send = lambda value, pairs: lax.ppermute(value, AXES, pairs)  94.6 us
    pallas_call x18, Pallas kernels, __call__(): pl.pallas_call(inner, out_shape=shapes, grid_spec=pltpu.PrefetchScalarGri...  94.2 us
    ppermute x28, starting transfers between devices, on_device(): send = lambda value, pairs: lax.ppermute(value, AXES, pairs)  50.6 us
    unnamed x32, local copies, waits for them, and re-layouts  7.56 us
  transfers between devices with their start and end apart: 29, of which 11 were waited for; matrix products, arithmetic and copies ran while one was open for 1% of the time, Pallas kernels for 27%

profile of v2, /device:TPU:1, one launch (start us, length us, event | category | flops | bytes accessed | tf_op | source)
XLA Modules:
  0.0 265.1 jit_solution(17861939895912589809)
XLA Ops:
  6.5 0.6 pad_add_fusion.where
  7.2 12.1 %shard_map.55 = (bf16[2048,768]{1,0:T(8,128)(2,1)}, f32[4,208,512]{2,1,0:T(8,128)}, f32[4,208,512]{2,1,0:T(8,128)}, f32[4,208,512]{2,1,0:T(8,128)}, f32[4,208,512]{2,1,0:T(8,128)}) custom-call(s32[32]{0:T(128)} %table.35, s32[3]{0:T(128)} %pad_add_fusion.where, bf16[768,2048]{1,0:T(8,128)(2,1)} %refs_0_.7, bf16[768,4096]{1,0:T(8,128)(2,1)} %refs_1_.13, ...), custom_call_target="tpu_custom_call" | custom-call | bytes 3690000 | tf_op jit(solution)/shard_map/pallas_call | solution.py:115
  19.2 2.1 collective-permute-start
  21.3 1.3 collective-permute-start.1
  22.7 1.1 collective-permute-start.2
  23.7 1.8 collective-permute-start.3
  25.5 8.2 %shard_map.56.after = f32[16,96,512]{2,1,0:T(8,128)} custom-call(s32[32]{0:T(128)} %table.35, s32[3]{0:T(128)} %pad_add_fusion.where, f32[4,208,512]{2,1,0:T(8,128)} %get-tuple-element.49.after, bf16[2048,768]{1,0:T(8,128)(2,1)} %get-tuple-element.50.refs_0_, bf16[768,4096]{1,0:T(8,128)(2,1)} %refs_1_.13), custom_call_target="tpu_custom_call" | custom-call | bytes 3690000 | tf_op jit(solution)/shard_map/pallas_call | solution.py:115
  33.7 1.7 collective-permute-start.8
  35.4 12.3 %shard_map.57 = (f32[4,208,512]{2,1,0:T(8,128)}, f32[4,208,512]{2,1,0:T(8,128)}, f32[4,208,512]{2,1,0:T(8,128)}, f32[4,208,512]{2,1,0:T(8,128)}, f32[4,208,512]{...) custom-call(s32[32]{0:T(128)} %table.35, s32[3]{0:T(128)} %pad_add_fusion.where, ...), custom_call_target="tpu_custom_call" | custom-call | bytes 3690000 | tf_op jit(solution)/shard_map/pallas_call | solution.py:115
  47.7 11.7 %collective-permute-done.refs_0_ = f32[4,208,512]{2,1,0:T(8,128)S(1)} collective-permute-done((f32[4,208,512]{2,1,0:T(8,128)}, f32[4,208,512]{2,1,0:T(8,128)S(1)}, u32[]{:S(2)}, u32[]{:S(2)}) %collective-permute-start) | collective-permute-done | bytes 1703968 | tf_op jit(solution)/shard_map/ppermute | solution.py:364
  59.4 0.3 collective-permute-start.6
  59.7 2.3 collective-permute-start.7
  62.1 1.1 collective-permute-start.4
  63.2 2.0 collective-permute-start.5
  65.2 8.4 %shard_map.58 = (f32[4,208,512]{2,1,0:T(8,128)}, f32[4,208,512]{2,1,0:T(8,128)}, f32[4,208,512]{2,1,0:T(8,128)}, f32[4,208,512]{2,1,0:T(8,128)}) custom-call(s32[32]{0:T(128)} %table.35, s32[3]{0:T(128)} %pad_add_fusion.where, f32[4,208,512]{2,1,0:T(8,128)} %get-tuple-element.51.after.refs_7_, f32[4,208,512]{2,1,0:T(8,128)} %copy-done.10, ...), custom_call_target="tpu_custom_call" | custom-call | bytes 3690000 | tf_op jit(solution)/shard_map/pallas_call | solution.py:115
  73.6 7.3 %shard_map.59.after = f32[4,1,512]{2,1,0:T(1,128)} custom-call(s32[32]{0:T(128)} %table.35, s32[3]{0:T(128)} %pad_add_fusion.where, f32[4,208,512]{2,1,0:T(8,128)} %get-tuple-element.59.after.refs_1_, bf16[768,4096]{1,0:T(8,128)(2,1)} %refs_1_.13, f32[8,512,512]{2,1,0:T(8,128)} %refs_4_.1), custom_call_target="tpu_custom_call" | custom-call | bytes 3690000 | tf_op jit(solution)/shard_map/pallas_call | solution.py:115
  80.9 7.3 %shard_map.60.after = f32[4,1,512]{2,1,0:T(1,128)} custom-call(s32[32]{0:T(128)} %table.35, s32[3]{0:T(128)} %pad_add_fusion.where, f32[4,1,512]{2,1,0:T(1,128)} %shard_map.59.after, bf16[768,4096]{1,0:T(8,128)(2,1)} %refs_1_.13, f32[8,512,512]{2,1,0:T(8,128)} %refs_4_.1), custom_call_target="tpu_custom_call" | custom-call | bytes 3690000 | tf_op jit(solution)/shard_map/pallas_call | solution.py:115
  88.2 7.5 %shard_map.61.refs_4_ = f32[4,1,512]{2,1,0:T(1,128)} custom-call(s32[32]{0:T(128)} %table.35, s32[3]{0:T(128)} %pad_add_fusion.where, f32[4,1,512]{2,1,0:T(1,128)} %shard_map.60.after, bf16[768,2048]{1,0:T(8,128)(2,1)} %refs_0_.7, f32[4,512,512]{2,1,0:T(8,128)} %refs_5_.1), custom_call_target="tpu_custom_call" | custom-call | bytes 3690000 | tf_op jit(solution)/shard_map/pallas_call | solution.py:115
  95.7 0.7 pad_maximum_fusion.refs_2_
  96.4 1.6 collective-permute-done.6.refs_2_.refs_3_
  98.0 2.1 collective-permute-start.9
  100.1 0.8 collective-permute-done.4.refs_2_.refs_5_
  100.9 12.8 %shard_map.64 = (f32[4,208,512]{2,1,0:T(8,128)}, f32[4,208,512]{2,1,0:T(8,128)}, f32[4,208,512]{2,1,0:T(8,128)}, f32[4,208,512]{2,1,0:T(8,128)}, f32[16,96,512]{2,1,0:T(8,128)}) custom-call(s32[32]{0:T(128)} %table.35, s32[3]{0:T(128)} %pad_add_fusion.where, f32[4,208,512]{2,1,0:T(8,128)} %get-tuple-element.67.after, ...), custom_call_target="tpu_custom_call" | custom-call | bytes 3690000 | tf_op jit(solution)/shard_map/pallas_call | solution.py:115
  113.8 1.9 copy-done.4
  115.7 2.9 %shard_map.65.after = f32[16,104,512]{2,1,0:T(8,128)} custom-call(s32[32]{0:T(128)S(1)} %copy-done.8, s32[3]{0:T(128)S(1)} %copy-done.7, f32[16,96,512]{2,1,0:T(8,128)S(1)} %copy-done.4, f32[16,96,512]{2,1,0:T(8,128)S(1)} %collective-permute-done.8.refs_0_, f32[16,96,512]{2,1,0:T(8,128)S(1)} %copy-done.4, f32[12,1,512]{2,1,0:T(1,128)S(1)} %pad_maximum_fusion.refs_2_, ...), custom_call_target="tpu_custom_call" | custom-call | bytes 3690000 | tf_op jit(solution)/shard_map/pallas_call | solution.py:115
  118.6 2.6 collective-permute-start.13
  121.1 2.7 %collective-permute-start.11 = (f32[4,208,512]{2,1,0:T(8,128)}, f32[4,208,512]{2,1,0:T(8,128)S(1)}, u32[]{:S(2)}, u32[]{:S(2)}) collective-permute-start(f32[4,208,512]{2,1,0:T(8,128)} %get-tuple-element.66.refs_4_), channel_id=1, source_target_pairs={{0,96},{1,97},{2,98},{3,99},{4,100},{5,101},{6,102},{7,103},{8,104... | collective-permute-start | bytes 5111816 | tf_op jit(solution)/shard_map/ppermute | solution.py:364
  123.8 45.3 %collective-permute-done.12.refs_9_.refs_15_.refs_1_.refs_5_ = f32[4,208,512]{2,1,0:T(8,128)S(1)} collective-permute-done((f32[4,208,512]{2,1,0:T(8,128)}, f32[4,208,512]{2,1,0:T(8,128)S(1)}, u32[]{:S(2)}, u32[]{:S(2)}) %collective-permute-start.12) | collective-permute-done | bytes 1703968 | tf_op jit(solution)/shard_map/ppermute | solution.py:364
  169.1 1.5 copy-done.2
  170.6 1.5 copy-done.3
  172.1 0.9 shard_map.66
  173.1 2.9 %collective-permute-start.15 = (f32[2,208,512]{2,1,0:T(8,128)S(1)}, f32[2,208,512]{2,1,0:T(8,128)S(1)}, u32[]{:S(2)}, u32[]{:S(2)}) collective-permute-start(f32[2,208,512]{2,1,0:T(8,128)S(1)} %get-tuple-element.79), channel_id=1, source_target_pairs={{0,12},{1,13},{2,14},{3,15},{4,0},{5,1},{6,2},{7,3},{8,4},{9,5},{1... | collective-permute-start | bytes 2555912 | tf_op jit(solution)/shard_map/ppermute | solution.py:364
  176.0 2.9 %collective-permute-start.17 = (f32[2,208,512]{2,1,0:T(8,128)S(1)}, f32[2,208,512]{2,1,0:T(8,128)S(1)}, u32[]{:S(2)}, u32[]{:S(2)}) collective-permute-start(f32[2,208,512]{2,1,0:T(8,128)S(1)} %get-tuple-element.75.after), channel_id=1, source_target_pairs={{0,96},{1,97},{2,98},{3,99},{4,100},{5,101},{6,102},{7,103},{8,104... | collective-permute-start | bytes 2555912 | tf_op jit(solution)/shard_map/ppermute | solution.py:364
  178.8 0.7 shard_map.67
  179.5 0.8 shard_map.68
  180.3 10.0 %collective-permute-done.14.refs_0_.refs_1_ = f32[2,208,512]{2,1,0:T(8,128)S(1)} collective-permute-done((f32[2,208,512]{2,1,0:T(8,128)S(1)}, f32[2,208,512]{2,1,0:T(8,128)S(1)}, u32[]{:S(2)}, u32[]{:S(2)}) %collective-permute-start.14) | collective-permute-done | bytes 852000 | tf_op jit(solution)/shard_map/ppermute | solution.py:364
  190.3 0.6 shard_map.69
  191.0 0.6 collective-permute-start.18
  191.6 2.6 collective-permute-start.19
  194.2 0.6 shard_map.70
  194.9 2.7 %collective-permute-start.21 = (f32[208,512]{1,0:T(8,128)S(1)}, f32[208,512]{1,0:T(8,128)S(1)}, u32[]{:S(2)}, u32[]{:S(2)}) collective-permute-start(f32[208,512]{1,0:T(8,128)S(1)} %get-tuple-element.86.after), channel_id=1, source_target_pairs={{0,96},{1,97},{2,98},{3,99},{4,100},{5,101},{6,102},{7,103},{8,104... | collective-permute-start | bytes 1277960 | tf_op jit(solution)/shard_map/ppermute | solution.py:364
  197.6 6.3 %collective-permute-done.18.refs_3_ = f32[208,512]{1,0:T(8,128)S(1)} collective-permute-done((f32[208,512]{1,0:T(8,128)S(1)}, f32[208,512]{1,0:T(8,128)S(1)}, u32[]{:S(2)}, u32[]{:S(2)}) %collective-permute-start.18) | collective-permute-done | bytes 426016 | tf_op jit(solution)/shard_map/ppermute | solution.py:364
  203.9 0.7 shard_map.71
  204.6 1.3 collective-permute-start.22
  205.9 0.3 collective-permute-done.20.refs_3_
  206.1 0.7 shard_map.72
  206.8 0.8 copy-done.6
  207.6 1.2 collective-permute-start.23
  208.8 3.2 %collective-permute-done.22.refs_1_ = f32[208,512]{1,0:T(8,128)S(1)} collective-permute-done((f32[208,512]{1,0:T(8,128)S(1)}, f32[208,512]{1,0:T(8,128)S(1)}, u32[]{:S(2)}, u32[]{:S(2)}) %collective-permute-start.22) | collective-permute-done | bytes 426016 | tf_op jit(solution)/shard_map/ppermute | solution.py:364
  212.0 0.8 copy-done.13
  212.7 3.4 %shard_map.73.after.refs_0_ = f32[208,512]{1,0:T(8,128)} custom-call(s32[32]{0:T(128)} %table.35, s32[3]{0:T(128)} %pad_add_fusion.where, f32[208,512]{1,0:T(8,128)} %copy-done.6, f32[208,512]{1,0:T(8,128)} %copy-done.5, f32[208,512]{1,0:T(8,128)} %copy-done.13, f32[8,512,512]{2,1,0:T(8,128)} %refs_4_.1), custom_call_target="tpu_custom_call" | custom-call | bytes 3690000 | tf_op jit(solution)/shard_map/pallas_call | solution.py:115
  216.2 1.2 collective-permute-done.23.refs_2_
  217.4 0.8 copy-done.12
  218.2 7.1 %shard_map.74 = f32[512,512]{1,0:T(8,128)} custom-call(s32[32]{0:T(128)} %table.35, s32[3]{0:T(128)} %pad_add_fusion.where, f32[208,512]{1,0:T(8,128)} %shard_map.73.after.refs_0_, f32[208,512]{1,0:T(8,128)} %shard_map.73.after.refs_0_, f32[208,512]{1,0:T(8,128)} %copy-done.6, f32[208,512]{1,0:T(8,128)} %copy-done.12, ...), custom_call_target="tpu_custom_call" | custom-call | bytes 3690000 | tf_op jit(solution)/shard_map/pallas_call | solution.py:115
  225.2 0.6 collective-permute-start.24
  225.8 3.0 %collective-permute-start.25 = (f32[512,512]{1,0:T(8,128)}, f32[512,512]{1,0:T(8,128)S(1)}, u32[]{:S(2)}, u32[]{:S(2)}) collective-permute-start(f32[512,512]{1,0:T(8,128)} %shard_map.74), channel_id=1, source_target_pairs={{0,18},{1,19},{2,16},{3,17},{4,22},{5,23},{6,20},{7,21},{8,26},{9,... | collective-permute-start | bytes 3145736 | tf_op jit(solution)/shard_map/ppermute | solution.py:364
  228.8 12.6 %collective-permute-done.24 = f32[512,512]{1,0:T(8,128)S(1)} collective-permute-done((f32[512,512]{1,0:T(8,128)}, f32[512,512]{1,0:T(8,128)S(1)}, u32[]{:S(2)}, u32[]{:S(2)}) %collective-permute-start.24) | collective-permute-done | bytes 1048608 | tf_op jit(solution)/shard_map/ppermute | solution.py:364
  241.4 9.6 %collective-permute-start.26 = (f32[512,512]{1,0:T(8,128)S(1)}, f32[512,512]{1,0:T(8,128)S(1)}, u32[]{:S(2)}, u32[]{:S(2)}) collective-permute-start(f32[512,512]{1,0:T(8,128)S(1)} %collective-permute-done.24), channel_id=1, source_target_pairs={{0,1},{1,0},{2,3},{3,2},{4,5},{5,4},{6,7},{7,6},{8,9},{9,8},{10,11... | collective-permute-start | bytes 3145736 | tf_op jit(solution)/shard_map/ppermute | solution.py:364
  251.0 2.2 collective-permute-start.27
  253.2 0.5 broadcast_in_dim.17
  253.7 0.1 bitcast_dynamic-update-slice_fusion.3
  254.0 1.6 collective-permute-done.27
  255.6 0.4 copy-done.9
  256.0 2.3 bitcast_dynamic-update-slice_fusion
  (54 shorter events, 0.4 us)
Async XLA Ops:
  6.5 210.8 %reduce-scatter.4.cloned.1.call-start = ((), (), s32[]{:S(2)}) async-start(), calls=%async_computation.1 | async-start | bytes 3620864
  19.2 40.1 %collective-permute-start = (f32[4,208,512]{2,1,0:T(8,128)}, f32[4,208,512]{2,1,0:T(8,128)S(1)}, u32[]{:S(2)}, u32[]{:S(2)}) collective-permute-start(f32[4,208,512]{2,1,0:T(8,128)} %get-tuple-element.52), channel_id=1, source_target_pairs={{0,32},{1,33},{2,34},{3,35},{4,36},{5,37},{6,38},{7,39},{8,40},{9,... | collective-permute-start | bytes 5111816 | tf_op jit(solution)/shard_map/ppermute | solution.py:364
  21.3 38.4 %collective-permute-start.1 = (f32[4,208,512]{2,1,0:T(8,128)}, f32[4,208,512]{2,1,0:T(8,128)S(1)}, u32[]{:S(2)}, u32[]{:S(2)}) collective-permute-start(f32[4,208,512]{2,1,0:T(8,128)} %get-tuple-element.53), channel_id=1, source_target_pairs={{0,96},{1,97},{2,98},{3,99},{4,100},{5,101},{6,102},{7,103},{8,104... | collective-permute-start | bytes 5111816 | tf_op jit(solution)/shard_map/ppermute | solution.py:364
  22.7 39.4 %collective-permute-start.2 = (f32[4,208,512]{2,1,0:T(8,128)}, f32[4,208,512]{2,1,0:T(8,128)}, u32[]{:S(2)}, u32[]{:S(2)}) collective-permute-start(f32[4,208,512]{2,1,0:T(8,128)} %get-tuple-element.54), channel_id=1, source_target_pairs={{0,4},{1,5},{2,6},{3,7},{4,8},{5,9},{6,10},{7,11},{8,12},{9,13},{1... | collective-permute-start | bytes 5111816 | tf_op jit(solution)/shard_map/ppermute | solution.py:364
  23.7 39.5 %collective-permute-start.3 = (f32[4,208,512]{2,1,0:T(8,128)}, f32[4,208,512]{2,1,0:T(8,128)}, u32[]{:S(2)}, u32[]{:S(2)}) collective-permute-start(f32[4,208,512]{2,1,0:T(8,128)} %get-tuple-element.49.after), channel_id=1, source_target_pairs={{0,12},{1,13},{2,14},{3,15},{4,0},{5,1},{6,2},{7,3},{8,4},{9,5},{1... | collective-permute-start | bytes 5111816 | tf_op jit(solution)/shard_map/ppermute | solution.py:364
  33.7 80.0 %collective-permute-start.8 = (f32[16,96,512]{2,1,0:T(8,128)}, f32[16,96,512]{2,1,0:T(8,128)S(1)}, u32[]{:S(2)}, u32[]{:S(2)}) collective-permute-start(f32[16,96,512]{2,1,0:T(8,128)} %shard_map.56.after), channel_id=1, source_target_pairs={{0,16},{1,17},{2,18},{3,19},{4,20},{5,21},{6,22},{7,23},{8,24},{9,... | collective-permute-start | bytes 9437192 | tf_op jit(solution)/shard_map/ppermute | solution.py:364
  59.4 5.8 %copy-start.10 = (f32[4,208,512]{2,1,0:T(8,128)}, f32[4,208,512]{2,1,0:T(8,128)S(1)}, u32[]{:S(2)}) copy-start(f32[4,208,512]{2,1,0:T(8,128)S(1)} %collective-permute-done.refs_0_) | copy-start | bytes 5111812
  59.4 38.6 %collective-permute-start.6 = (f32[4,208,512]{2,1,0:T(8,128)}, f32[4,208,512]{2,1,0:T(8,128)}, u32[]{:S(2)}, u32[]{:S(2)}) collective-permute-start(f32[4,208,512]{2,1,0:T(8,128)} %get-tuple-element.64), channel_id=1, source_target_pairs={{0,32},{1,33},{2,34},{3,35},{4,36},{5,37},{6,38},{7,39},{8,40},{9,... | collective-permute-start | bytes 5111816 | tf_op jit(solution)/shard_map/ppermute | solution.py:364
  59.7 5.5 %copy-start.11 = (f32[4,208,512]{2,1,0:T(8,128)}, f32[4,208,512]{2,1,0:T(8,128)S(1)}, u32[]{:S(2)}) copy-start(f32[4,208,512]{2,1,0:T(8,128)S(1)} %collective-permute-done.1.refs_1_) | copy-start | bytes 5111812
  59.7 40.4 %collective-permute-start.7 = (f32[4,208,512]{2,1,0:T(8,128)}, f32[4,208,512]{2,1,0:T(8,128)}, u32[]{:S(2)}, u32[]{:S(2)}) collective-permute-start(f32[4,208,512]{2,1,0:T(8,128)} %get-tuple-element.65), channel_id=1, source_target_pairs={{0,96},{1,97},{2,98},{3,99},{4,100},{5,101},{6,102},{7,103},{8,104... | collective-permute-start | bytes 5111816 | tf_op jit(solution)/shard_map/ppermute | solution.py:364
  62.1 38.9 %collective-permute-start.4 = (f32[4,208,512]{2,1,0:T(8,128)}, f32[4,208,512]{2,1,0:T(8,128)}, u32[]{:S(2)}, u32[]{:S(2)}) collective-permute-start(f32[4,208,512]{2,1,0:T(8,128)} %get-tuple-element.60), channel_id=1, source_target_pairs={{0,4},{1,5},{2,6},{3,7},{4,8},{5,9},{6,10},{7,11},{8,12},{9,13},{1... | collective-permute-start | bytes 5111816 | tf_op jit(solution)/shard_map/ppermute | solution.py:364
  63.2 37.7 %collective-permute-start.5 = (f32[4,208,512]{2,1,0:T(8,128)}, f32[4,208,512]{2,1,0:T(8,128)}, u32[]{:S(2)}, u32[]{:S(2)}) collective-permute-start(f32[4,208,512]{2,1,0:T(8,128)} %get-tuple-element.61), channel_id=1, source_target_pairs={{0,12},{1,13},{2,14},{3,15},{4,0},{5,1},{6,2},{7,3},{8,4},{9,5},{1... | collective-permute-start | bytes 5111816 | tf_op jit(solution)/shard_map/ppermute | solution.py:364
  88.2 7.5 %copy-start.14 = (f32[4,1,512]{2,1,0:T(1,128)S(1)}, f32[4,1,512]{2,1,0:T(1,128)}, u32[]{:S(2)}) copy-start(f32[4,1,512]{2,1,0:T(1,128)} %shard_map.59.after) | copy-start | bytes 24580
  88.2 7.5 %copy-start.15 = (f32[4,1,512]{2,1,0:T(1,128)S(1)}, f32[4,1,512]{2,1,0:T(1,128)}, u32[]{:S(2)}) copy-start(f32[4,1,512]{2,1,0:T(1,128)} %shard_map.60.after) | copy-start | bytes 24580
  98.0 15.7 %collective-permute-start.9 = (f32[12,1,512]{2,1,0:T(1,128)S(1)}, f32[12,1,512]{2,1,0:T(1,128)S(1)}, u32[]{:S(2)}, u32[]{:S(2)}) collective-permute-start(f32[12,1,512]{2,1,0:T(1,128)S(1)} %pad_maximum_fusion.refs_2_), channel_id=1, source_target_pairs={{0,16},{1,17},{2,18},{3,19},{4,20},{5,21},{6,22},{7,23},{8,24},{9,... | collective-permute-start | bytes 73736 | tf_op jit(solution)/shard_map/ppermute | solution.py:364
  100.9 12.8 %copy-start.7 = (s32[3]{0:T(128)S(1)}, s32[3]{0:T(128)}, u32[]{:S(2)}) copy-start(s32[3]{0:T(128)} %pad_add_fusion.where) | copy-start | bytes 40
  100.9 12.8 %copy-start.8 = (s32[32]{0:T(128)S(1)}, s32[32]{0:T(128)}, u32[]{:S(2)}) copy-start(s32[32]{0:T(128)} %table.35) | copy-start | bytes 388
  113.8 1.9 copy-start.4
  118.5 50.6 %copy-start = (f32[4,208,512]{2,1,0:T(8,128)S(1)}, f32[4,208,512]{2,1,0:T(8,128)}, u32[]{:S(2)}) copy-start(f32[4,208,512]{2,1,0:T(8,128)} %get-tuple-element.72.refs_8_.refs_14_.refs_0_.refs_4_) | copy-start | bytes 5111812
  118.5 50.6 %copy-start.1 = (f32[4,208,512]{2,1,0:T(8,128)S(1)}, f32[4,208,512]{2,1,0:T(8,128)}, u32[]{:S(2)}) copy-start(f32[4,208,512]{2,1,0:T(8,128)} %get-tuple-element.74.refs_10_.refs_12_.refs_2_.refs_6_) | copy-start | bytes 5111812
  118.6 50.5 %collective-permute-start.13 = (f32[4,208,512]{2,1,0:T(8,128)}, f32[4,208,512]{2,1,0:T(8,128)S(1)}, u32[]{:S(2)}, u32[]{:S(2)}) collective-permute-start(f32[4,208,512]{2,1,0:T(8,128)} %get-tuple-element.67.after), channel_id=1, source_target_pairs={{0,12},{1,13},{2,14},{3,15},{4,0},{5,1},{6,2},{7,3},{8,4},{9,5},{1... | collective-permute-start | bytes 5111816 | tf_op jit(solution)/shard_map/ppermute | solution.py:364
  121.1 47.9 %collective-permute-start.12 = (f32[4,208,512]{2,1,0:T(8,128)}, f32[4,208,512]{2,1,0:T(8,128)S(1)}, u32[]{:S(2)}, u32[]{:S(2)}) collective-permute-start(f32[4,208,512]{2,1,0:T(8,128)} %get-tuple-element.73), channel_id=1, source_target_pairs={{0,4},{1,5},{2,6},{3,7},{4,8},{5,9},{6,10},{7,11},{8,12},{9,13},{1... | collective-permute-start | bytes 5111816 | tf_op jit(solution)/shard_map/ppermute | solution.py:364
  121.1 48.0 %collective-permute-start.10 = (f32[4,208,512]{2,1,0:T(8,128)}, f32[4,208,512]{2,1,0:T(8,128)S(1)}, u32[]{:S(2)}, u32[]{:S(2)}) collective-permute-start(f32[4,208,512]{2,1,0:T(8,128)} %get-tuple-element.70), channel_id=1, source_target_pairs={{0,32},{1,33},{2,34},{3,35},{4,36},{5,37},{6,38},{7,39},{8,40},{9,... | collective-permute-start | bytes 5111816 | tf_op jit(solution)/shard_map/ppermute | solution.py:364
  121.1 48.0 %collective-permute-start.11 = (f32[4,208,512]{2,1,0:T(8,128)}, f32[4,208,512]{2,1,0:T(8,128)S(1)}, u32[]{:S(2)}, u32[]{:S(2)}) collective-permute-start(f32[4,208,512]{2,1,0:T(8,128)} %get-tuple-element.66.refs_4_), channel_id=1, source_target_pairs={{0,96},{1,97},{2,98},{3,99},{4,100},{5,101},{6,102},{7,103},{8,104... | collective-permute-start | bytes 5111816 | tf_op jit(solution)/shard_map/ppermute | solution.py:364
  169.1 1.5 copy-start.2
  170.6 1.5 copy-start.3
  173.0 17.3 %collective-permute-start.14 = (f32[2,208,512]{2,1,0:T(8,128)S(1)}, f32[2,208,512]{2,1,0:T(8,128)S(1)}, u32[]{:S(2)}, u32[]{:S(2)}) collective-permute-start(f32[2,208,512]{2,1,0:T(8,128)S(1)} %get-tuple-element.78), channel_id=1, source_target_pairs={{0,4},{1,5},{2,6},{3,7},{4,8},{5,9},{6,10},{7,11},{8,12},{9,13},{1... | collective-permute-start | bytes 2555912 | tf_op jit(solution)/shard_map/ppermute | solution.py:364
  173.1 17.3 %collective-permute-start.15 = (f32[2,208,512]{2,1,0:T(8,128)S(1)}, f32[2,208,512]{2,1,0:T(8,128)S(1)}, u32[]{:S(2)}, u32[]{:S(2)}) collective-permute-start(f32[2,208,512]{2,1,0:T(8,128)S(1)} %get-tuple-element.79), channel_id=1, source_target_pairs={{0,12},{1,13},{2,14},{3,15},{4,0},{5,1},{6,2},{7,3},{8,4},{9,5},{1... | collective-permute-start | bytes 2555912 | tf_op jit(solution)/shard_map/ppermute | solution.py:364
  176.0 18.3 %collective-permute-start.16 = (f32[2,208,512]{2,1,0:T(8,128)S(1)}, f32[2,208,512]{2,1,0:T(8,128)S(1)}, u32[]{:S(2)}, u32[]{:S(2)}) collective-permute-start(f32[2,208,512]{2,1,0:T(8,128)S(1)} %get-tuple-element.83), channel_id=1, source_target_pairs={{0,32},{1,33},{2,34},{3,35},{4,36},{5,37},{6,38},{7,39},{8,40},{9,... | collective-permute-start | bytes 2555912 | tf_op jit(solution)/shard_map/ppermute | solution.py:364
  176.0 18.3 %collective-permute-start.17 = (f32[2,208,512]{2,1,0:T(8,128)S(1)}, f32[2,208,512]{2,1,0:T(8,128)S(1)}, u32[]{:S(2)}, u32[]{:S(2)}) collective-permute-start(f32[2,208,512]{2,1,0:T(8,128)S(1)} %get-tuple-element.75.after), channel_id=1, source_target_pairs={{0,96},{1,97},{2,98},{3,99},{4,100},{5,101},{6,102},{7,103},{8,104... | collective-permute-start | bytes 2555912 | tf_op jit(solution)/shard_map/ppermute | solution.py:364
  191.0 13.0 %collective-permute-start.18 = (f32[208,512]{1,0:T(8,128)S(1)}, f32[208,512]{1,0:T(8,128)S(1)}, u32[]{:S(2)}, u32[]{:S(2)}) collective-permute-start(f32[208,512]{1,0:T(8,128)S(1)} %get-tuple-element.87), channel_id=1, source_target_pairs={{0,4},{1,5},{2,6},{3,7},{4,8},{5,9},{6,10},{7,11},{8,12},{9,13},{1... | collective-permute-start | bytes 1277960 | tf_op jit(solution)/shard_map/ppermute | solution.py:364
  191.6 12.3 %collective-permute-start.19 = (f32[208,512]{1,0:T(8,128)S(1)}, f32[208,512]{1,0:T(8,128)S(1)}, u32[]{:S(2)}, u32[]{:S(2)}) collective-permute-start(f32[208,512]{1,0:T(8,128)S(1)} %get-tuple-element.82.after), channel_id=1, source_target_pairs={{0,12},{1,13},{2,14},{3,15},{4,0},{5,1},{6,2},{7,3},{8,4},{9,5},{1... | collective-permute-start | bytes 1277960 | tf_op jit(solution)/shard_map/ppermute | solution.py:364
  194.9 11.3 %collective-permute-start.20 = (f32[208,512]{1,0:T(8,128)S(1)}, f32[208,512]{1,0:T(8,128)S(1)}, u32[]{:S(2)}, u32[]{:S(2)}) collective-permute-start(f32[208,512]{1,0:T(8,128)S(1)} %get-tuple-element.89), channel_id=1, source_target_pairs={{0,32},{1,33},{2,34},{3,35},{4,36},{5,37},{6,38},{7,39},{8,40},{9,... | collective-permute-start | bytes 1277960 | tf_op jit(solution)/shard_map/ppermute | solution.py:364
  194.9 11.2 %collective-permute-start.21 = (f32[208,512]{1,0:T(8,128)S(1)}, f32[208,512]{1,0:T(8,128)S(1)}, u32[]{:S(2)}, u32[]{:S(2)}) collective-permute-start(f32[208,512]{1,0:T(8,128)S(1)} %get-tuple-element.86.after), channel_id=1, source_target_pairs={{0,96},{1,97},{2,98},{3,99},{4,100},{5,101},{6,102},{7,103},{8,104... | collective-permute-start | bytes 1277960 | tf_op jit(solution)/shard_map/ppermute | solution.py:364
  204.6 2.2 copy-start.5
  204.6 7.4 %collective-permute-start.22 = (f32[208,512]{1,0:T(8,128)S(1)}, f32[208,512]{1,0:T(8,128)S(1)}, u32[]{:S(2)}, u32[]{:S(2)}) collective-permute-start(f32[208,512]{1,0:T(8,128)S(1)} %get-tuple-element.91), channel_id=1, source_target_pairs={{0,16},{1,17},{2,18},{3,19},{4,20},{5,21},{6,22},{7,23},{8,24},{9,... | collective-permute-start | bytes 1277960 | tf_op jit(solution)/shard_map/ppermute | solution.py:364
  206.8 0.8 copy-start.6
  207.6 9.8 %collective-permute-start.23 = (f32[208,512]{1,0:T(8,128)S(1)}, f32[208,512]{1,0:T(8,128)S(1)}, u32[]{:S(2)}, u32[]{:S(2)}) collective-permute-start(f32[208,512]{1,0:T(8,128)S(1)} %get-tuple-element.92), channel_id=1, source_target_pairs={{0,16},{1,17},{2,18},{3,19},{4,20},{5,21},{6,22},{7,23},{8,24},{9,... | collective-permute-start | bytes 1277960 | tf_op jit(solution)/shard_map/ppermute | solution.py:364
  212.0 0.8 copy-start.13
  217.4 0.8 copy-start.12
  225.2 16.2 %collective-permute-start.24 = (f32[512,512]{1,0:T(8,128)}, f32[512,512]{1,0:T(8,128)S(1)}, u32[]{:S(2)}, u32[]{:S(2)}) collective-permute-start(f32[512,512]{1,0:T(8,128)} %shard_map.74), channel_id=1, source_target_pairs={{0,16},{1,17},{2,18},{3,19},{4,20},{5,21},{6,22},{7,23},{8,24},{9,... | collective-permute-start | bytes 3145736 | tf_op jit(solution)/shard_map/ppermute | solution.py:364
  225.8 25.2 %collective-permute-start.25 = (f32[512,512]{1,0:T(8,128)}, f32[512,512]{1,0:T(8,128)S(1)}, u32[]{:S(2)}, u32[]{:S(2)}) collective-permute-start(f32[512,512]{1,0:T(8,128)} %shard_map.74), channel_id=1, source_target_pairs={{0,18},{1,19},{2,16},{3,17},{4,22},{5,23},{6,20},{7,21},{8,26},{9,... | collective-permute-start | bytes 3145736 | tf_op jit(solution)/shard_map/ppermute | solution.py:364
  241.4 12.4 %collective-permute-start.26 = (f32[512,512]{1,0:T(8,128)S(1)}, f32[512,512]{1,0:T(8,128)S(1)}, u32[]{:S(2)}, u32[]{:S(2)}) collective-permute-start(f32[512,512]{1,0:T(8,128)S(1)} %collective-permute-done.24), channel_id=1, source_target_pairs={{0,1},{1,0},{2,3},{3,2},{4,5},{5,4},{6,7},{7,6},{8,9},{9,8},{10,11... | collective-permute-start | bytes 3145736 | tf_op jit(solution)/shard_map/ppermute | solution.py:364
  251.0 4.6 %collective-permute-start.27 = (f32[512,512]{1,0:T(8,128)S(1)}, f32[512,512]{1,0:T(8,128)}, u32[]{:S(2)}, u32[]{:S(2)}) collective-permute-start(f32[512,512]{1,0:T(8,128)S(1)} %collective-permute-done.25), channel_id=1, source_target_pairs={{0,1},{1,0},{2,3},{3,2},{4,5},{5,4},{6,7},{7,6},{8,9},{9,8},{10,11... | collective-permute-start | bytes 3145736 | tf_op jit(solution)/shard_map/ppermute | solution.py:364
  254.0 2.0 copy-start.9
Sparse Core Ops, SparseCore 0:
  118.7 82.5 reduce-scatter.3

commit v3 on v1

--- a/solution.py
+++ b/solution.py
@@ -15,7 +15,7 @@
 ROWS_A = 192
 ROWS_C = (BLK - 2 * ROWS_A) // 2
 EXTRA = 8
-SMALL, LARGE = 16 * 1024 * 1024, 56 * 1024 * 1024
+SMALL, TURN, LARGE = 16 * 1024 * 1024, 30 * 1024 * 1024, 56 * 1024 * 1024
 
 
 def flat(x, zl, y, zh, core):
@@ -90,6 +90,7 @@
 class Order:
     def __init__(self, table, where):
         self.table, self.where, self.last = table, where, None
+        self.also = []
 
     def gate(self, held, behind):
         anywhere = pl.BlockSpec(memory_space=pl.ANY)
@@ -110,8 +111,10 @@
         ]
         inner = body
         if self.last is not None:
-            ins = [(self.last, pl.BlockSpec(memory_space=pl.ANY))] + ins
-            inner = lambda table, where, after, *refs: body(table, where, *refs)
+            after = [self.last] + self.also
+            self.also = []
+            ins = [(a, pl.BlockSpec(memory_space=pl.ANY)) for a in after] + ins
+            inner = lambda table, where, *refs: body(table, where, *refs[len(after) :])
         made = pl.pallas_call(
             inner,
             out_shape=shapes,
@@ -229,14 +232,14 @@
 TERMS = ((1, 0, (0,)), (3, 1, (1,)), (0, 0, (2, 0)), (0, 1, (2, 1)))
 
 
-def turn_body(stream, jobs, table, where, *refs):
-    sums = refs[16:19] if stream == "x" else ()
-    outs = refs[16 + len(sums) :]
-    rows = (half_rows(stream) - ROWS_A) // 2
-    for n, (r, half, place) in enumerate(jobs):
-        base, more, got, term = refs[4 * n : 4 * n + 4]
+def turn_body(jobs, table, where, *refs):
+    sums, refs = refs[:3], refs[3:]
+    ins, outs = refs[: 4 * len(jobs)], refs[4 * len(jobs) :]
+    for n, (stream, r, half, place) in enumerate(jobs):
+        base, more, got, term = ins[4 * n : 4 * n + 4]
         out = outs[place[0]].at[place[1]] if len(place) == 2 else outs[place[0]]
         out[:ROWS_A, :] = base[0] + more[0]
+        rows = (half_rows(stream) - ROWS_A) // 2
         for v in range(2):
             at = (0, v) if stream == "y" else (v, 0)
             low = ROWS_A + v * rows
@@ -254,24 +257,30 @@
             out[low + ROWS_C : low + rows, :] = jnp.concatenate(parts, axis=0)
 
 
-def turn(order, stream, jobs, halves, got, terms, sums):
-    ins = []
-    for r, half, _ in jobs:
-        if stream == "x":
-            here = lambda i, t, w, r=r: ((w[2] + r) & 3, 0, 0)
-            side = spec((2, 1, ROWS_C, BLK), lambda i, t, w, r=r, h=half: (h, (w[2] + r) & 3, 1, 0))
+def turn(order, streams, pieces, halves, got, terms, sums):
+    once = dict(pipeline_mode=pl.Buffered(1))
+    ins = [(s, whole(s)) for s in sums]
+    jobs, outs = [], []
+    for stream in streams:
+        for r, half, place in pieces:
+            jobs.append((stream, r, half, (place[0] + len(outs), *place[1:])))
+            if stream == "x":
+                here = lambda i, t, w, r=r: ((w[2] + r) & 3, 0, 0)
+                shape = (2, 1, ROWS_C, BLK)
+                side = lambda i, t, w, r=r, h=half: (h, (w[2] + r) & 3, 1, 0)
+            else:
+                here = lambda i, t, w, r=r: ((w[0] + r) & 3, 0, 0)
+                shape = (1, 2, ROWS_C, BLK)
+                side = lambda i, t, w, r=r, h=half: ((w[0] + r) & 3, h, 0, 0)
+            ins += [(a, spec((1, ROWS_A, BLK), here, **once)) for a in halves[stream][half]]
+            for a in (got, terms):
+                ins.append((a.reshape(4, 4, 2 * ROWS_C, BLK), spec(shape, side, **once)))
+        rows = half_rows(stream)
+        if pieces is TERMS:
+            outs += [full(rows, BLK)] * 2 + [full(2, rows, BLK)]
         else:
-            here = lambda i, t, w, r=r: ((w[0] + r) & 3, 0, 0)
-            side = spec((1, 2, ROWS_C, BLK), lambda i, t, w, r=r, h=half: ((w[0] + r) & 3, h, 0, 0))
-        ins += [(a, spec((1, ROWS_A, BLK), here)) for a in halves[half]]
-        ins += [(a.reshape(4, 4, 2 * ROWS_C, BLK), side) for a in (got, terms)]
-    if stream == "x":
-        ins += [(s, whole(s)) for s in sums]
-    rows = half_rows(stream)
-    outs = [full(2, rows, BLK)] * 2
-    if jobs is TERMS:
-        outs = [full(rows, BLK)] * 2 + [full(2, rows, BLK)]
-    return order(functools.partial(turn_body, stream, jobs), 1, ins, outs, vmem=LARGE)
+            outs += [full(2, rows, BLK)] * 2
+    return order(functools.partial(turn_body, jobs), 1, ins, outs, vmem=TURN)
 
 
 def relay_half_body(table, where, message, term, out):
@@ -327,7 +336,7 @@
         (basis, spec((1, BLK, BLK), lambda i, t, w: (first + i, 0, 0))),
     ]
     out = ((n, 1, BLK), spec((1, 1, BLK), lambda i, t, w: (i, 0, 0)))
-    return order(sums_body, n, ins, [out], vmem=LARGE)[0]
+    return order(sums_body, n, ins, [out], vmem=SMALL)[0]
 
 
 def total_body(table, where, *refs):
@@ -343,24 +352,37 @@
     return order(total_body, 1, [(p, whole(p)) for p in parts], outs)
 
 
-def join_body(table, where, a, b, out):
-    out[...] = a[...] + b[...]
-
-
-def join(order, a, b):
-    return order(join_body, 1, [(a, whole(a)), (b, whole(b))], [full(*a.shape)])[0]
+def mine(w):
+    return w[0] * 8 + (1 - w[1]) * 4 + w[2]
+
+
+def rotate_body(joined, table, where, first, second, basis, out):
+    a = split(basis[0])
+    if joined:
+        value = first[...] + second[...]
+    else:
+        value = jnp.concatenate([first[...], second[...]], axis=0)
+    out[...] = dot3(split(value), a, ((1,), (0,)))
+
+
+def rotate(order, first, second, eig_in, joined):
+    ins = [(a, whole(a)) for a in (first, second)]
+    ins.append((eig_in, spec((1, BLK, BLK), lambda i, t, w: (t[mine(w)] >> 2, 0, 0))))
+    rows = first.shape[0] * (1 if joined else 2)
+    body = functools.partial(rotate_body, joined)
+    return order(body, 1, ins, [full(rows, BLK)], vmem=TURN)[0]
 
 
 def precondition_body(tokens_all, table, where, *refs):
-    x, y0, y1, cx, cy, ours, theirs = (r[...] for r in refs[:7])
-    basis_in, basis_out, out = refs[7:]
+    x, c, y0, y1, ours, theirs = (r[...] for r in refs[:6])
+    basis_in, basis_out, out = refs[6:]
     scale = 1.0 / tokens_all
-    grad = jnp.concatenate([x, y0 + y1, cx, cy], axis=0) * scale
     values_in = (ours[0:1] + theirs[2:3]) * scale
     values_out = (ours[1:2] + theirs[3:4]) * scale
     a = split(basis_in[0])
     b = split(basis_out[0])
-    rotated = dot3(split(grad), a, ((1,), (0,)))
+    y = dot3(split(y0 + y1), a, ((1,), (0,)))
+    rotated = jnp.concatenate([x, y, c], axis=0) * scale
     rotated = dot3(b, split(rotated), ((0,), (0,)))
     scaled = rotated / (values_out.reshape(BLK, 1) * values_in + DAMPING)
     back = dot3(b, split(scaled), ((1,), (0,)))
@@ -368,7 +390,6 @@
 
 
 def precondition(tokens_all, order, parts, eig_in, eig_out):
-    mine = lambda w: w[0] * 8 + (1 - w[1]) * 4 + w[2]
     ins = [(q, whole(q)) for q in parts]
     ins.append((eig_in, spec((1, BLK, BLK), lambda i, t, w: (t[mine(w)] >> 2, 0, 0))))
     ins.append((eig_out, spec((1, BLK, BLK), lambda i, t, w: (t[mine(w)] & 3, 0, 0))))
@@ -377,8 +398,7 @@
         1,
         ins,
         [full(BLK, BLK)],
-        cost=3.0,
-        vmem=LARGE,
+        vmem=TURN,
     )[0]
 
 
@@ -410,15 +430,15 @@
     sums.append(square_sums(order, latents, eig_in, 4, 4))
     sums.append(square_sums(order, out_grads, eig_out, 0, 4))
 
-    def pieces(stream, jobs):
-        n = 0 if stream == "x" else 2
-        halves = ((own[n], got_t[n]), (own[n + 1], got_t[n + 1]))
-        return turn(order, stream, jobs, halves, got_c, terms_c, sums)
-
-    msgs_x = both(*pieces("x", MESSAGES), "y")
-    msgs_y = both(*pieces("y", MESSAGES), "x")
-    *parts_x, mine_x = pieces("x", TERMS)
-    *parts_y, mine_y = pieces("y", TERMS)
+    halves = {
+        stream: ((own[n], got_t[n]), (own[n + 1], got_t[n + 1]))
+        for n, stream in ((0, "x"), (2, "y"))
+    }
+    rest = (halves, got_c, terms_c, sums)
+    messages = turn(order, "xy", MESSAGES, *rest)
+    msgs_x, msgs_y = both(*messages[:2], "y"), both(*messages[2:], "x")
+    *parts_x, mine_x = turn(order, "x", TERMS, *rest)
+    *parts_y, mine_y = turn(order, "y", TERMS, *rest)
 
     def follow(stream, messages, parts):
         more = [relay_half(order, m, p) for m, p in zip(messages, parts)]
@@ -429,18 +449,17 @@
 
     away_x, keep_x, *parts_cy = end(order, "x", mine_x, *msgs_x, *more_x)
     got_x = send(away_x, near)
+    parts_cy = far(parts_cy, "x")
+    order.also = [parts_cy[1], parts_cy[3]]
     away_y, keep_y, *parts_cx = end(order, "y", mine_y, *msgs_y, *more_y)
     got_y = send(away_y, near)
-    done_cy, ours = total(order, far(parts_cy, "x"))
+    done_cy, ours = total(order, parts_cy)
     theirs = send(ours, near)
+    turned_x = rotate(order, keep_x, got_x, eig_in, True)
     (done_cx,) = total(order, far(parts_cx, "y"))
-    done_x = join(order, keep_x, got_x)
+    turned_c = rotate(order, done_cx, done_cy, eig_in, False)
     update = precondition(
-        tokens_all,
-        order,
-        [done_x, keep_y, got_y, done_cx, done_cy, ours, theirs],
-        eig_in,
-        eig_out,
+        tokens_all, order, [turned_x, turned_c, keep_y, got_y, ours, theirs], eig_in, eig_out
     )
     same = send(update, near)
     other = send(update, cross)

time: 242 us -> 234 us (0.967)
  Pallas kernels: 107 us -> 87.8 us
  waiting for transfers between devices: 64.8 us -> 76.6 us
  local copies, waits for them, and re-layouts: 10.1 us -> 16.9 us
  starting transfers between devices: 58.4 us -> 51.8 us
    pallas_call x22, Pallas kernels: 107 us -> 87.8 us  [__call__(): pl.pallas_call(inner, out_shape=shapes, grid_spec=pltpu.PrefetchScalarGri...]
    ppermute x34, waiting for transfers between devices: 64.8 us -> 76.6 us  [on_device(): send = lambda value, pairs: lax.ppermute(value, AXES, pairs)]
    unnamed x48 -> x54, local copies, waits for them, and re-layouts: 7.08 us -> 13.8 us
    ppermute x34, starting transfers between devices: 58.4 us -> 51.8 us  [on_device(): send = lambda value, pairs: lax.ppermute(value, AXES, pairs)]
  transfers between devices with their start and end apart: 34 -> 34, of which waited for: 15 -> 12; matrix products, arithmetic and copies ran while one was open for 0% -> 0% of each run, Pallas kernels for 36% -> 29%
where the time goes in v3:
time: 234 us
  Pallas kernels  87.8 us (38%)
  waiting for transfers between devices  76.6 us (33%)
  starting transfers between devices  51.8 us (22%)
  local copies, waits for them, and re-layouts  16.9 us (7%)
    pallas_call x22, Pallas kernels, __call__(): pl.pallas_call(inner, out_shape=shapes, grid_spec=pltpu.PrefetchScalarGri...  87.8 us
    ppermute x34, waiting for transfers between devices, on_device(): send = lambda value, pairs: lax.ppermute(value, AXES, pairs)  76.6 us
    ppermute x34, starting transfers between devices, on_device(): send = lambda value, pairs: lax.ppermute(value, AXES, pairs)  51.8 us
    unnamed x54, local copies, waits for them, and re-layouts  13.8 us
  transfers between devices with their start and end apart: 34, of which 12 were waited for; matrix products, arithmetic and copies ran while one was open for 0% of the time, Pallas kernels for 29%

profile of v3, /device:TPU:1, one launch (start us, length us, event | category | flops | bytes accessed | tf_op | source)
XLA Modules:
  0.0 234.2 jit_solution(1040723521821679012)
XLA Ops:
  0.0 0.6 pad_add_fusion.where
  0.6 11.4 %shard_map.55 = (bf16[2048,768]{1,0:T(8,128)(2,1)}, f32[4,192,512]{2,1,0:T(8,128)}, f32[4,192,512]{2,1,0:T(8,128)}, f32[4,192,512]{2,1,0:T(8,128)}, f32[4,192,512]{2,1,0:T(8,128)}) custom-call(s32[32]{0:T(128)} %table.43, s32[3]{0:T(128)} %pad_add_fusion.where, bf16[768,2048]{1,0:T(8,128)(2,1)} %refs_1_.7, bf16[768,4096]{1,0:T(8,128)(2,1)} %refs_1_.6, ...), custom_call_target="tpu_custom_call" | custom-call | bytes 3690000 | tf_op jit(solution)/shard_map/pallas_call | solution.py:118
  12.0 2.3 collective-permute-start
  14.3 1.6 collective-permute-start.1
  15.9 1.3 collective-permute-start.2
  17.2 1.4 collective-permute-start.3
  18.6 8.2 %shard_map.56.refs_0_ = f32[16,128,512]{2,1,0:T(8,128)} custom-call(s32[32]{0:T(128)} %table.43, s32[3]{0:T(128)} %pad_add_fusion.where, f32[4,192,512]{2,1,0:T(8,128)} %get-tuple-element.55.refs_0_, bf16[2048,768]{1,0:T(8,128)(2,1)} %get-tuple-element.56.refs_1_, bf16[768,4096]{1,0:T(8,128)(2,1)} %refs_1_.6), custom_call_target="tpu_custom_call" | custom-call | bytes 3690000 | tf_op jit(solution)/shard_map/pallas_call | solution.py:118
  26.9 1.6 collective-permute-start.9
  28.5 12.3 %shard_map.57 = (f32[4,192,512]{2,1,0:T(8,128)}, f32[4,192,512]{2,1,0:T(8,128)}, f32[4,192,512]{2,1,0:T(8,128)}, f32[4,192,512]{2,1,0:T(8,128)}, f32[4,192,512]{...) custom-call(s32[32]{0:T(128)} %table.43, s32[3]{0:T(128)} %pad_add_fusion.where, ...), custom_call_target="tpu_custom_call" | custom-call | bytes 3690000 | tf_op jit(solution)/shard_map/pallas_call | solution.py:118
  40.8 9.5 %collective-permute-done.refs_1_ = f32[4,192,512]{2,1,0:T(8,128)S(1)} collective-permute-done((f32[4,192,512]{2,1,0:T(8,128)}, f32[4,192,512]{2,1,0:T(8,128)S(1)}, u32[]{:S(2)}, u32[]{:S(2)}) %collective-permute-start) | collective-permute-done | bytes 1572896 | tf_op jit(solution)/shard_map/ppermute | solution.py:413
  50.3 2.7 %collective-permute-start.7 = (f32[4,192,512]{2,1,0:T(8,128)}, f32[4,192,512]{2,1,0:T(8,128)}, u32[]{:S(2)}, u32[]{:S(2)}) collective-permute-start(f32[4,192,512]{2,1,0:T(8,128)} %get-tuple-element.71), channel_id=1, source_target_pairs={{0,96},{1,97},{2,98},{3,99},{4,100},{5,101},{6,102},{7,103},{8,104... | collective-permute-start | bytes 4718600 | tf_op jit(solution)/shard_map/ppermute | solution.py:413
  52.9 1.2 collective-permute-start.4
  54.1 1.6 collective-permute-start.5
  55.8 8.1 %shard_map.58 = (f32[4,192,512]{2,1,0:T(8,128)}, f32[4,192,512]{2,1,0:T(8,128)}, f32[4,192,512]{2,1,0:T(8,128)}, f32[4,192,512]{2,1,0:T(8,128)}) custom-call(s32[32]{0:T(128)} %table.43, s32[3]{0:T(128)} %pad_add_fusion.where, f32[4,192,512]{2,1,0:T(8,128)} %get-tuple-element.57.refs_0_.refs_8_, f32[4,192,512]{2,1,0:T(8,128)} %copy-done.20, ...), custom_call_target="tpu_custom_call" | custom-call | bytes 3690000 | tf_op jit(solution)/shard_map/pallas_call | solution.py:118
  63.9 3.4 %copy-done.2 = f32[8,512,512]{2,1,0:T(8,128)S(1)} copy-done((f32[8,512,512]{2,1,0:T(8,128)S(1)}, f32[8,512,512]{2,1,0:T(8,128)}, u32[]{:S(2)}) %copy-start.2) | copy-done | bytes 8388632
  67.3 1.4 copy-done.10
  68.7 4.8 %shard_map.59.refs_4_.refs_1_ = f32[4,1,512]{2,1,0:T(1,128)S(1)} custom-call(s32[32]{0:T(128)S(1)} %copy-done.14, s32[3]{0:T(128)S(1)} %copy-done.12, f32[4,192,512]{2,1,0:T(8,128)S(1)} %copy-done.10, bf16[768,4096]{1,0:T(8,128)(2,1)S(1)} %bitcast.30, f32[8,512,512]{2,1,0:T(8,128)S(1)} %copy-done.2), custom_call_target="tpu_custom_call" | custom-call | bytes 3690000 | tf_op jit(solution)/shard_map/pallas_call | solution.py:118
  73.5 0.6 copy-done.16
  74.1 12.4 %collective-permute-done.6.refs_2_.refs_4_ = f32[4,192,512]{2,1,0:T(8,128)S(1)} collective-permute-done((f32[4,192,512]{2,1,0:T(8,128)}, f32[4,192,512]{2,1,0:T(8,128)S(1)}, u32[]{:S(2)}, u32[]{:S(2)}) %collective-permute-start.6) | collective-permute-done | bytes 1572896 | tf_op jit(solution)/shard_map/ppermute | solution.py:413
  86.6 1.2 copy-done.18
  87.8 1.2 collective-permute-start.10
  89.0 1.1 collective-permute-start.11
  90.1 1.7 collective-permute-start.12
  92.2 12.6 %shard_map.62 = (f32[4,192,512]{2,1,0:T(8,128)}, f32[4,192,512]{2,1,0:T(8,128)}, f32[4,192,512]{2,1,0:T(8,128)}, f32[4,192,512]{2,1,0:T(8,128)}, f32[16,128,512]{2,1,0:T(8,128)}) custom-call(s32[32]{0:T(128)} %table.43, s32[3]{0:T(128)} %pad_add_fusion.where, f32[4,192,512]{2,1,0:T(8,128)} %get-tuple-element.73.refs_0_, ...), custom_call_target="tpu_custom_call" | custom-call | bytes 3690000 | tf_op jit(solution)/shard_map/pallas_call | solution.py:118
  104.8 2.2 copy-done
  107.0 3.4 %copy-done.3 = f32[8,512,512]{2,1,0:T(8,128)S(1)} copy-done((f32[8,512,512]{2,1,0:T(8,128)S(1)}, f32[8,512,512]{2,1,0:T(8,128)}, u32[]{:S(2)}) %copy-start.3) | copy-done | bytes 8388632
  110.4 4.9 %shard_map.63.refs_0_.refs_2_ = f32[4,1,512]{2,1,0:T(1,128)S(1)} custom-call(s32[32]{0:T(128)S(1)} %copy-done.15, s32[3]{0:T(128)S(1)} %copy-done.13, f32[16,128,512]{2,1,0:T(8,128)S(1)} %copy-done, bf16[768,4096]{1,0:T(8,128)(2,1)S(1)} %bitcast.32, f32[8,512,512]{2,1,0:T(8,128)S(1)} %copy-done.3), custom_call_target="tpu_custom_call" | custom-call | bytes 3690000 | tf_op jit(solution)/shard_map/pallas_call | solution.py:118
  115.3 4.8 %shard_map.64.refs_0_.refs_3_ = f32[4,1,512]{2,1,0:T(1,128)S(1)} custom-call(s32[32]{0:T(128)S(1)} %copy-done.15, s32[3]{0:T(128)S(1)} %copy-done.13, f32[4,1,512]{2,1,0:T(1,128)S(1)} %shard_map.63.refs_0_.refs_2_, bf16[768,2048]{1,0:T(8,128)(2,1)S(1)} %copy-done.11, f32[4,512,512]{2,1,0:T(8,128)S(1)} %copy-done.8), custom_call_target="tpu_custom_call" | custom-call | bytes 3690000 | tf_op jit(solution)/shard_map/pallas_call | solution.py:118
  120.1 3.9 %collective-permute-done.11.refs_21_.refs_33_.refs_5_.refs_13_ = f32[4,192,512]{2,1,0:T(8,128)} collective-permute-done((f32[4,192,512]{2,1,0:T(8,128)}, f32[4,192,512]{2,1,0:T(8,128)}, u32[]{:S(2)}, u32[]{:S(2)}) %collective-permute-start.11) | collective-permute-done | bytes 1572896 | tf_op jit(solution)/shard_map/ppermute | solution.py:413
  124.0 2.3 collective-permute-done.8.refs_5_.refs_17_.refs_13_
  126.3 4.5 %shard_map.65 = (f32[2,336,512]{2,1,0:T(8,128)S(1)}, f32[2,336,512]{2,1,0:T(8,128)S(1)}, f32[2,320,512]{2,1,0:T(8,128)S(1)}, f32[2,320,512]{2,1,0:T(8,128)S(1)}) custom-call(s32[32]{0:T(128)S(1)} %copy-done.15, s32[3]{0:T(128)S(1)} %copy-done.13, f32[4,1,512]{2,1,0:T(1,128)S(1)} %shard_map.64.refs_0_.refs_3_, f32[4,1,512]{2,1,0:T(1,128)S(1)} %copy-done.17, ...), custom_call_target="tpu_custom_call" | custom-call | bytes 3690000 | tf_op jit(solution)/shard_map/pallas_call | solution.py:118
  130.9 2.7 %collective-permute-start.14 = (f32[2,336,512]{2,1,0:T(8,128)S(1)}, f32[2,336,512]{2,1,0:T(8,128)S(1)}, u32[]{:S(2)}, u32[]{:S(2)}) collective-permute-start(f32[2,336,512]{2,1,0:T(8,128)S(1)} %get-tuple-element.86), channel_id=1, source_target_pairs={{0,12},{1,13},{2,14},{3,15},{4,0},{5,1},{6,2},{7,3},{8,4},{9,5},{1... | collective-permute-start | bytes 4128776 | tf_op jit(solution)/shard_map/ppermute | solution.py:413
  133.6 2.7 %collective-permute-start.16 = (f32[2,320,512]{2,1,0:T(8,128)S(1)}, f32[2,320,512]{2,1,0:T(8,128)S(1)}, u32[]{:S(2)}, u32[]{:S(2)}) collective-permute-start(f32[2,320,512]{2,1,0:T(8,128)S(1)} %get-tuple-element.81.refs_0_), channel_id=1, source_target_pairs={{0,96},{1,97},{2,98},{3,99},{4,100},{5,101},{6,102},{7,103},{8,104... | collective-permute-start | bytes 3932168 | tf_op jit(solution)/shard_map/ppermute | solution.py:413
  136.3 2.5 %shard_map.66 = (f32[336,512]{1,0:T(8,128)S(1)}, f32[336,512]{1,0:T(8,128)S(1)}, f32[2,336,512]{2,1,0:T(8,128)S(1)}) custom-call(s32[32]{0:T(128)S(1)} %copy-done.15, s32[3]{0:T(128)S(1)} %copy-done.13, f32[2,320,512]{2,1,0:T(8,128)S(1)} %get-tuple-element.81.refs_0_, f32[4,1,512]{2,1,0:T(1,128)S(1)} %copy-done.17, ...), custom_call_target="tpu_custom_call" | custom-call | bytes 3690000 | tf_op jit(solution)/shard_map/pallas_call | solution.py:118
  138.8 2.5 %shard_map.67 = (f32[320,512]{1,0:T(8,128)S(1)}, f32[320,512]{1,0:T(8,128)S(1)}, f32[2,320,512]{2,1,0:T(8,128)S(1)}) custom-call(s32[32]{0:T(128)S(1)} %copy-done.15, s32[3]{0:T(128)S(1)} %copy-done.13, f32[2,336,512]{2,1,0:T(8,128)S(1)} %get-tuple-element.82.refs_0_.refs_1_, f32[4,1,512]{2,1,0:T(1,128)S(1)} %copy-done.17, ...), custom_call_target="tpu_custom_call" | custom-call | bytes 3690000 | tf_op jit(solution)/shard_map/pallas_call | solution.py:118
  141.3 18.5 %collective-permute-done.13.refs_1_.refs_2_ = f32[2,336,512]{2,1,0:T(8,128)S(1)} collective-permute-done((f32[2,336,512]{2,1,0:T(8,128)S(1)}, f32[2,336,512]{2,1,0:T(8,128)S(1)}, u32[]{:S(2)}, u32[]{:S(2)}) %collective-permute-start.13) | collective-permute-done | bytes 1376288 | tf_op jit(solution)/shard_map/ppermute | solution.py:413
  159.9 0.6 shard_map.68.refs_0_
  160.5 0.6 shard_map.69.refs_0_
  161.1 1.8 collective-permute-start.18
  162.9 0.6 shard_map.70.refs_0_
  163.6 0.6 shard_map.71.refs_0_
  164.3 1.5 collective-permute-start.21
  165.8 7.5 %collective-permute-done.18.refs_5_ = f32[336,512]{1,0:T(8,128)S(1)} collective-permute-done((f32[336,512]{1,0:T(8,128)S(1)}, f32[336,512]{1,0:T(8,128)S(1)}, u32[]{:S(2)}, u32[]{:S(2)}) %collective-permute-start.18) | collective-permute-done | bytes 688160 | tf_op jit(solution)/shard_map/ppermute | solution.py:413
  173.2 2.3 collective-permute-done.17.refs_4_
  175.6 0.9 shard_map.72
  176.8 2.3 %collective-permute-start.20 = (f32[72,512]{1,0:T(8,128)S(1)}, f32[72,512]{1,0:T(8,128)S(1)}, u32[]{:S(2)}, u32[]{:S(2)}) collective-permute-start(f32[72,512]{1,0:T(8,128)S(1)} %get-tuple-element.91.refs_0_), channel_id=1, source_target_pairs={{0,96},{1,97},{2,98},{3,99},{4,100},{5,101},{6,102},{7,103},{8,104... | collective-permute-start | bytes 442376 | tf_op jit(solution)/shard_map/ppermute | solution.py:413
  179.3 4.3 %collective-permute-done.19.refs_1_.refs_2_ = f32[72,512]{1,0:T(8,128)S(1)} collective-permute-done((f32[72,512]{1,0:T(8,128)S(1)}, f32[72,512]{1,0:T(8,128)S(1)}, u32[]{:S(2)}, u32[]{:S(2)}) %collective-permute-start.19) | collective-permute-done | bytes 147488 | tf_op jit(solution)/shard_map/ppermute | solution.py:413
  183.6 0.8 shard_map.73
  184.8 2.7 %collective-permute-start.26 = (f32[64,512]{1,0:T(8,128)S(1)}, f32[64,512]{1,0:T(8,128)S(1)}, u32[]{:S(2)}, u32[]{:S(2)}) collective-permute-start(f32[64,512]{1,0:T(8,128)S(1)} %get-tuple-element.101), channel_id=1, source_target_pairs={{0,8},{1,9},{2,10},{3,11},{4,12},{5,13},{6,14},{7,15},{8,0},{9,1},... | collective-permute-start | bytes 393224 | tf_op jit(solution)/shard_map/ppermute | solution.py:413
  187.5 2.7 %collective-permute-done.23.refs_3_ = f32[72,512]{1,0:T(8,128)S(1)} collective-permute-done((f32[72,512]{1,0:T(8,128)S(1)}, f32[72,512]{1,0:T(8,128)S(1)}, u32[]{:S(2)}, u32[]{:S(2)}) %collective-permute-start.23) | collective-permute-done | bytes 147488 | tf_op jit(solution)/shard_map/ppermute | solution.py:413
  190.2 1.1 collective-permute-start.27
  191.3 0.6 shard_map.74
  191.9 1.2 collective-permute-start.29
  193.0 1.1 shard_map.75.refs_0_.refs_1_
  194.9 1.0 shard_map.77.refs_0_.refs_2_
  195.9 1.2 copy-done.9
  197.1 3.8 %shard_map.78 = f32[512,512]{1,0:T(8,128)S(1)} custom-call(s32[32]{0:T(128)S(1)} %copy-done.15, s32[3]{0:T(128)S(1)} %copy-done.13, f32[128,512]{1,0:T(8,128)S(1)} %shard_map.77.refs_0_.refs_2_, f32[192,512]{1,0:T(8,128)S(1)} %shard_map.75.refs_0_.refs_1_, f32[128,512]{1,0:T(8,128)S(1)} %shard_map.77.refs_0_.refs_2_, ...), custom_call_target="tpu_custom_call" | custom-call | bytes 3690000 | tf_op jit(solution)/shard_map/pallas_call | solution.py:118
  200.9 1.4 collective-permute-start.30
  202.3 2.5 %collective-permute-start.31 = (f32[512,512]{1,0:T(8,128)S(1)}, f32[512,512]{1,0:T(8,128)S(1)}, u32[]{:S(2)}, u32[]{:S(2)}) collective-permute-start(f32[512,512]{1,0:T(8,128)S(1)} %shard_map.78), channel_id=1, source_target_pairs={{0,18},{1,19},{2,16},{3,17},{4,22},{5,23},{6,20},{7,21},{8,26},{9,... | collective-permute-start | bytes 3145736 | tf_op jit(solution)/shard_map/ppermute | solution.py:413
  204.8 11.3 %collective-permute-done.30 = f32[512,512]{1,0:T(8,128)S(1)} collective-permute-done((f32[512,512]{1,0:T(8,128)S(1)}, f32[512,512]{1,0:T(8,128)S(1)}, u32[]{:S(2)}, u32[]{:S(2)}) %collective-permute-start.30) | collective-permute-done | bytes 1048608 | tf_op jit(solution)/shard_map/ppermute | solution.py:413
  216.1 10.5 %collective-permute-start.32 = (f32[512,512]{1,0:T(8,128)S(1)}, f32[512,512]{1,0:T(8,128)S(1)}, u32[]{:S(2)}, u32[]{:S(2)}) collective-permute-start(f32[512,512]{1,0:T(8,128)S(1)} %collective-permute-done.30), channel_id=1, source_target_pairs={{0,1},{1,0},{2,3},{3,2},{4,5},{5,4},{6,7},{7,6},{8,9},{9,8},{10,11... | collective-permute-start | bytes 3145736 | tf_op jit(solution)/shard_map/ppermute | solution.py:413
  226.6 2.5 %collective-permute-start.33 = (f32[512,512]{1,0:T(8,128)S(1)}, f32[512,512]{1,0:T(8,128)}, u32[]{:S(2)}, u32[]{:S(2)}) collective-permute-start(f32[512,512]{1,0:T(8,128)S(1)} %collective-permute-done.31), channel_id=1, source_target_pairs={{0,1},{1,0},{2,3},{3,2},{4,5},{5,4},{6,7},{7,6},{8,9},{9,8},{10,11... | collective-permute-start | bytes 3145736 | tf_op jit(solution)/shard_map/ppermute | solution.py:413
  229.9 1.6 collective-permute-done.33
  231.9 2.3 bitcast_dynamic-update-slice_fusion
  (91 shorter events, 3.3 us)
Async XLA Ops:
  12.0 38.2 %collective-permute-start = (f32[4,192,512]{2,1,0:T(8,128)}, f32[4,192,512]{2,1,0:T(8,128)S(1)}, u32[]{:S(2)}, u32[]{:S(2)}) collective-permute-start(f32[4,192,512]{2,1,0:T(8,128)} %get-tuple-element.58), channel_id=1, source_target_pairs={{0,32},{1,33},{2,34},{3,35},{4,36},{5,37},{6,38},{7,39},{8,40},{9,... | collective-permute-start | bytes 4718600 | tf_op jit(solution)/shard_map/ppermute | solution.py:413
  14.3 36.0 %collective-permute-start.1 = (f32[4,192,512]{2,1,0:T(8,128)}, f32[4,192,512]{2,1,0:T(8,128)}, u32[]{:S(2)}, u32[]{:S(2)}) collective-permute-start(f32[4,192,512]{2,1,0:T(8,128)} %get-tuple-element.59), channel_id=1, source_target_pairs={{0,96},{1,97},{2,98},{3,99},{4,100},{5,101},{6,102},{7,103},{8,104... | collective-permute-start | bytes 4718600 | tf_op jit(solution)/shard_map/ppermute | solution.py:413
  15.9 37.0 %collective-permute-start.2 = (f32[4,192,512]{2,1,0:T(8,128)}, f32[4,192,512]{2,1,0:T(8,128)}, u32[]{:S(2)}, u32[]{:S(2)}) collective-permute-start(f32[4,192,512]{2,1,0:T(8,128)} %get-tuple-element.60), channel_id=1, source_target_pairs={{0,4},{1,5},{2,6},{3,7},{4,8},{5,9},{6,10},{7,11},{8,12},{9,13},{1... | collective-permute-start | bytes 4718600 | tf_op jit(solution)/shard_map/ppermute | solution.py:413
  17.2 36.9 %collective-permute-start.3 = (f32[4,192,512]{2,1,0:T(8,128)}, f32[4,192,512]{2,1,0:T(8,128)}, u32[]{:S(2)}, u32[]{:S(2)}) collective-permute-start(f32[4,192,512]{2,1,0:T(8,128)} %get-tuple-element.55.refs_0_), channel_id=1, source_target_pairs={{0,12},{1,13},{2,14},{3,15},{4,0},{5,1},{6,2},{7,3},{8,4},{9,5},{1... | collective-permute-start | bytes 4718600 | tf_op jit(solution)/shard_map/ppermute | solution.py:413
  26.9 99.4 %collective-permute-start.9 = (f32[16,128,512]{2,1,0:T(8,128)}, f32[16,128,512]{2,1,0:T(8,128)}, u32[]{:S(2)}, u32[]{:S(2)}) collective-permute-start(f32[16,128,512]{2,1,0:T(8,128)} %shard_map.56.refs_0_), channel_id=1, source_target_pairs={{0,16},{1,17},{2,18},{3,19},{4,20},{5,21},{6,22},{7,23},{8,24},{9,... | collective-permute-start | bytes 12582920 | tf_op jit(solution)/shard_map/ppermute | solution.py:413
  28.5 35.4 %slice-start = ((s8[6291456]{0:T(1024)(128)(4,1)}), s8[4194304]{0:T(1024)(128)(4,1)S(1)}, s32[]{:S(2)}) async-start(s8[6291456]{0:T(1024)(128)(4,1)} %bitcast.29), calls=%async_computation | async-start | bytes 8388608
  50.3 5.5 %copy-start.20 = (f32[4,192,512]{2,1,0:T(8,128)}, f32[4,192,512]{2,1,0:T(8,128)S(1)}, u32[]{:S(2)}) copy-start(f32[4,192,512]{2,1,0:T(8,128)S(1)} %collective-permute-done.refs_1_) | copy-start | bytes 4718596
  50.3 36.3 %collective-permute-start.6 = (f32[4,192,512]{2,1,0:T(8,128)}, f32[4,192,512]{2,1,0:T(8,128)S(1)}, u32[]{:S(2)}, u32[]{:S(2)}) collective-permute-start(f32[4,192,512]{2,1,0:T(8,128)} %get-tuple-element.70), channel_id=1, source_target_pairs={{0,32},{1,33},{2,34},{3,35},{4,36},{5,37},{6,38},{7,39},{8,40},{9,... | collective-permute-start | bytes 4718600 | tf_op jit(solution)/shard_map/ppermute | solution.py:413
  50.3 36.3 %collective-permute-start.7 = (f32[4,192,512]{2,1,0:T(8,128)}, f32[4,192,512]{2,1,0:T(8,128)}, u32[]{:S(2)}, u32[]{:S(2)}) collective-permute-start(f32[4,192,512]{2,1,0:T(8,128)} %get-tuple-element.71), channel_id=1, source_target_pairs={{0,96},{1,97},{2,98},{3,99},{4,100},{5,101},{6,102},{7,103},{8,104... | collective-permute-start | bytes 4718600 | tf_op jit(solution)/shard_map/ppermute | solution.py:413
  52.9 36.0 %collective-permute-start.4 = (f32[4,192,512]{2,1,0:T(8,128)}, f32[4,192,512]{2,1,0:T(8,128)}, u32[]{:S(2)}, u32[]{:S(2)}) collective-permute-start(f32[4,192,512]{2,1,0:T(8,128)} %get-tuple-element.66), channel_id=1, source_target_pairs={{0,4},{1,5},{2,6},{3,7},{4,8},{5,9},{6,10},{7,11},{8,12},{9,13},{1... | collective-permute-start | bytes 4718600 | tf_op jit(solution)/shard_map/ppermute | solution.py:413
  54.1 34.8 %collective-permute-start.5 = (f32[4,192,512]{2,1,0:T(8,128)}, f32[4,192,512]{2,1,0:T(8,128)}, u32[]{:S(2)}, u32[]{:S(2)}) collective-permute-start(f32[4,192,512]{2,1,0:T(8,128)} %get-tuple-element.67), channel_id=1, source_target_pairs={{0,12},{1,13},{2,14},{3,15},{4,0},{5,1},{6,2},{7,3},{8,4},{9,5},{1... | collective-permute-start | bytes 4718600 | tf_op jit(solution)/shard_map/ppermute | solution.py:413
  55.8 8.1 %slice-start.1 = ((s8[6291456]{0:T(1024)(128)(4,1)}), s8[2097152]{0:T(1024)(128)(4,1)S(1)}, s32[]{:S(2)}) async-start(s8[6291456]{0:T(1024)(128)(4,1)} %bitcast.29), calls=%async_computation.1 | async-start | bytes 4194304
  55.8 8.1 %copy-start.12 = (s32[3]{0:T(128)S(1)}, s32[3]{0:T(128)}, u32[]{:S(2)}) copy-start(s32[3]{0:T(128)} %pad_add_fusion.where) | copy-start | bytes 40
  55.8 8.1 %copy-start.14 = (s32[32]{0:T(128)S(1)}, s32[32]{0:T(128)}, u32[]{:S(2)}) copy-start(s32[32]{0:T(128)} %table.43) | copy-start | bytes 388
  63.9 3.4 %copy-start.2 = (f32[8,512,512]{2,1,0:T(8,128)S(1)}, f32[8,512,512]{2,1,0:T(8,128)}, u32[]{:S(2)}) copy-start(f32[8,512,512]{2,1,0:T(8,128)} %refs_7_.1) | copy-start | bytes 25165828
  67.3 1.4 copy-start.10
  73.5 0.6 copy-start.16
  86.6 1.2 copy-start.18
  87.8 36.2 %collective-permute-start.10 = (f32[4,192,512]{2,1,0:T(8,128)}, f32[4,192,512]{2,1,0:T(8,128)}, u32[]{:S(2)}, u32[]{:S(2)}) collective-permute-start(f32[4,192,512]{2,1,0:T(8,128)} %get-tuple-element.72.refs_4_), channel_id=1, source_target_pairs={{0,96},{1,97},{2,98},{3,99},{4,100},{5,101},{6,102},{7,103},{8,104... | collective-permute-start | bytes 4718600 | tf_op jit(solution)/shard_map/ppermute | solution.py:413
  89.0 15.8 %slice-start.2 = ((s8[6291456]{0:T(1024)(128)(4,1)}), s8[2097152]{0:T(1024)(128)(4,1)S(1)}, s32[]{:S(2)}) async-start(s8[6291456]{0:T(1024)(128)(4,1)} %bitcast.31), calls=%async_computation.2 | async-start | bytes 4194304
  89.0 35.0 %collective-permute-start.11 = (f32[4,192,512]{2,1,0:T(8,128)}, f32[4,192,512]{2,1,0:T(8,128)}, u32[]{:S(2)}, u32[]{:S(2)}) collective-permute-start(f32[4,192,512]{2,1,0:T(8,128)} %get-tuple-element.79), channel_id=1, source_target_pairs={{0,4},{1,5},{2,6},{3,7},{4,8},{5,9},{6,10},{7,11},{8,12},{9,13},{1... | collective-permute-start | bytes 4718600 | tf_op jit(solution)/shard_map/ppermute | solution.py:413
  90.1 33.9 %collective-permute-start.12 = (f32[4,192,512]{2,1,0:T(8,128)}, f32[4,192,512]{2,1,0:T(8,128)}, u32[]{:S(2)}, u32[]{:S(2)}) collective-permute-start(f32[4,192,512]{2,1,0:T(8,128)} %get-tuple-element.73.refs_0_), channel_id=1, source_target_pairs={{0,12},{1,13},{2,14},{3,15},{4,0},{5,1},{6,2},{7,3},{8,4},{9,5},{1... | collective-permute-start | bytes 4718600 | tf_op jit(solution)/shard_map/ppermute | solution.py:413
  91.9 12.9 %slice-start.3 = ((s8[6291456]{0:T(1024)(128)(4,1)}), s8[4194304]{0:T(1024)(128)(4,1)S(1)}, s32[]{:S(2)}) async-start(s8[6291456]{0:T(1024)(128)(4,1)} %bitcast.31), calls=%async_computation.3 | async-start | bytes 8388608
  91.9 12.9 %copy-start.13 = (s32[3]{0:T(128)S(1)}, s32[3]{0:T(128)}, u32[]{:S(2)}) copy-start(s32[3]{0:T(128)} %pad_add_fusion.where) | copy-start | bytes 40
  91.9 12.9 %copy-start.15 = (s32[32]{0:T(128)S(1)}, s32[32]{0:T(128)}, u32[]{:S(2)}) copy-start(s32[32]{0:T(128)} %table.43) | copy-start | bytes 388
  91.9 34.4 %collective-permute-start.8 = (f32[4,192,512]{2,1,0:T(8,128)}, f32[4,192,512]{2,1,0:T(8,128)}, u32[]{:S(2)}, u32[]{:S(2)}) collective-permute-start(f32[4,192,512]{2,1,0:T(8,128)} %get-tuple-element.76), channel_id=1, source_target_pairs={{0,32},{1,33},{2,34},{3,35},{4,36},{5,37},{6,38},{7,39},{8,40},{9,... | collective-permute-start | bytes 4718600 | tf_op jit(solution)/shard_map/ppermute | solution.py:413
  104.8 2.2 copy-start
  107.0 3.4 %copy-start.3 = (f32[8,512,512]{2,1,0:T(8,128)S(1)}, f32[8,512,512]{2,1,0:T(8,128)}, u32[]{:S(2)}) copy-start(f32[8,512,512]{2,1,0:T(8,128)} %refs_7_.1) | copy-start | bytes 25165828
  110.4 4.9 %copy-start.8 = (f32[4,512,512]{2,1,0:T(8,128)S(1)}, f32[4,512,512]{2,1,0:T(8,128)}, u32[]{:S(2)}) copy-start(f32[4,512,512]{2,1,0:T(8,128)} %refs_8_.1) | copy-start | bytes 12582916
  110.4 4.9 %copy-start.11 = (bf16[768,2048]{1,0:T(8,128)(2,1)S(1)}, bf16[768,2048]{1,0:T(8,128)(2,1)}, u32[]{:S(2)}) copy-start(bf16[768,2048]{1,0:T(8,128)(2,1)} %refs_1_.7) | copy-start | bytes 9437188
  115.3 11.0 %copy-start.4 = (f32[4,192,512]{2,1,0:T(8,128)S(1)}, f32[4,192,512]{2,1,0:T(8,128)}, u32[]{:S(2)}) copy-start(f32[4,192,512]{2,1,0:T(8,128)} %get-tuple-element.78.refs_20_.refs_32_.refs_4_.refs_12_) | copy-start | bytes 4718596
  115.3 11.0 %copy-start.5 = (f32[4,192,512]{2,1,0:T(8,128)S(1)}, f32[4,192,512]{2,1,0:T(8,128)}, u32[]{:S(2)}) copy-start(f32[4,192,512]{2,1,0:T(8,128)} %get-tuple-element.80.refs_24_.refs_28_.refs_8_.refs_16_) | copy-start | bytes 4718596
  115.3 11.0 %copy-start.6 = (f32[4,192,512]{2,1,0:T(8,128)S(1)}, f32[4,192,512]{2,1,0:T(8,128)}, u32[]{:S(2)}) copy-start(f32[4,192,512]{2,1,0:T(8,128)} %get-tuple-element.75.refs_4_.refs_16_.refs_12_) | copy-start | bytes 4718596
  115.3 11.0 %copy-start.7 = (f32[4,192,512]{2,1,0:T(8,128)S(1)}, f32[4,192,512]{2,1,0:T(8,128)}, u32[]{:S(2)}) copy-start(f32[4,192,512]{2,1,0:T(8,128)} %get-tuple-element.77.refs_8_.refs_12_.refs_16_) | copy-start | bytes 4718596
  115.3 11.0 %copy-start.17 = (f32[4,1,512]{2,1,0:T(1,128)S(1)}, f32[4,1,512]{2,1,0:T(1,128)}, u32[]{:S(2)}) copy-start(f32[4,1,512]{2,1,0:T(1,128)} %copy-done.16) | copy-start | bytes 24580
  126.3 10.0 %copy-start.1 = (f32[16,128,512]{2,1,0:T(8,128)S(1)}, f32[16,128,512]{2,1,0:T(8,128)}, u32[]{:S(2)}) copy-start(f32[16,128,512]{2,1,0:T(8,128)} %get-tuple-element.74.refs_0_) | copy-start | bytes 12582916
  130.8 29.0 %collective-permute-start.13 = (f32[2,336,512]{2,1,0:T(8,128)S(1)}, f32[2,336,512]{2,1,0:T(8,128)S(1)}, u32[]{:S(2)}, u32[]{:S(2)}) collective-permute-start(f32[2,336,512]{2,1,0:T(8,128)S(1)} %get-tuple-element.84), channel_id=1, source_target_pairs={{0,4},{1,5},{2,6},{3,7},{4,8},{5,9},{6,10},{7,11},{8,12},{9,13},{1... | collective-permute-start | bytes 4128776 | tf_op jit(solution)/shard_map/ppermute | solution.py:413
  130.9 29.5 %collective-permute-start.14 = (f32[2,336,512]{2,1,0:T(8,128)S(1)}, f32[2,336,512]{2,1,0:T(8,128)S(1)}, u32[]{:S(2)}, u32[]{:S(2)}) collective-permute-start(f32[2,336,512]{2,1,0:T(8,128)S(1)} %get-tuple-element.86), channel_id=1, source_target_pairs={{0,12},{1,13},{2,14},{3,15},{4,0},{5,1},{6,2},{7,3},{8,4},{9,5},{1... | collective-permute-start | bytes 4128776 | tf_op jit(solution)/shard_map/ppermute | solution.py:413
  133.6 29.3 %collective-permute-start.15 = (f32[2,320,512]{2,1,0:T(8,128)S(1)}, f32[2,320,512]{2,1,0:T(8,128)S(1)}, u32[]{:S(2)}, u32[]{:S(2)}) collective-permute-start(f32[2,320,512]{2,1,0:T(8,128)S(1)} %get-tuple-element.88), channel_id=1, source_target_pairs={{0,32},{1,33},{2,34},{3,35},{4,36},{5,37},{6,38},{7,39},{8,40},{9,... | collective-permute-start | bytes 3932168 | tf_op jit(solution)/shard_map/ppermute | solution.py:413
  133.6 30.0 %collective-permute-start.16 = (f32[2,320,512]{2,1,0:T(8,128)S(1)}, f32[2,320,512]{2,1,0:T(8,128)S(1)}, u32[]{:S(2)}, u32[]{:S(2)}) collective-permute-start(f32[2,320,512]{2,1,0:T(8,128)S(1)} %get-tuple-element.81.refs_0_), channel_id=1, source_target_pairs={{0,96},{1,97},{2,98},{3,99},{4,100},{5,101},{6,102},{7,103},{8,104... | collective-permute-start | bytes 3932168 | tf_op jit(solution)/shard_map/ppermute | solution.py:413
  161.1 12.1 %collective-permute-start.18 = (f32[336,512]{1,0:T(8,128)S(1)}, f32[336,512]{1,0:T(8,128)S(1)}, u32[]{:S(2)}, u32[]{:S(2)}) collective-permute-start(f32[336,512]{1,0:T(8,128)S(1)} %shard_map.69.refs_0_), channel_id=1, source_target_pairs={{0,12},{1,13},{2,14},{3,15},{4,0},{5,1},{6,2},{7,3},{8,4},{9,5},{1... | collective-permute-start | bytes 2064392 | tf_op jit(solution)/shard_map/ppermute | solution.py:413
  162.9 12.6 %collective-permute-start.17 = (f32[336,512]{1,0:T(8,128)S(1)}, f32[336,512]{1,0:T(8,128)S(1)}, u32[]{:S(2)}, u32[]{:S(2)}) collective-permute-start(f32[336,512]{1,0:T(8,128)S(1)} %shard_map.68.refs_0_), channel_id=1, source_target_pairs={{0,4},{1,5},{2,6},{3,7},{4,8},{5,9},{6,10},{7,11},{8,12},{9,13},{1... | collective-permute-start | bytes 2064392 | tf_op jit(solution)/shard_map/ppermute | solution.py:413
  163.6 29.5 %slice-start.4 = ((s8[8388608]{0:T(1024)(128)(4,1)}), s8[4194304]{0:T(1024)(128)(4,1)S(1)}, s32[]{:S(2)}) async-start(s8[8388608]{0:T(1024)(128)(4,1)} %bitcast.33), calls=%async_computation.4 | async-start | bytes 8388608
  164.2 28.8 %slice-start.5 = ((s8[8388608]{0:T(1024)(128)(4,1)}), s8[4194304]{0:T(1024)(128)(4,1)S(1)}, s32[]{:S(2)}) async-start(s8[8388608]{0:T(1024)(128)(4,1)} %bitcast.33), calls=%async_computation.5 | async-start | bytes 8388608
  164.2 15.1 %collective-permute-start.22 = (f32[320,512]{1,0:T(8,128)S(1)}, f32[320,512]{1,0:T(8,128)S(1)}, u32[]{:S(2)}, u32[]{:S(2)}) collective-permute-start(f32[320,512]{1,0:T(8,128)S(1)} %shard_map.71.refs_0_), channel_id=1, source_target_pairs={{0,96},{1,97},{2,98},{3,99},{4,100},{5,101},{6,102},{7,103},{8,104... | collective-permute-start | bytes 1966088 | tf_op jit(solution)/shard_map/ppermute | solution.py:413
  164.3 15.0 %collective-permute-start.21 = (f32[320,512]{1,0:T(8,128)S(1)}, f32[320,512]{1,0:T(8,128)S(1)}, u32[]{:S(2)}, u32[]{:S(2)}) collective-permute-start(f32[320,512]{1,0:T(8,128)S(1)} %shard_map.70.refs_0_), channel_id=1, source_target_pairs={{0,32},{1,33},{2,34},{3,35},{4,36},{5,37},{6,38},{7,39},{8,40},{9,... | collective-permute-start | bytes 1966088 | tf_op jit(solution)/shard_map/ppermute | solution.py:413
  176.4 7.2 %collective-permute-start.19 = (f32[72,512]{1,0:T(8,128)S(1)}, f32[72,512]{1,0:T(8,128)S(1)}, u32[]{:S(2)}, u32[]{:S(2)}) collective-permute-start(f32[72,512]{1,0:T(8,128)S(1)} %get-tuple-element.92), channel_id=1, source_target_pairs={{0,32},{1,33},{2,34},{3,35},{4,36},{5,37},{6,38},{7,39},{8,40},{9,... | collective-permute-start | bytes 442376 | tf_op jit(solution)/shard_map/ppermute | solution.py:413
  176.8 6.8 %collective-permute-start.20 = (f32[72,512]{1,0:T(8,128)S(1)}, f32[72,512]{1,0:T(8,128)S(1)}, u32[]{:S(2)}, u32[]{:S(2)}) collective-permute-start(f32[72,512]{1,0:T(8,128)S(1)} %get-tuple-element.91.refs_0_), channel_id=1, source_target_pairs={{0,96},{1,97},{2,98},{3,99},{4,100},{5,101},{6,102},{7,103},{8,104... | collective-permute-start | bytes 442376 | tf_op jit(solution)/shard_map/ppermute | solution.py:413
  179.2 12.7 %collective-permute-start.24 = (f32[192,512]{1,0:T(8,128)S(1)}, f32[192,512]{1,0:T(8,128)S(1)}, u32[]{:S(2)}, u32[]{:S(2)}) collective-permute-start(f32[192,512]{1,0:T(8,128)S(1)} %get-tuple-element.98), channel_id=1, source_target_pairs={{0,16},{1,17},{2,18},{3,19},{4,20},{5,21},{6,22},{7,23},{8,24},{9,... | collective-permute-start | bytes 1179656 | tf_op jit(solution)/shard_map/ppermute | solution.py:413
  184.5 11.4 %collective-permute-start.28 = (f32[192,512]{1,0:T(8,128)S(1)}, f32[192,512]{1,0:T(8,128)S(1)}, u32[]{:S(2)}, u32[]{:S(2)}) collective-permute-start(f32[192,512]{1,0:T(8,128)S(1)} %get-tuple-element.104), channel_id=1, source_target_pairs={{0,16},{1,17},{2,18},{3,19},{4,20},{5,21},{6,22},{7,23},{8,24},{9,... | collective-permute-start | bytes 1179656 | tf_op jit(solution)/shard_map/ppermute | solution.py:413
  184.7 5.5 %collective-permute-start.23 = (f32[72,512]{1,0:T(8,128)S(1)}, f32[72,512]{1,0:T(8,128)S(1)}, u32[]{:S(2)}, u32[]{:S(2)}) collective-permute-start(f32[72,512]{1,0:T(8,128)S(1)} %get-tuple-element.95), channel_id=1, source_target_pairs={{0,64},{1,65},{2,66},{3,67},{4,68},{5,69},{6,70},{7,71},{8,72},{9,... | collective-permute-start | bytes 442376 | tf_op jit(solution)/shard_map/ppermute | solution.py:413
  184.7 9.4 %collective-permute-start.25 = (f32[64,512]{1,0:T(8,128)S(1)}, f32[64,512]{1,0:T(8,128)S(1)}, u32[]{:S(2)}, u32[]{:S(2)}) collective-permute-start(f32[64,512]{1,0:T(8,128)S(1)} %get-tuple-element.100), channel_id=1, source_target_pairs={{0,4},{1,5},{2,6},{3,7},{4,8},{5,9},{6,10},{7,11},{8,12},{9,13},{1... | collective-permute-start | bytes 393224 | tf_op jit(solution)/shard_map/ppermute | solution.py:413
  184.8 9.3 %collective-permute-start.26 = (f32[64,512]{1,0:T(8,128)S(1)}, f32[64,512]{1,0:T(8,128)S(1)}, u32[]{:S(2)}, u32[]{:S(2)}) collective-permute-start(f32[64,512]{1,0:T(8,128)S(1)} %get-tuple-element.101), channel_id=1, source_target_pairs={{0,8},{1,9},{2,10},{3,11},{4,12},{5,13},{6,14},{7,15},{8,0},{9,1},... | collective-permute-start | bytes 393224 | tf_op jit(solution)/shard_map/ppermute | solution.py:413
  190.2 4.1 %collective-permute-start.27 = (f32[64,512]{1,0:T(8,128)S(1)}, f32[64,512]{1,0:T(8,128)S(1)}, u32[]{:S(2)}, u32[]{:S(2)}) collective-permute-start(f32[64,512]{1,0:T(8,128)S(1)} %get-tuple-element.93.refs_0_), channel_id=1, source_target_pairs={{0,12},{1,13},{2,14},{3,15},{4,0},{5,1},{6,2},{7,3},{8,4},{9,5},{1... | collective-permute-start | bytes 393224 | tf_op jit(solution)/shard_map/ppermute | solution.py:413
  191.9 4.0 %collective-permute-start.29 = (f32[8,512]{1,0:T(8,128)S(1)}, f32[8,512]{1,0:T(8,128)S(1)}, u32[]{:S(2)}, u32[]{:S(2)}) collective-permute-start(f32[8,512]{1,0:T(8,128)S(1)} %get-tuple-element.96.refs_0_.refs_5_), channel_id=1, source_target_pairs={{0,16},{1,17},{2,18},{3,19},{4,20},{5,21},{6,22},{7,23},{8,24},{9,... | collective-permute-start | bytes 49160 | tf_op jit(solution)/shard_map/ppermute | solution.py:413
  194.9 2.2 copy-start.9
  200.9 15.2 %collective-permute-start.30 = (f32[512,512]{1,0:T(8,128)S(1)}, f32[512,512]{1,0:T(8,128)S(1)}, u32[]{:S(2)}, u32[]{:S(2)}) collective-permute-start(f32[512,512]{1,0:T(8,128)S(1)} %shard_map.78), channel_id=1, source_target_pairs={{0,16},{1,17},{2,18},{3,19},{4,20},{5,21},{6,22},{7,23},{8,24},{9,... | collective-permute-start | bytes 3145736 | tf_op jit(solution)/shard_map/ppermute | solution.py:413
  202.3 24.2 %collective-permute-start.31 = (f32[512,512]{1,0:T(8,128)S(1)}, f32[512,512]{1,0:T(8,128)S(1)}, u32[]{:S(2)}, u32[]{:S(2)}) collective-permute-start(f32[512,512]{1,0:T(8,128)S(1)} %shard_map.78), channel_id=1, source_target_pairs={{0,18},{1,19},{2,16},{3,17},{4,22},{5,23},{6,20},{7,21},{8,26},{9,... | collective-permute-start | bytes 3145736 | tf_op jit(solution)/shard_map/ppermute | solution.py:413
  216.1 13.7 %collective-permute-start.32 = (f32[512,512]{1,0:T(8,128)S(1)}, f32[512,512]{1,0:T(8,128)S(1)}, u32[]{:S(2)}, u32[]{:S(2)}) collective-permute-start(f32[512,512]{1,0:T(8,128)S(1)} %collective-permute-done.30), channel_id=1, source_target_pairs={{0,1},{1,0},{2,3},{3,2},{4,5},{5,4},{6,7},{7,6},{8,9},{9,8},{10,11... | collective-permute-start | bytes 3145736 | tf_op jit(solution)/shard_map/ppermute | solution.py:413
  226.6 5.0 %collective-permute-start.33 = (f32[512,512]{1,0:T(8,128)S(1)}, f32[512,512]{1,0:T(8,128)}, u32[]{:S(2)}, u32[]{:S(2)}) collective-permute-start(f32[512,512]{1,0:T(8,128)S(1)} %collective-permute-done.31), channel_id=1, source_target_pairs={{0,1},{1,0},{2,3},{3,2},{4,5},{5,4},{6,7},{7,6},{8,9},{9,8},{10,11... | collective-permute-start | bytes 3145736 | tf_op jit(solution)/shard_map/ppermute | solution.py:413
  229.9 2.0 copy-start.19

commit v4 on v3

--- a/solution.py
+++ b/solution.py
@@ -356,31 +356,43 @@
     return w[0] * 8 + (1 - w[1]) * 4 + w[2]
 
 
-def rotate_body(joined, table, where, first, second, basis, out):
-    a = split(basis[0])
-    if joined:
-        value = first[...] + second[...]
-    else:
-        value = jnp.concatenate([first[...], second[...]], axis=0)
-    out[...] = dot3(split(value), a, ((1,), (0,)))
-
-
-def rotate(order, first, second, eig_in, joined):
-    ins = [(a, whole(a)) for a in (first, second)]
-    ins.append((eig_in, spec((1, BLK, BLK), lambda i, t, w: (t[mine(w)] >> 2, 0, 0))))
-    rows = first.shape[0] * (1 if joined else 2)
-    body = functools.partial(rotate_body, joined)
-    return order(body, 1, ins, [full(rows, BLK)], vmem=TURN)[0]
+def bases_body(table, where, basis_in, basis_out, *outs):
+    outs[0][...], outs[1][...] = split(basis_in[0])
+    outs[2][...], outs[3][...] = split(basis_out[0])
+
+
+def bases(order, eig_in, eig_out):
+    ins = [
+        (eig_in, spec((1, BLK, BLK), lambda i, t, w: (t[mine(w)] >> 2, 0, 0))),
+        (eig_out, spec((1, BLK, BLK), lambda i, t, w: (t[mine(w)] & 3, 0, 0))),
+    ]
+    outs = [(*full(BLK, BLK), jnp.bfloat16)] * 4
+    made = order(bases_body, 1, ins, outs)
+    return made[:2], made[2:]
+
+
+def rotate_body(table, where, high, low, *refs):
+    parts, out = refs[:-1], refs[-1]
+    value = parts[0][...] + parts[1][...]
+    if len(parts) > 2:
+        value = value + (parts[2][...] + parts[3][...])
+        value = jnp.concatenate([value, parts[4][...]], axis=0)
+    out[...] = dot3(split(value), (high[...], low[...]), ((1,), (0,)))
+
+
+def rotate(order, basis, parts):
+    ins = [(a, whole(a)) for a in (*basis, *parts)]
+    rows = parts[0].shape[0] * (1 if len(parts) == 2 else 2)
+    return order(rotate_body, 1, ins, [full(rows, BLK)])[0]
 
 
 def precondition_body(tokens_all, table, where, *refs):
     x, c, y0, y1, ours, theirs = (r[...] for r in refs[:6])
-    basis_in, basis_out, out = refs[6:]
+    a, b = (refs[6][...], refs[7][...]), (refs[8][...], refs[9][...])
+    out = refs[10]
     scale = 1.0 / tokens_all
     values_in = (ours[0:1] + theirs[2:3]) * scale
     values_out = (ours[1:2] + theirs[3:4]) * scale
-    a = split(basis_in[0])
-    b = split(basis_out[0])
     y = dot3(split(y0 + y1), a, ((1,), (0,)))
     rotated = jnp.concatenate([x, y, c], axis=0) * scale
     rotated = dot3(b, split(rotated), ((0,), (0,)))
@@ -389,10 +401,8 @@
     out[...] = dot3(a, split(back), ((1,), (1,)))
 
 
-def precondition(tokens_all, order, parts, eig_in, eig_out):
-    ins = [(q, whole(q)) for q in parts]
-    ins.append((eig_in, spec((1, BLK, BLK), lambda i, t, w: (t[mine(w)] >> 2, 0, 0))))
-    ins.append((eig_out, spec((1, BLK, BLK), lambda i, t, w: (t[mine(w)] & 3, 0, 0))))
+def precondition(tokens_all, order, parts, basis_in, basis_out):
+    ins = [(q, whole(q)) for q in (*parts, *basis_in, *basis_out)]
     return order(
         functools.partial(precondition_body, tokens_all),
         1,
@@ -423,6 +433,7 @@
     got_b = both(*made[:2], "x") + both(*made[2:4], "y")
     sets_t = relay(order, got_a, made[4:])
     sums = [square_sums(order, latents, eig_in, 0, 4)]
+    basis_in, basis_out = bases(order, eig_in, eig_out)
     got_t = both(*order.gate(sets_t[:2], got_b[:2]), "x")
     got_t += both(*order.gate(sets_t[2:], got_b[2:]), "y")
     got_b = [got_b[n] for n in (1, 0, 3, 2)]
@@ -453,13 +464,16 @@
     order.also = [parts_cy[1], parts_cy[3]]
     away_y, keep_y, *parts_cx = end(order, "y", mine_y, *msgs_y, *more_y)
     got_y = send(away_y, near)
+    turned_x = rotate(order, basis_in, [keep_x, got_x])
     done_cy, ours = total(order, parts_cy)
     theirs = send(ours, near)
-    turned_x = rotate(order, keep_x, got_x, eig_in, True)
-    (done_cx,) = total(order, far(parts_cx, "y"))
-    turned_c = rotate(order, done_cx, done_cy, eig_in, False)
+    turned_c = rotate(order, basis_in, [*far(parts_cx, "y"), done_cy])
     update = precondition(
-        tokens_all, order, [turned_x, turned_c, keep_y, got_y, ours, theirs], eig_in, eig_out
+        tokens_all,
+        order,
+        [turned_x, turned_c, keep_y, got_y, ours, theirs],
+        basis_in,
+        basis_out,
     )
     same = send(update, near)
     other = send(update, cross)

time: 234 us -> 233 us (level)
  waiting for transfers between devices: 76.6 us -> 70.3 us
    ppermute x34, waiting for transfers between devices: 76.6 us -> 70.3 us  [on_device(): send = lambda value, pairs: lax.ppermute(value, AXES, pairs)]
    unnamed x54 -> x56, local copies, waits for them, and re-layouts: 13.8 us -> 15.8 us
  transfers between devices with their start and end apart: 34 -> 34, of which waited for: 12 -> 13; matrix products, arithmetic and copies ran while one was open for 0% -> 0% of each run, Pallas kernels for 29% -> 30%
where the time goes in v4:
time: 233 us
  Pallas kernels  89.3 us (38%)
  waiting for transfers between devices  70.3 us (30%)
  starting transfers between devices  53.2 us (23%)
  local copies, waits for them, and re-layouts  18.8 us (8%)
    pallas_call x22, Pallas kernels, __call__(): pl.pallas_call(inner, out_shape=shapes, grid_spec=pltpu.PrefetchScalarGri...  89.3 us
    ppermute x34, waiting for transfers between devices, on_device(): send = lambda value, pairs: lax.ppermute(value, AXES, pairs)  70.3 us
    ppermute x34, starting transfers between devices, on_device(): send = lambda value, pairs: lax.ppermute(value, AXES, pairs)  53.2 us
    unnamed x56, local copies, waits for them, and re-layouts  15.8 us
  transfers between devices with their start and end apart: 34, of which 13 were waited for; matrix products, arithmetic and copies ran while one was open for 0% of the time, Pallas kernels for 30%

profile of v4, /device:TPU:1, one launch (start us, length us, event | category | flops | bytes accessed | tf_op | source)
XLA Modules:
  0.0 232.7 jit_solution(653772795365383532)
XLA Ops:
  0.0 0.7 pad_add_fusion.where
  0.7 11.4 %shard_map.55 = (bf16[2048,768]{1,0:T(8,128)(2,1)}, f32[4,192,512]{2,1,0:T(8,128)}, f32[4,192,512]{2,1,0:T(8,128)}, f32[4,192,512]{2,1,0:T(8,128)}, f32[4,192,512]{2,1,0:T(8,128)}) custom-call(s32[32]{0:T(128)} %table.43, s32[3]{0:T(128)} %pad_add_fusion.where, bf16[768,2048]{1,0:T(8,128)(2,1)} %refs_1_.9, bf16[768,4096]{1,0:T(8,128)(2,1)} %refs_1_.8, ...), custom_call_target="tpu_custom_call" | custom-call | bytes 3690000 | tf_op jit(solution)/shard_map/pallas_call | solution.py:118
  12.1 2.3 collective-permute-start
  14.4 1.5 collective-permute-start.1
  15.9 1.3 collective-permute-start.2
  17.2 1.4 collective-permute-start.3
  18.6 8.2 %shard_map.56.refs_0_ = f32[16,128,512]{2,1,0:T(8,128)} custom-call(s32[32]{0:T(128)} %table.43, s32[3]{0:T(128)} %pad_add_fusion.where, f32[4,192,512]{2,1,0:T(8,128)} %get-tuple-element.59.refs_0_, bf16[2048,768]{1,0:T(8,128)(2,1)} %get-tuple-element.60.refs_1_, bf16[768,4096]{1,0:T(8,128)(2,1)} %refs_1_.8), custom_call_target="tpu_custom_call" | custom-call | bytes 3690000 | tf_op jit(solution)/shard_map/pallas_call | solution.py:118
  26.8 1.6 collective-permute-start.9
  28.5 12.4 %shard_map.57 = (f32[4,192,512]{2,1,0:T(8,128)}, f32[4,192,512]{2,1,0:T(8,128)}, f32[4,192,512]{2,1,0:T(8,128)}, f32[4,192,512]{2,1,0:T(8,128)}, f32[4,192,512]{...) custom-call(s32[32]{0:T(128)} %table.43, s32[3]{0:T(128)} %pad_add_fusion.where, ...), custom_call_target="tpu_custom_call" | custom-call | bytes 3690000 | tf_op jit(solution)/shard_map/pallas_call | solution.py:118
  40.9 9.3 %collective-permute-done.refs_1_ = f32[4,192,512]{2,1,0:T(8,128)S(1)} collective-permute-done((f32[4,192,512]{2,1,0:T(8,128)}, f32[4,192,512]{2,1,0:T(8,128)S(1)}, u32[]{:S(2)}, u32[]{:S(2)}) %collective-permute-start) | collective-permute-done | bytes 1572896 | tf_op jit(solution)/shard_map/ppermute | solution.py:423
  50.2 2.7 %collective-permute-start.7 = (f32[4,192,512]{2,1,0:T(8,128)}, f32[4,192,512]{2,1,0:T(8,128)}, u32[]{:S(2)}, u32[]{:S(2)}) collective-permute-start(f32[4,192,512]{2,1,0:T(8,128)} %get-tuple-element.75), channel_id=1, source_target_pairs={{0,96},{1,97},{2,98},{3,99},{4,100},{5,101},{6,102},{7,103},{8,104... | collective-permute-start | bytes 4718600 | tf_op jit(solution)/shard_map/ppermute | solution.py:423
  52.9 1.1 collective-permute-start.4
  54.0 1.7 collective-permute-start.5
  55.7 8.2 %shard_map.58 = (f32[4,192,512]{2,1,0:T(8,128)}, f32[4,192,512]{2,1,0:T(8,128)}, f32[4,192,512]{2,1,0:T(8,128)}, f32[4,192,512]{2,1,0:T(8,128)}) custom-call(s32[32]{0:T(128)} %table.43, s32[3]{0:T(128)} %pad_add_fusion.where, f32[4,192,512]{2,1,0:T(8,128)} %get-tuple-element.61.refs_0_.refs_8_, f32[4,192,512]{2,1,0:T(8,128)} %copy-done.22, ...), custom_call_target="tpu_custom_call" | custom-call | bytes 3690000 | tf_op jit(solution)/shard_map/pallas_call | solution.py:118
  63.9 3.4 %copy-done.2 = f32[8,512,512]{2,1,0:T(8,128)S(1)} copy-done((f32[8,512,512]{2,1,0:T(8,128)S(1)}, f32[8,512,512]{2,1,0:T(8,128)}, u32[]{:S(2)}) %copy-start.2) | copy-done | bytes 8388632
  67.2 1.4 copy-done.11
  68.7 4.8 %shard_map.59.refs_0_.refs_1_ = f32[4,1,512]{2,1,0:T(1,128)S(1)} custom-call(s32[32]{0:T(128)S(1)} %copy-done.19, s32[3]{0:T(128)S(1)} %copy-done.17, f32[4,192,512]{2,1,0:T(8,128)S(1)} %copy-done.11, bf16[768,4096]{1,0:T(8,128)(2,1)S(1)} %bitcast.30, f32[8,512,512]{2,1,0:T(8,128)S(1)} %copy-done.2), custom_call_target="tpu_custom_call" | custom-call | bytes 3690000 | tf_op jit(solution)/shard_map/pallas_call | solution.py:118
  73.5 3.4 %copy-done.3 = f32[8,512,512]{2,1,0:T(8,128)S(1)} copy-done((f32[8,512,512]{2,1,0:T(8,128)S(1)}, f32[8,512,512]{2,1,0:T(8,128)}, u32[]{:S(2)}) %copy-start.3) | copy-done | bytes 8388632
  76.9 0.8 shard_map.60
  77.7 0.8 copy-done.13
  78.5 0.8 copy-done.15
  79.3 7.2 %collective-permute-done.6.refs_2_.refs_4_ = f32[4,192,512]{2,1,0:T(8,128)} collective-permute-done((f32[4,192,512]{2,1,0:T(8,128)}, f32[4,192,512]{2,1,0:T(8,128)}, u32[]{:S(2)}, u32[]{:S(2)}) %collective-permute-start.6) | collective-permute-done | bytes 1572896 | tf_op jit(solution)/shard_map/ppermute | solution.py:423
  86.5 2.4 %collective-permute-start.10 = (f32[4,192,512]{2,1,0:T(8,128)}, f32[4,192,512]{2,1,0:T(8,128)}, u32[]{:S(2)}, u32[]{:S(2)}) collective-permute-start(f32[4,192,512]{2,1,0:T(8,128)} %get-tuple-element.77.refs_4_), channel_id=1, source_target_pairs={{0,96},{1,97},{2,98},{3,99},{4,100},{5,101},{6,102},{7,103},{8,104... | collective-permute-start | bytes 4718600 | tf_op jit(solution)/shard_map/ppermute | solution.py:423
  88.9 0.9 collective-permute-start.11
  89.9 1.8 collective-permute-start.12
  91.7 12.9 %shard_map.63 = (f32[4,192,512]{2,1,0:T(8,128)}, f32[4,192,512]{2,1,0:T(8,128)}, f32[4,192,512]{2,1,0:T(8,128)}, f32[4,192,512]{2,1,0:T(8,128)}, f32[16,128,512]{2,1,0:T(8,128)}) custom-call(s32[32]{0:T(128)} %table.43, s32[3]{0:T(128)} %pad_add_fusion.where, f32[4,192,512]{2,1,0:T(8,128)} %get-tuple-element.78.refs_0_, ...), custom_call_target="tpu_custom_call" | custom-call | bytes 3690000 | tf_op jit(solution)/shard_map/pallas_call | solution.py:118
  104.7 2.2 copy-done
  106.9 3.4 %copy-done.4 = f32[8,512,512]{2,1,0:T(8,128)S(1)} copy-done((f32[8,512,512]{2,1,0:T(8,128)S(1)}, f32[8,512,512]{2,1,0:T(8,128)}, u32[]{:S(2)}) %copy-start.4) | copy-done | bytes 8388632
  110.3 4.8 %shard_map.64.refs_0_.refs_2_ = f32[4,1,512]{2,1,0:T(1,128)S(1)} custom-call(s32[32]{0:T(128)S(1)} %copy-done.20, s32[3]{0:T(128)S(1)} %copy-done.18, f32[16,128,512]{2,1,0:T(8,128)S(1)} %copy-done, bf16[768,4096]{1,0:T(8,128)(2,1)S(1)} %bitcast.32, f32[8,512,512]{2,1,0:T(8,128)S(1)} %copy-done.4), custom_call_target="tpu_custom_call" | custom-call | bytes 3690000 | tf_op jit(solution)/shard_map/pallas_call | solution.py:118
  115.1 4.8 %shard_map.65.refs_0_.refs_3_ = f32[4,1,512]{2,1,0:T(1,128)S(1)} custom-call(s32[32]{0:T(128)S(1)} %copy-done.20, s32[3]{0:T(128)S(1)} %copy-done.18, f32[4,1,512]{2,1,0:T(1,128)S(1)} %shard_map.64.refs_0_.refs_2_, bf16[768,2048]{1,0:T(8,128)(2,1)S(1)} %copy-done.12, f32[4,512,512]{2,1,0:T(8,128)S(1)} %copy-done.10), custom_call_target="tpu_custom_call" | custom-call | bytes 3690000 | tf_op jit(solution)/shard_map/pallas_call | solution.py:118
  120.0 3.9 %collective-permute-done.11.refs_21_.refs_33_.refs_5_.refs_13_ = f32[4,192,512]{2,1,0:T(8,128)} collective-permute-done((f32[4,192,512]{2,1,0:T(8,128)}, f32[4,192,512]{2,1,0:T(8,128)}, u32[]{:S(2)}, u32[]{:S(2)}) %collective-permute-start.11) | collective-permute-done | bytes 1572896 | tf_op jit(solution)/shard_map/ppermute | solution.py:423
  123.8 2.1 collective-permute-done.8.refs_5_.refs_17_.refs_13_
  126.0 5.4 %shard_map.66 = (f32[2,336,512]{2,1,0:T(8,128)S(1)}, f32[2,336,512]{2,1,0:T(8,128)S(1)}, f32[2,320,512]{2,1,0:T(8,128)}, f32[2,320,512]{2,1,0:T(8,128)S(1)}) custom-call(s32[32]{0:T(128)S(1)} %copy-done.20, s32[3]{0:T(128)S(1)} %copy-done.18, f32[4,1,512]{2,1,0:T(1,128)S(1)} %shard_map.65.refs_0_.refs_3_, f32[4,1,512]{2,1,0:T(1,128)S(1)} %shard_map.59.refs_0_.refs_1_, ...), custom_call_target="tpu_custom_call" | custom-call | bytes 3690000 | tf_op jit(solution)/shard_map/pallas_call | solution.py:118
  131.4 2.7 %collective-permute-start.14 = (f32[2,336,512]{2,1,0:T(8,128)S(1)}, f32[2,336,512]{2,1,0:T(8,128)S(1)}, u32[]{:S(2)}, u32[]{:S(2)}) collective-permute-start(f32[2,336,512]{2,1,0:T(8,128)S(1)} %get-tuple-element.91), channel_id=1, source_target_pairs={{0,12},{1,13},{2,14},{3,15},{4,0},{5,1},{6,2},{7,3},{8,4},{9,5},{1... | collective-permute-start | bytes 4128776 | tf_op jit(solution)/shard_map/ppermute | solution.py:423
  134.1 2.7 %collective-permute-start.16 = (f32[2,320,512]{2,1,0:T(8,128)S(1)}, f32[2,320,512]{2,1,0:T(8,128)S(1)}, u32[]{:S(2)}, u32[]{:S(2)}) collective-permute-start(f32[2,320,512]{2,1,0:T(8,128)S(1)} %get-tuple-element.86.refs_0_), channel_id=1, source_target_pairs={{0,96},{1,97},{2,98},{3,99},{4,100},{5,101},{6,102},{7,103},{8,104... | collective-permute-start | bytes 3932168 | tf_op jit(solution)/shard_map/ppermute | solution.py:423
  136.8 2.5 %shard_map.67 = (f32[336,512]{1,0:T(8,128)S(1)}, f32[336,512]{1,0:T(8,128)S(1)}, f32[2,336,512]{2,1,0:T(8,128)S(1)}) custom-call(s32[32]{0:T(128)S(1)} %copy-done.20, s32[3]{0:T(128)S(1)} %copy-done.18, f32[2,320,512]{2,1,0:T(8,128)S(1)} %get-tuple-element.86.refs_0_, f32[4,1,512]{2,1,0:T(1,128)S(1)} %shard_map.59.refs_0_.refs_1_, ...), custom_call_target="tpu_custom_call" | custom-call | bytes 3690000 | tf_op jit(solution)/shard_map/pallas_call | solution.py:118
  139.3 2.5 %shard_map.68 = (f32[320,512]{1,0:T(8,128)S(1)}, f32[320,512]{1,0:T(8,128)S(1)}, f32[2,320,512]{2,1,0:T(8,128)S(1)}) custom-call(s32[32]{0:T(128)S(1)} %copy-done.20, s32[3]{0:T(128)S(1)} %copy-done.18, f32[2,336,512]{2,1,0:T(8,128)S(1)} %get-tuple-element.87.refs_0_.refs_1_, f32[4,1,512]{2,1,0:T(1,128)S(1)} %shard_map.59.refs_0_.refs_1_, ...), custom_call_target="tpu_custom_call" | custom-call | bytes 3690000 | tf_op jit(solution)/shard_map/pallas_call | solution.py:118
  141.8 18.4 %collective-permute-done.13.refs_1_.refs_2_ = f32[2,336,512]{2,1,0:T(8,128)S(1)} collective-permute-done((f32[2,336,512]{2,1,0:T(8,128)S(1)}, f32[2,336,512]{2,1,0:T(8,128)S(1)}, u32[]{:S(2)}, u32[]{:S(2)}) %collective-permute-start.13) | collective-permute-done | bytes 1376288 | tf_op jit(solution)/shard_map/ppermute | solution.py:423
  160.2 0.6 shard_map.69.refs_0_
  160.8 0.6 shard_map.70.refs_0_
  161.5 1.8 collective-permute-start.18
  164.6 1.5 collective-permute-start.21
  166.1 7.4 %collective-permute-done.18.refs_5_ = f32[336,512]{1,0:T(8,128)S(1)} collective-permute-done((f32[336,512]{1,0:T(8,128)S(1)}, f32[336,512]{1,0:T(8,128)S(1)}, u32[]{:S(2)}, u32[]{:S(2)}) %collective-permute-start.18) | collective-permute-done | bytes 688160 | tf_op jit(solution)/shard_map/ppermute | solution.py:423
  173.4 2.2 collective-permute-done.17.refs_4_
  175.6 0.9 shard_map.73
  176.6 2.7 %collective-permute-start.20 = (f32[72,512]{1,0:T(8,128)S(1)}, f32[72,512]{1,0:T(8,128)S(1)}, u32[]{:S(2)}, u32[]{:S(2)}) collective-permute-start(f32[72,512]{1,0:T(8,128)S(1)} %get-tuple-element.96.refs_0_), channel_id=1, source_target_pairs={{0,96},{1,97},{2,98},{3,99},{4,100},{5,101},{6,102},{7,103},{8,104... | collective-permute-start | bytes 442376 | tf_op jit(solution)/shard_map/ppermute | solution.py:423
  179.3 2.0 collective-permute-start.23
  181.3 2.4 %collective-permute-done.19.refs_1_.refs_2_ = f32[72,512]{1,0:T(8,128)S(1)} collective-permute-done((f32[72,512]{1,0:T(8,128)S(1)}, f32[72,512]{1,0:T(8,128)S(1)}, u32[]{:S(2)}, u32[]{:S(2)}) %collective-permute-start.19) | collective-permute-done | bytes 147488 | tf_op jit(solution)/shard_map/ppermute | solution.py:423
  183.7 0.8 shard_map.74
  184.6 2.1 collective-permute-start.28
  186.7 1.9 collective-permute-start.26
  188.6 0.8 collective-permute-start.27
  189.4 1.0 shard_map.75.refs_0_.refs_1_
  190.4 1.8 collective-permute-done.24.refs_3_
  193.3 0.8 collective-permute-done.27.refs_6_
  194.1 0.9 shard_map.77.refs_0_.refs_2_
  195.0 1.2 collective-permute-done.29.refs_6_
  196.2 3.8 %shard_map.78 = f32[512,512]{1,0:T(8,128)S(1)} custom-call(s32[32]{0:T(128)S(1)} %copy-done.20, s32[3]{0:T(128)S(1)} %copy-done.18, f32[128,512]{1,0:T(8,128)S(1)} %shard_map.77.refs_0_.refs_2_, f32[192,512]{1,0:T(8,128)S(1)} %shard_map.75.refs_0_.refs_1_, f32[128,512]{1,0:T(8,128)S(1)} %shard_map.77.refs_0_.refs_2_, ...), custom_call_target="tpu_custom_call" | custom-call | bytes 3690000 | tf_op jit(solution)/shard_map/pallas_call | solution.py:118
  200.3 3.2 %collective-permute-start.31 = (f32[512,512]{1,0:T(8,128)S(1)}, f32[512,512]{1,0:T(8,128)S(1)}, u32[]{:S(2)}, u32[]{:S(2)}) collective-permute-start(f32[512,512]{1,0:T(8,128)S(1)} %shard_map.78), channel_id=1, source_target_pairs={{0,18},{1,19},{2,16},{3,17},{4,22},{5,23},{6,20},{7,21},{8,26},{9,... | collective-permute-start | bytes 3145736 | tf_op jit(solution)/shard_map/ppermute | solution.py:423
  203.5 12.0 %collective-permute-done.30 = f32[512,512]{1,0:T(8,128)S(1)} collective-permute-done((f32[512,512]{1,0:T(8,128)S(1)}, f32[512,512]{1,0:T(8,128)S(1)}, u32[]{:S(2)}, u32[]{:S(2)}) %collective-permute-start.30) | collective-permute-done | bytes 1048608 | tf_op jit(solution)/shard_map/ppermute | solution.py:423
  215.5 10.4 %collective-permute-start.32 = (f32[512,512]{1,0:T(8,128)S(1)}, f32[512,512]{1,0:T(8,128)S(1)}, u32[]{:S(2)}, u32[]{:S(2)}) collective-permute-start(f32[512,512]{1,0:T(8,128)S(1)} %collective-permute-done.30), channel_id=1, source_target_pairs={{0,1},{1,0},{2,3},{3,2},{4,5},{5,4},{6,7},{7,6},{8,9},{9,8},{10,11... | collective-permute-start | bytes 3145736 | tf_op jit(solution)/shard_map/ppermute | solution.py:423
  225.8 1.8 collective-permute-start.33
  228.4 1.6 collective-permute-done.33
  230.4 2.3 bitcast_dynamic-update-slice_fusion
  (92 shorter events, 4.0 us)
Async XLA Ops:
  12.1 38.2 %collective-permute-start = (f32[4,192,512]{2,1,0:T(8,128)}, f32[4,192,512]{2,1,0:T(8,128)S(1)}, u32[]{:S(2)}, u32[]{:S(2)}) collective-permute-start(f32[4,192,512]{2,1,0:T(8,128)} %get-tuple-element.62), channel_id=1, source_target_pairs={{0,32},{1,33},{2,34},{3,35},{4,36},{5,37},{6,38},{7,39},{8,40},{9,... | collective-permute-start | bytes 4718600 | tf_op jit(solution)/shard_map/ppermute | solution.py:423
  14.4 35.9 %collective-permute-start.1 = (f32[4,192,512]{2,1,0:T(8,128)}, f32[4,192,512]{2,1,0:T(8,128)S(1)}, u32[]{:S(2)}, u32[]{:S(2)}) collective-permute-start(f32[4,192,512]{2,1,0:T(8,128)} %get-tuple-element.63), channel_id=1, source_target_pairs={{0,96},{1,97},{2,98},{3,99},{4,100},{5,101},{6,102},{7,103},{8,104... | collective-permute-start | bytes 4718600 | tf_op jit(solution)/shard_map/ppermute | solution.py:423
  15.9 37.0 %collective-permute-start.2 = (f32[4,192,512]{2,1,0:T(8,128)}, f32[4,192,512]{2,1,0:T(8,128)}, u32[]{:S(2)}, u32[]{:S(2)}) collective-permute-start(f32[4,192,512]{2,1,0:T(8,128)} %get-tuple-element.64), channel_id=1, source_target_pairs={{0,4},{1,5},{2,6},{3,7},{4,8},{5,9},{6,10},{7,11},{8,12},{9,13},{1... | collective-permute-start | bytes 4718600 | tf_op jit(solution)/shard_map/ppermute | solution.py:423
  17.2 36.8 %collective-permute-start.3 = (f32[4,192,512]{2,1,0:T(8,128)}, f32[4,192,512]{2,1,0:T(8,128)}, u32[]{:S(2)}, u32[]{:S(2)}) collective-permute-start(f32[4,192,512]{2,1,0:T(8,128)} %get-tuple-element.59.refs_0_), channel_id=1, source_target_pairs={{0,12},{1,13},{2,14},{3,15},{4,0},{5,1},{6,2},{7,3},{8,4},{9,5},{1... | collective-permute-start | bytes 4718600 | tf_op jit(solution)/shard_map/ppermute | solution.py:423
  26.8 99.1 %collective-permute-start.9 = (f32[16,128,512]{2,1,0:T(8,128)}, f32[16,128,512]{2,1,0:T(8,128)}, u32[]{:S(2)}, u32[]{:S(2)}) collective-permute-start(f32[16,128,512]{2,1,0:T(8,128)} %shard_map.56.refs_0_), channel_id=1, source_target_pairs={{0,16},{1,17},{2,18},{3,19},{4,20},{5,21},{6,22},{7,23},{8,24},{9,... | collective-permute-start | bytes 12582920 | tf_op jit(solution)/shard_map/ppermute | solution.py:423
  28.5 35.4 %slice-start = ((s8[6291456]{0:T(1024)(128)(4,1)}), s8[4194304]{0:T(1024)(128)(4,1)S(1)}, s32[]{:S(2)}) async-start(s8[6291456]{0:T(1024)(128)(4,1)} %bitcast.29), calls=%async_computation | async-start | bytes 8388608
  50.2 5.4 %copy-start.22 = (f32[4,192,512]{2,1,0:T(8,128)}, f32[4,192,512]{2,1,0:T(8,128)S(1)}, u32[]{:S(2)}) copy-start(f32[4,192,512]{2,1,0:T(8,128)S(1)} %collective-permute-done.refs_1_) | copy-start | bytes 4718596
  50.2 36.3 %collective-permute-start.6 = (f32[4,192,512]{2,1,0:T(8,128)}, f32[4,192,512]{2,1,0:T(8,128)}, u32[]{:S(2)}, u32[]{:S(2)}) collective-permute-start(f32[4,192,512]{2,1,0:T(8,128)} %get-tuple-element.74), channel_id=1, source_target_pairs={{0,32},{1,33},{2,34},{3,35},{4,36},{5,37},{6,38},{7,39},{8,40},{9,... | collective-permute-start | bytes 4718600 | tf_op jit(solution)/shard_map/ppermute | solution.py:423
  50.2 5.4 %copy-start.23 = (f32[4,192,512]{2,1,0:T(8,128)}, f32[4,192,512]{2,1,0:T(8,128)S(1)}, u32[]{:S(2)}) copy-start(f32[4,192,512]{2,1,0:T(8,128)S(1)} %collective-permute-done.1.refs_2_) | copy-start | bytes 4718596
  50.2 36.3 %collective-permute-start.7 = (f32[4,192,512]{2,1,0:T(8,128)}, f32[4,192,512]{2,1,0:T(8,128)}, u32[]{:S(2)}, u32[]{:S(2)}) collective-permute-start(f32[4,192,512]{2,1,0:T(8,128)} %get-tuple-element.75), channel_id=1, source_target_pairs={{0,96},{1,97},{2,98},{3,99},{4,100},{5,101},{6,102},{7,103},{8,104... | collective-permute-start | bytes 4718600 | tf_op jit(solution)/shard_map/ppermute | solution.py:423
  52.9 36.0 %collective-permute-start.4 = (f32[4,192,512]{2,1,0:T(8,128)}, f32[4,192,512]{2,1,0:T(8,128)}, u32[]{:S(2)}, u32[]{:S(2)}) collective-permute-start(f32[4,192,512]{2,1,0:T(8,128)} %get-tuple-element.70), channel_id=1, source_target_pairs={{0,4},{1,5},{2,6},{3,7},{4,8},{5,9},{6,10},{7,11},{8,12},{9,13},{1... | collective-permute-start | bytes 4718600 | tf_op jit(solution)/shard_map/ppermute | solution.py:423
  54.0 34.9 %collective-permute-start.5 = (f32[4,192,512]{2,1,0:T(8,128)}, f32[4,192,512]{2,1,0:T(8,128)}, u32[]{:S(2)}, u32[]{:S(2)}) collective-permute-start(f32[4,192,512]{2,1,0:T(8,128)} %get-tuple-element.71), channel_id=1, source_target_pairs={{0,12},{1,13},{2,14},{3,15},{4,0},{5,1},{6,2},{7,3},{8,4},{9,5},{1... | collective-permute-start | bytes 4718600 | tf_op jit(solution)/shard_map/ppermute | solution.py:423
  55.7 8.2 %slice-start.1 = ((s8[6291456]{0:T(1024)(128)(4,1)}), s8[2097152]{0:T(1024)(128)(4,1)S(1)}, s32[]{:S(2)}) async-start(s8[6291456]{0:T(1024)(128)(4,1)} %bitcast.29), calls=%async_computation.1 | async-start | bytes 4194304
  55.7 8.2 %copy-start.17 = (s32[3]{0:T(128)S(1)}, s32[3]{0:T(128)}, u32[]{:S(2)}) copy-start(s32[3]{0:T(128)} %pad_add_fusion.where) | copy-start | bytes 40
  55.7 8.2 %copy-start.19 = (s32[32]{0:T(128)S(1)}, s32[32]{0:T(128)}, u32[]{:S(2)}) copy-start(s32[32]{0:T(128)} %table.43) | copy-start | bytes 388
  63.9 3.4 %copy-start.2 = (f32[8,512,512]{2,1,0:T(8,128)S(1)}, f32[8,512,512]{2,1,0:T(8,128)}, u32[]{:S(2)}) copy-start(f32[8,512,512]{2,1,0:T(8,128)} %refs_2_.14) | copy-start | bytes 25165828
  67.2 1.4 copy-start.11
  68.7 4.8 %copy-start.9 = (f32[4,512,512]{2,1,0:T(8,128)S(1)}, f32[4,512,512]{2,1,0:T(8,128)}, u32[]{:S(2)}) copy-start(f32[4,512,512]{2,1,0:T(8,128)} %refs_2_.15) | copy-start | bytes 12582916
  73.5 3.4 %copy-start.3 = (f32[8,512,512]{2,1,0:T(8,128)S(1)}, f32[8,512,512]{2,1,0:T(8,128)}, u32[]{:S(2)}) copy-start(f32[8,512,512]{2,1,0:T(8,128)} %refs_2_.14) | copy-start | bytes 25165828
  77.7 0.8 copy-start.13
  78.5 0.8 copy-start.15
  86.5 37.3 %collective-permute-start.10 = (f32[4,192,512]{2,1,0:T(8,128)}, f32[4,192,512]{2,1,0:T(8,128)}, u32[]{:S(2)}, u32[]{:S(2)}) collective-permute-start(f32[4,192,512]{2,1,0:T(8,128)} %get-tuple-element.77.refs_4_), channel_id=1, source_target_pairs={{0,96},{1,97},{2,98},{3,99},{4,100},{5,101},{6,102},{7,103},{8,104... | collective-permute-start | bytes 4718600 | tf_op jit(solution)/shard_map/ppermute | solution.py:423
  88.9 15.7 %slice-start.2 = ((s8[6291456]{0:T(1024)(128)(4,1)}), s8[2097152]{0:T(1024)(128)(4,1)S(1)}, s32[]{:S(2)}) async-start(s8[6291456]{0:T(1024)(128)(4,1)} %bitcast.31), calls=%async_computation.2 | async-start | bytes 4194304
  88.9 34.9 %collective-permute-start.11 = (f32[4,192,512]{2,1,0:T(8,128)}, f32[4,192,512]{2,1,0:T(8,128)}, u32[]{:S(2)}, u32[]{:S(2)}) collective-permute-start(f32[4,192,512]{2,1,0:T(8,128)} %get-tuple-element.84), channel_id=1, source_target_pairs={{0,4},{1,5},{2,6},{3,7},{4,8},{5,9},{6,10},{7,11},{8,12},{9,13},{1... | collective-permute-start | bytes 4718600 | tf_op jit(solution)/shard_map/ppermute | solution.py:423
  89.9 34.0 %collective-permute-start.12 = (f32[4,192,512]{2,1,0:T(8,128)}, f32[4,192,512]{2,1,0:T(8,128)}, u32[]{:S(2)}, u32[]{:S(2)}) collective-permute-start(f32[4,192,512]{2,1,0:T(8,128)} %get-tuple-element.78.refs_0_), channel_id=1, source_target_pairs={{0,12},{1,13},{2,14},{3,15},{4,0},{5,1},{6,2},{7,3},{8,4},{9,5},{1... | collective-permute-start | bytes 4718600 | tf_op jit(solution)/shard_map/ppermute | solution.py:423
  91.7 13.0 %slice-start.3 = ((s8[6291456]{0:T(1024)(128)(4,1)}), s8[4194304]{0:T(1024)(128)(4,1)S(1)}, s32[]{:S(2)}) async-start(s8[6291456]{0:T(1024)(128)(4,1)} %bitcast.31), calls=%async_computation.3 | async-start | bytes 8388608
  91.7 13.0 %copy-start.18 = (s32[3]{0:T(128)S(1)}, s32[3]{0:T(128)}, u32[]{:S(2)}) copy-start(s32[3]{0:T(128)} %pad_add_fusion.where) | copy-start | bytes 40
  91.7 13.0 %copy-start.20 = (s32[32]{0:T(128)S(1)}, s32[32]{0:T(128)}, u32[]{:S(2)}) copy-start(s32[32]{0:T(128)} %table.43) | copy-start | bytes 388
  91.7 34.2 %collective-permute-start.8 = (f32[4,192,512]{2,1,0:T(8,128)}, f32[4,192,512]{2,1,0:T(8,128)}, u32[]{:S(2)}, u32[]{:S(2)}) collective-permute-start(f32[4,192,512]{2,1,0:T(8,128)} %get-tuple-element.81), channel_id=1, source_target_pairs={{0,32},{1,33},{2,34},{3,35},{4,36},{5,37},{6,38},{7,39},{8,40},{9,... | collective-permute-start | bytes 4718600 | tf_op jit(solution)/shard_map/ppermute | solution.py:423
  104.7 2.2 copy-start
  106.9 3.4 %copy-start.4 = (f32[8,512,512]{2,1,0:T(8,128)S(1)}, f32[8,512,512]{2,1,0:T(8,128)}, u32[]{:S(2)}) copy-start(f32[8,512,512]{2,1,0:T(8,128)} %refs_2_.14) | copy-start | bytes 25165828
  110.3 4.8 %copy-start.10 = (f32[4,512,512]{2,1,0:T(8,128)S(1)}, f32[4,512,512]{2,1,0:T(8,128)}, u32[]{:S(2)}) copy-start(f32[4,512,512]{2,1,0:T(8,128)} %refs_2_.15) | copy-start | bytes 12582916
  110.3 4.8 %copy-start.12 = (bf16[768,2048]{1,0:T(8,128)(2,1)S(1)}, bf16[768,2048]{1,0:T(8,128)(2,1)}, u32[]{:S(2)}) copy-start(bf16[768,2048]{1,0:T(8,128)(2,1)} %refs_1_.9) | copy-start | bytes 9437188
  115.1 10.8 %copy-start.5 = (f32[4,192,512]{2,1,0:T(8,128)S(1)}, f32[4,192,512]{2,1,0:T(8,128)}, u32[]{:S(2)}) copy-start(f32[4,192,512]{2,1,0:T(8,128)} %get-tuple-element.83.refs_20_.refs_32_.refs_4_.refs_12_) | copy-start | bytes 4718596
  115.1 10.8 %copy-start.6 = (f32[4,192,512]{2,1,0:T(8,128)S(1)}, f32[4,192,512]{2,1,0:T(8,128)}, u32[]{:S(2)}) copy-start(f32[4,192,512]{2,1,0:T(8,128)} %get-tuple-element.85.refs_24_.refs_28_.refs_8_.refs_16_) | copy-start | bytes 4718596
  115.1 10.8 %copy-start.7 = (f32[4,192,512]{2,1,0:T(8,128)S(1)}, f32[4,192,512]{2,1,0:T(8,128)}, u32[]{:S(2)}) copy-start(f32[4,192,512]{2,1,0:T(8,128)} %get-tuple-element.80.refs_4_.refs_16_.refs_12_) | copy-start | bytes 4718596
  115.1 10.8 %copy-start.8 = (f32[4,192,512]{2,1,0:T(8,128)S(1)}, f32[4,192,512]{2,1,0:T(8,128)}, u32[]{:S(2)}) copy-start(f32[4,192,512]{2,1,0:T(8,128)} %get-tuple-element.82.refs_8_.refs_12_.refs_16_) | copy-start | bytes 4718596
  126.0 10.8 %copy-start.1 = (f32[16,128,512]{2,1,0:T(8,128)S(1)}, f32[16,128,512]{2,1,0:T(8,128)}, u32[]{:S(2)}) copy-start(f32[16,128,512]{2,1,0:T(8,128)} %get-tuple-element.79.refs_0_) | copy-start | bytes 12582916
  131.4 28.8 %collective-permute-start.13 = (f32[2,336,512]{2,1,0:T(8,128)S(1)}, f32[2,336,512]{2,1,0:T(8,128)S(1)}, u32[]{:S(2)}, u32[]{:S(2)}) collective-permute-start(f32[2,336,512]{2,1,0:T(8,128)S(1)} %get-tuple-element.89), channel_id=1, source_target_pairs={{0,4},{1,5},{2,6},{3,7},{4,8},{5,9},{6,10},{7,11},{8,12},{9,13},{1... | collective-permute-start | bytes 4128776 | tf_op jit(solution)/shard_map/ppermute | solution.py:423
  131.4 29.4 %collective-permute-start.14 = (f32[2,336,512]{2,1,0:T(8,128)S(1)}, f32[2,336,512]{2,1,0:T(8,128)S(1)}, u32[]{:S(2)}, u32[]{:S(2)}) collective-permute-start(f32[2,336,512]{2,1,0:T(8,128)S(1)} %get-tuple-element.91), channel_id=1, source_target_pairs={{0,12},{1,13},{2,14},{3,15},{4,0},{5,1},{6,2},{7,3},{8,4},{9,5},{1... | collective-permute-start | bytes 4128776 | tf_op jit(solution)/shard_map/ppermute | solution.py:423
  134.1 29.2 %collective-permute-start.15 = (f32[2,320,512]{2,1,0:T(8,128)}, f32[2,320,512]{2,1,0:T(8,128)S(1)}, u32[]{:S(2)}, u32[]{:S(2)}) collective-permute-start(f32[2,320,512]{2,1,0:T(8,128)} %get-tuple-element.93), channel_id=1, source_target_pairs={{0,32},{1,33},{2,34},{3,35},{4,36},{5,37},{6,38},{7,39},{8,40},{9,... | collective-permute-start | bytes 3932168 | tf_op jit(solution)/shard_map/ppermute | solution.py:423
  134.1 29.8 %collective-permute-start.16 = (f32[2,320,512]{2,1,0:T(8,128)S(1)}, f32[2,320,512]{2,1,0:T(8,128)S(1)}, u32[]{:S(2)}, u32[]{:S(2)}) collective-permute-start(f32[2,320,512]{2,1,0:T(8,128)S(1)} %get-tuple-element.86.refs_0_), channel_id=1, source_target_pairs={{0,96},{1,97},{2,98},{3,99},{4,100},{5,101},{6,102},{7,103},{8,104... | collective-permute-start | bytes 3932168 | tf_op jit(solution)/shard_map/ppermute | solution.py:423
  161.5 12.0 %collective-permute-start.18 = (f32[336,512]{1,0:T(8,128)S(1)}, f32[336,512]{1,0:T(8,128)S(1)}, u32[]{:S(2)}, u32[]{:S(2)}) collective-permute-start(f32[336,512]{1,0:T(8,128)S(1)} %shard_map.70.refs_0_), channel_id=1, source_target_pairs={{0,12},{1,13},{2,14},{3,15},{4,0},{5,1},{6,2},{7,3},{8,4},{9,5},{1... | collective-permute-start | bytes 2064392 | tf_op jit(solution)/shard_map/ppermute | solution.py:423
  163.3 12.3 %collective-permute-start.17 = (f32[336,512]{1,0:T(8,128)S(1)}, f32[336,512]{1,0:T(8,128)S(1)}, u32[]{:S(2)}, u32[]{:S(2)}) collective-permute-start(f32[336,512]{1,0:T(8,128)S(1)} %shard_map.69.refs_0_), channel_id=1, source_target_pairs={{0,4},{1,5},{2,6},{3,7},{4,8},{5,9},{6,10},{7,11},{8,12},{9,13},{1... | collective-permute-start | bytes 2064392 | tf_op jit(solution)/shard_map/ppermute | solution.py:423
  164.5 16.8 %collective-permute-start.22 = (f32[320,512]{1,0:T(8,128)S(1)}, f32[320,512]{1,0:T(8,128)S(1)}, u32[]{:S(2)}, u32[]{:S(2)}) collective-permute-start(f32[320,512]{1,0:T(8,128)S(1)} %shard_map.72.refs_0_), channel_id=1, source_target_pairs={{0,96},{1,97},{2,98},{3,99},{4,100},{5,101},{6,102},{7,103},{8,104... | collective-permute-start | bytes 1966088 | tf_op jit(solution)/shard_map/ppermute | solution.py:423
  164.6 16.7 %collective-permute-start.21 = (f32[320,512]{1,0:T(8,128)S(1)}, f32[320,512]{1,0:T(8,128)S(1)}, u32[]{:S(2)}, u32[]{:S(2)}) collective-permute-start(f32[320,512]{1,0:T(8,128)S(1)} %shard_map.71.refs_0_), channel_id=1, source_target_pairs={{0,32},{1,33},{2,34},{3,35},{4,36},{5,37},{6,38},{7,39},{8,40},{9,... | collective-permute-start | bytes 1966088 | tf_op jit(solution)/shard_map/ppermute | solution.py:423
  176.5 7.2 %collective-permute-start.19 = (f32[72,512]{1,0:T(8,128)S(1)}, f32[72,512]{1,0:T(8,128)S(1)}, u32[]{:S(2)}, u32[]{:S(2)}) collective-permute-start(f32[72,512]{1,0:T(8,128)S(1)} %get-tuple-element.97), channel_id=1, source_target_pairs={{0,32},{1,33},{2,34},{3,35},{4,36},{5,37},{6,38},{7,39},{8,40},{9,... | collective-permute-start | bytes 442376 | tf_op jit(solution)/shard_map/ppermute | solution.py:423
  176.6 7.1 %collective-permute-start.20 = (f32[72,512]{1,0:T(8,128)S(1)}, f32[72,512]{1,0:T(8,128)S(1)}, u32[]{:S(2)}, u32[]{:S(2)}) collective-permute-start(f32[72,512]{1,0:T(8,128)S(1)} %get-tuple-element.96.refs_0_), channel_id=1, source_target_pairs={{0,96},{1,97},{2,98},{3,99},{4,100},{5,101},{6,102},{7,103},{8,104... | collective-permute-start | bytes 442376 | tf_op jit(solution)/shard_map/ppermute | solution.py:423
  179.3 9.3 %collective-permute-start.23 = (f32[192,512]{1,0:T(8,128)S(1)}, f32[192,512]{1,0:T(8,128)S(1)}, u32[]{:S(2)}, u32[]{:S(2)}) collective-permute-start(f32[192,512]{1,0:T(8,128)S(1)} %get-tuple-element.102), channel_id=1, source_target_pairs={{0,16},{1,17},{2,18},{3,19},{4,20},{5,21},{6,22},{7,23},{8,24},{9,... | collective-permute-start | bytes 1179656 | tf_op jit(solution)/shard_map/ppermute | solution.py:423
  184.6 11.6 %collective-permute-start.28 = (f32[192,512]{1,0:T(8,128)S(1)}, f32[192,512]{1,0:T(8,128)S(1)}, u32[]{:S(2)}, u32[]{:S(2)}) collective-permute-start(f32[192,512]{1,0:T(8,128)S(1)} %get-tuple-element.111), channel_id=1, source_target_pairs={{0,16},{1,17},{2,18},{3,19},{4,20},{5,21},{6,22},{7,23},{8,24},{9,... | collective-permute-start | bytes 1179656 | tf_op jit(solution)/shard_map/ppermute | solution.py:423
  186.7 5.5 %collective-permute-start.24 = (f32[72,512]{1,0:T(8,128)S(1)}, f32[72,512]{1,0:T(8,128)S(1)}, u32[]{:S(2)}, u32[]{:S(2)}) collective-permute-start(f32[72,512]{1,0:T(8,128)S(1)} %get-tuple-element.104), channel_id=1, source_target_pairs={{0,64},{1,65},{2,66},{3,67},{4,68},{5,69},{6,70},{7,71},{8,72},{9,... | collective-permute-start | bytes 442376 | tf_op jit(solution)/shard_map/ppermute | solution.py:423
  186.7 6.6 %collective-permute-start.25 = (f32[64,512]{1,0:T(8,128)S(1)}, f32[64,512]{1,0:T(8,128)S(1)}, u32[]{:S(2)}, u32[]{:S(2)}) collective-permute-start(f32[64,512]{1,0:T(8,128)S(1)} %get-tuple-element.107), channel_id=1, source_target_pairs={{0,4},{1,5},{2,6},{3,7},{4,8},{5,9},{6,10},{7,11},{8,12},{9,13},{1... | collective-permute-start | bytes 393224 | tf_op jit(solution)/shard_map/ppermute | solution.py:423
  186.7 6.6 %collective-permute-start.26 = (f32[64,512]{1,0:T(8,128)S(1)}, f32[64,512]{1,0:T(8,128)S(1)}, u32[]{:S(2)}, u32[]{:S(2)}) collective-permute-start(f32[64,512]{1,0:T(8,128)S(1)} %get-tuple-element.108), channel_id=1, source_target_pairs={{0,8},{1,9},{2,10},{3,11},{4,12},{5,13},{6,14},{7,15},{8,0},{9,1},... | collective-permute-start | bytes 393224 | tf_op jit(solution)/shard_map/ppermute | solution.py:423
  188.6 5.5 %collective-permute-start.27 = (f32[64,512]{1,0:T(8,128)S(1)}, f32[64,512]{1,0:T(8,128)S(1)}, u32[]{:S(2)}, u32[]{:S(2)}) collective-permute-start(f32[64,512]{1,0:T(8,128)S(1)} %get-tuple-element.98.refs_0_), channel_id=1, source_target_pairs={{0,12},{1,13},{2,14},{3,15},{4,0},{5,1},{6,2},{7,3},{8,4},{9,5},{1... | collective-permute-start | bytes 393224 | tf_op jit(solution)/shard_map/ppermute | solution.py:423
  190.4 5.8 %copy-start.14 = (bf16[512,512]{1,0:T(8,128)(2,1)S(1)}, bf16[512,512]{1,0:T(8,128)(2,1)}, u32[]{:S(2)}) copy-start(bf16[512,512]{1,0:T(8,128)(2,1)} %copy-done.13) | copy-start | bytes 1572868
  190.4 5.8 %copy-start.16 = (bf16[512,512]{1,0:T(8,128)(2,1)S(1)}, bf16[512,512]{1,0:T(8,128)(2,1)}, u32[]{:S(2)}) copy-start(bf16[512,512]{1,0:T(8,128)(2,1)} %copy-done.15) | copy-start | bytes 1572868
  192.8 3.4 %collective-permute-start.29 = (f32[8,512]{1,0:T(8,128)S(1)}, f32[8,512]{1,0:T(8,128)S(1)}, u32[]{:S(2)}, u32[]{:S(2)}) collective-permute-start(f32[8,512]{1,0:T(8,128)S(1)} %get-tuple-element.105.refs_0_.refs_5_), channel_id=1, source_target_pairs={{0,16},{1,17},{2,18},{3,19},{4,20},{5,21},{6,22},{7,23},{8,24},{9,... | collective-permute-start | bytes 49160 | tf_op jit(solution)/shard_map/ppermute | solution.py:423
  200.0 15.5 %collective-permute-start.30 = (f32[512,512]{1,0:T(8,128)S(1)}, f32[512,512]{1,0:T(8,128)S(1)}, u32[]{:S(2)}, u32[]{:S(2)}) collective-permute-start(f32[512,512]{1,0:T(8,128)S(1)} %shard_map.78), channel_id=1, source_target_pairs={{0,16},{1,17},{2,18},{3,19},{4,20},{5,21},{6,22},{7,23},{8,24},{9,... | collective-permute-start | bytes 3145736 | tf_op jit(solution)/shard_map/ppermute | solution.py:423
  200.3 25.6 %collective-permute-start.31 = (f32[512,512]{1,0:T(8,128)S(1)}, f32[512,512]{1,0:T(8,128)S(1)}, u32[]{:S(2)}, u32[]{:S(2)}) collective-permute-start(f32[512,512]{1,0:T(8,128)S(1)} %shard_map.78), channel_id=1, source_target_pairs={{0,18},{1,19},{2,16},{3,17},{4,22},{5,23},{6,20},{7,21},{8,26},{9,... | collective-permute-start | bytes 3145736 | tf_op jit(solution)/shard_map/ppermute | solution.py:423
  215.5 12.8 %collective-permute-start.32 = (f32[512,512]{1,0:T(8,128)S(1)}, f32[512,512]{1,0:T(8,128)S(1)}, u32[]{:S(2)}, u32[]{:S(2)}) collective-permute-start(f32[512,512]{1,0:T(8,128)S(1)} %collective-permute-done.30), channel_id=1, source_target_pairs={{0,1},{1,0},{2,3},{3,2},{4,5},{5,4},{6,7},{7,6},{8,9},{9,8},{10,11... | collective-permute-start | bytes 3145736 | tf_op jit(solution)/shard_map/ppermute | solution.py:423
  225.8 4.2 %collective-permute-start.33 = (f32[512,512]{1,0:T(8,128)S(1)}, f32[512,512]{1,0:T(8,128)}, u32[]{:S(2)}, u32[]{:S(2)}) collective-permute-start(f32[512,512]{1,0:T(8,128)S(1)} %collective-permute-done.31), channel_id=1, source_target_pairs={{0,1},{1,0},{2,3},{3,2},{4,5},{5,4},{6,7},{7,6},{8,9},{9,8},{10,11... | collective-permute-start | bytes 3145736 | tf_op jit(solution)/shard_map/ppermute | solution.py:423
  228.4 2.0 copy-start.21

commit v5 on v4

--- a/solution.py
+++ b/solution.py
@@ -446,8 +446,8 @@
         for n, stream in ((0, "x"), (2, "y"))
     }
     rest = (halves, got_c, terms_c, sums)
-    messages = turn(order, "xy", MESSAGES, *rest)
-    msgs_x, msgs_y = both(*messages[:2], "y"), both(*messages[2:], "x")
+    msgs_x = both(*turn(order, "x", MESSAGES, *rest), "y")
+    msgs_y = both(*turn(order, "y", MESSAGES, *rest), "x")
     *parts_x, mine_x = turn(order, "x", TERMS, *rest)
     *parts_y, mine_y = turn(order, "y", TERMS, *rest)
 

time: 233 us -> 229 us (0.983)
  waiting for transfers between devices: 70.3 us -> 65.4 us
    ppermute x34, waiting for transfers between devices: 70.3 us -> 65.4 us  [on_device(): send = lambda value, pairs: lax.ppermute(value, AXES, pairs)]
    pallas_call x22 -> x23, Pallas kernels: 89.3 us -> 90 us  [__call__(): pl.pallas_call(inner, out_shape=shapes, grid_spec=pltpu.PrefetchScalarGri...]
  transfers between devices with their start and end apart: 34 -> 34, of which waited for: 13 -> 15; matrix products, arithmetic and copies ran while one was open for 0% -> 0% of each run, Pallas kernels for 30% -> 33%
where the time goes in v5:
time: 229 us; the launch traced here: 228 us
  Pallas kernels  90 us (39%)
  waiting for transfers between devices  65.4 us (29%)
  starting transfers between devices  53.1 us (23%)
  local copies, waits for them, and re-layouts  18.8 us (8%)
    pallas_call x23, Pallas kernels, __call__(): pl.pallas_call(inner, out_shape=shapes, grid_spec=pltpu.PrefetchScalarGri...  90 us
    ppermute x34, waiting for transfers between devices, on_device(): send = lambda value, pairs: lax.ppermute(value, AXES, pairs)  65.4 us
    ppermute x34, starting transfers between devices, on_device(): send = lambda value, pairs: lax.ppermute(value, AXES, pairs)  53.1 us
    unnamed x56, local copies, waits for them, and re-layouts  15.8 us
  transfers between devices with their start and end apart: 34, of which 15 were waited for; matrix products, arithmetic and copies ran while one was open for 0% of the time, Pallas kernels for 33%

profile of v5, /device:TPU:1, one launch (start us, length us, event | category | flops | bytes accessed | tf_op | source)
XLA Modules:
  0.0 228.4 jit_solution(12088717482880669708)
XLA Ops:
  0.0 0.6 pad_add_fusion.where
  0.6 11.7 %shard_map.55 = (bf16[2048,768]{1,0:T(8,128)(2,1)}, f32[4,192,512]{2,1,0:T(8,128)}, f32[4,192,512]{2,1,0:T(8,128)}, f32[4,192,512]{2,1,0:T(8,128)}, f32[4,192,512]{2,1,0:T(8,128)}) custom-call(s32[32]{0:T(128)} %table.45, s32[3]{0:T(128)} %pad_add_fusion.where, bf16[768,2048]{1,0:T(8,128)(2,1)} %refs_1_.9, bf16[768,4096]{1,0:T(8,128)(2,1)} %refs_1_.8, ...), custom_call_target="tpu_custom_call" | custom-call | bytes 3690000 | tf_op jit(solution)/shard_map/pallas_call | solution.py:118
  12.3 2.0 collective-permute-start
  14.4 1.3 collective-permute-start.1
  15.7 1.2 collective-permute-start.2
  16.9 1.6 collective-permute-start.3
  18.5 8.2 %shard_map.56.refs_0_ = f32[16,128,512]{2,1,0:T(8,128)} custom-call(s32[32]{0:T(128)} %table.45, s32[3]{0:T(128)} %pad_add_fusion.where, f32[4,192,512]{2,1,0:T(8,128)} %get-tuple-element.59.refs_0_, bf16[2048,768]{1,0:T(8,128)(2,1)} %get-tuple-element.60.refs_1_, bf16[768,4096]{1,0:T(8,128)(2,1)} %refs_1_.8), custom_call_target="tpu_custom_call" | custom-call | bytes 3690000 | tf_op jit(solution)/shard_map/pallas_call | solution.py:118
  26.8 1.6 collective-permute-start.9
  28.4 12.5 %shard_map.57 = (f32[4,192,512]{2,1,0:T(8,128)}, f32[4,192,512]{2,1,0:T(8,128)}, f32[4,192,512]{2,1,0:T(8,128)}, f32[4,192,512]{2,1,0:T(8,128)}, f32[4,192,512]{...) custom-call(s32[32]{0:T(128)} %table.45, s32[3]{0:T(128)} %pad_add_fusion.where, ...), custom_call_target="tpu_custom_call" | custom-call | bytes 3690000 | tf_op jit(solution)/shard_map/pallas_call | solution.py:118
  40.9 8.8 %collective-permute-done.refs_1_ = f32[4,192,512]{2,1,0:T(8,128)S(1)} collective-permute-done((f32[4,192,512]{2,1,0:T(8,128)}, f32[4,192,512]{2,1,0:T(8,128)S(1)}, u32[]{:S(2)}, u32[]{:S(2)}) %collective-permute-start) | collective-permute-done | bytes 1572896 | tf_op jit(solution)/shard_map/ppermute | solution.py:423
  50.0 2.3 %collective-permute-start.7 = (f32[4,192,512]{2,1,0:T(8,128)}, f32[4,192,512]{2,1,0:T(8,128)}, u32[]{:S(2)}, u32[]{:S(2)}) collective-permute-start(f32[4,192,512]{2,1,0:T(8,128)} %get-tuple-element.75), channel_id=1, source_target_pairs={{0,96},{1,97},{2,98},{3,99},{4,100},{5,101},{6,102},{7,103},{8,104... | collective-permute-start | bytes 4718600 | tf_op jit(solution)/shard_map/ppermute | solution.py:423
  52.3 1.3 collective-permute-start.4
  53.6 1.8 collective-permute-start.5
  55.4 8.1 %shard_map.58 = (f32[4,192,512]{2,1,0:T(8,128)}, f32[4,192,512]{2,1,0:T(8,128)}, f32[4,192,512]{2,1,0:T(8,128)}, f32[4,192,512]{2,1,0:T(8,128)}) custom-call(s32[32]{0:T(128)} %table.45, s32[3]{0:T(128)} %pad_add_fusion.where, f32[4,192,512]{2,1,0:T(8,128)} %get-tuple-element.61.refs_0_.refs_8_, f32[4,192,512]{2,1,0:T(8,128)} %copy-done.22, ...), custom_call_target="tpu_custom_call" | custom-call | bytes 3690000 | tf_op jit(solution)/shard_map/pallas_call | solution.py:118
  63.6 3.4 %copy-done.2 = f32[8,512,512]{2,1,0:T(8,128)S(1)} copy-done((f32[8,512,512]{2,1,0:T(8,128)S(1)}, f32[8,512,512]{2,1,0:T(8,128)}, u32[]{:S(2)}) %copy-start.2) | copy-done | bytes 8388632
  67.0 1.4 copy-done.11
  68.4 4.8 %shard_map.59.refs_0_.refs_1_ = f32[4,1,512]{2,1,0:T(1,128)S(1)} custom-call(s32[32]{0:T(128)S(1)} %copy-done.19, s32[3]{0:T(128)S(1)} %copy-done.17, f32[4,192,512]{2,1,0:T(8,128)S(1)} %copy-done.11, bf16[768,4096]{1,0:T(8,128)(2,1)S(1)} %bitcast.30, f32[8,512,512]{2,1,0:T(8,128)S(1)} %copy-done.2), custom_call_target="tpu_custom_call" | custom-call | bytes 3690000 | tf_op jit(solution)/shard_map/pallas_call | solution.py:118
  73.2 3.4 %copy-done.3 = f32[8,512,512]{2,1,0:T(8,128)S(1)} copy-done((f32[8,512,512]{2,1,0:T(8,128)S(1)}, f32[8,512,512]{2,1,0:T(8,128)}, u32[]{:S(2)}) %copy-start.3) | copy-done | bytes 8388632
  76.6 0.8 shard_map.60
  77.5 0.8 copy-done.13
  78.3 0.8 copy-done.15
  79.1 6.4 %collective-permute-done.6.refs_2_.refs_4_ = f32[4,192,512]{2,1,0:T(8,128)} collective-permute-done((f32[4,192,512]{2,1,0:T(8,128)}, f32[4,192,512]{2,1,0:T(8,128)}, u32[]{:S(2)}, u32[]{:S(2)}) %collective-permute-start.6) | collective-permute-done | bytes 1572896 | tf_op jit(solution)/shard_map/ppermute | solution.py:423
  85.5 2.4 %collective-permute-start.10 = (f32[4,192,512]{2,1,0:T(8,128)}, f32[4,192,512]{2,1,0:T(8,128)}, u32[]{:S(2)}, u32[]{:S(2)}) collective-permute-start(f32[4,192,512]{2,1,0:T(8,128)} %get-tuple-element.77.refs_4_), channel_id=1, source_target_pairs={{0,96},{1,97},{2,98},{3,99},{4,100},{5,101},{6,102},{7,103},{8,104... | collective-permute-start | bytes 4718600 | tf_op jit(solution)/shard_map/ppermute | solution.py:423
  88.2 1.0 collective-permute-start.11
  89.3 2.1 collective-permute-start.12
  91.4 12.5 %shard_map.63 = (f32[4,192,512]{2,1,0:T(8,128)}, f32[4,192,512]{2,1,0:T(8,128)}, f32[4,192,512]{2,1,0:T(8,128)}, f32[4,192,512]{2,1,0:T(8,128)}, f32[16,128,512]{2,1,0:T(8,128)}) custom-call(s32[32]{0:T(128)} %table.45, s32[3]{0:T(128)} %pad_add_fusion.where, f32[4,192,512]{2,1,0:T(8,128)} %get-tuple-element.78.refs_0_, ...), custom_call_target="tpu_custom_call" | custom-call | bytes 3690000 | tf_op jit(solution)/shard_map/pallas_call | solution.py:118
  103.9 2.2 copy-done
  106.1 3.4 %copy-done.4 = f32[8,512,512]{2,1,0:T(8,128)S(1)} copy-done((f32[8,512,512]{2,1,0:T(8,128)S(1)}, f32[8,512,512]{2,1,0:T(8,128)}, u32[]{:S(2)}) %copy-start.4) | copy-done | bytes 8388632
  109.5 4.8 %shard_map.64.refs_0_.refs_2_ = f32[4,1,512]{2,1,0:T(1,128)S(1)} custom-call(s32[32]{0:T(128)S(1)} %copy-done.20, s32[3]{0:T(128)S(1)} %copy-done.18, f32[16,128,512]{2,1,0:T(8,128)S(1)} %copy-done, bf16[768,4096]{1,0:T(8,128)(2,1)S(1)} %bitcast.32, f32[8,512,512]{2,1,0:T(8,128)S(1)} %copy-done.4), custom_call_target="tpu_custom_call" | custom-call | bytes 3690000 | tf_op jit(solution)/shard_map/pallas_call | solution.py:118
  114.3 4.8 %shard_map.65.refs_0_.refs_3_ = f32[4,1,512]{2,1,0:T(1,128)S(1)} custom-call(s32[32]{0:T(128)S(1)} %copy-done.20, s32[3]{0:T(128)S(1)} %copy-done.18, f32[4,1,512]{2,1,0:T(1,128)S(1)} %shard_map.64.refs_0_.refs_2_, bf16[768,2048]{1,0:T(8,128)(2,1)S(1)} %copy-done.12, f32[4,512,512]{2,1,0:T(8,128)S(1)} %copy-done.10), custom_call_target="tpu_custom_call" | custom-call | bytes 3690000 | tf_op jit(solution)/shard_map/pallas_call | solution.py:118
  119.2 3.0 %collective-permute-done.8.refs_5_.refs_17_.refs_13_ = f32[4,192,512]{2,1,0:T(8,128)} collective-permute-done((f32[4,192,512]{2,1,0:T(8,128)}, f32[4,192,512]{2,1,0:T(8,128)}, u32[]{:S(2)}, u32[]{:S(2)}) %collective-permute-start.8) | collective-permute-done | bytes 1572896 | tf_op jit(solution)/shard_map/ppermute | solution.py:423
  122.3 3.8 %shard_map.66 = (f32[2,336,512]{2,1,0:T(8,128)}, f32[2,336,512]{2,1,0:T(8,128)S(1)}) custom-call(s32[32]{0:T(128)S(1)} %copy-done.20, s32[3]{0:T(128)S(1)} %copy-done.18, f32[4,1,512]{2,1,0:T(1,128)S(1)} %shard_map.65.refs_0_.refs_3_, f32[4,1,512]{2,1,0:T(1,128)S(1)} %shard_map.59.refs_0_.refs_1_, f32[4,1,512]{2,1,0:T(1,128)S(1)} %shard_map.64.refs_0_.refs_2_, ...), custom_call_target="tpu_custom_call" | custom-call | bytes 3690000 | tf_op jit(solution)/shard_map/pallas_call | solution.py:118
  126.1 1.3 collective-permute-start.13
  127.4 1.9 collective-permute-start.14
  129.3 2.5 %shard_map.67 = (f32[2,320,512]{2,1,0:T(8,128)S(1)}, f32[2,320,512]{2,1,0:T(8,128)S(1)}) custom-call(s32[32]{0:T(128)S(1)} %copy-done.20, s32[3]{0:T(128)S(1)} %copy-done.18, f32[2,336,512]{2,1,0:T(8,128)S(1)} %get-tuple-element.83.refs_0_, f32[4,1,512]{2,1,0:T(1,128)S(1)} %shard_map.59.refs_0_.refs_1_, f32[4,1,512]{2,1,0:T(1,128)S(1)} %shard_map.64.refs_0_.refs_2_, ...), custom_call_target="tpu_custom_call" | custom-call | bytes 3690000 | tf_op jit(solution)/shard_map/pallas_call | solution.py:118
  131.9 2.7 %collective-permute-start.16 = (f32[2,320,512]{2,1,0:T(8,128)S(1)}, f32[2,320,512]{2,1,0:T(8,128)S(1)}, u32[]{:S(2)}, u32[]{:S(2)}) collective-permute-start(f32[2,320,512]{2,1,0:T(8,128)S(1)} %get-tuple-element.87.refs_0_), channel_id=1, source_target_pairs={{0,96},{1,97},{2,98},{3,99},{4,100},{5,101},{6,102},{7,103},{8,104... | collective-permute-start | bytes 3932168 | tf_op jit(solution)/shard_map/ppermute | solution.py:423
  134.6 2.5 %shard_map.68 = (f32[336,512]{1,0:T(8,128)S(1)}, f32[336,512]{1,0:T(8,128)S(1)}, f32[2,336,512]{2,1,0:T(8,128)S(1)}) custom-call(s32[32]{0:T(128)S(1)} %copy-done.20, s32[3]{0:T(128)S(1)} %copy-done.18, f32[2,320,512]{2,1,0:T(8,128)S(1)} %get-tuple-element.87.refs_0_, f32[4,1,512]{2,1,0:T(1,128)S(1)} %shard_map.59.refs_0_.refs_1_, ...), custom_call_target="tpu_custom_call" | custom-call | bytes 3690000 | tf_op jit(solution)/shard_map/pallas_call | solution.py:118
  137.1 2.5 %shard_map.69 = (f32[320,512]{1,0:T(8,128)S(1)}, f32[320,512]{1,0:T(8,128)S(1)}, f32[2,320,512]{2,1,0:T(8,128)S(1)}) custom-call(s32[32]{0:T(128)S(1)} %copy-done.20, s32[3]{0:T(128)S(1)} %copy-done.18, f32[2,336,512]{2,1,0:T(8,128)S(1)} %get-tuple-element.88.refs_0_.refs_1_, f32[4,1,512]{2,1,0:T(1,128)S(1)} %shard_map.59.refs_0_.refs_1_, ...), custom_call_target="tpu_custom_call" | custom-call | bytes 3690000 | tf_op jit(solution)/shard_map/pallas_call | solution.py:118
  139.6 16.6 %collective-permute-done.13.refs_1_.refs_2_ = f32[2,336,512]{2,1,0:T(8,128)S(1)} collective-permute-done((f32[2,336,512]{2,1,0:T(8,128)}, f32[2,336,512]{2,1,0:T(8,128)S(1)}, u32[]{:S(2)}, u32[]{:S(2)}) %collective-permute-start.13) | collective-permute-done | bytes 1376288 | tf_op jit(solution)/shard_map/ppermute | solution.py:423
  157.4 1.6 collective-permute-start.18
  160.5 1.8 collective-permute-start.22
  162.4 7.6 %collective-permute-done.18.refs_5_ = f32[336,512]{1,0:T(8,128)S(1)} collective-permute-done((f32[336,512]{1,0:T(8,128)S(1)}, f32[336,512]{1,0:T(8,128)S(1)}, u32[]{:S(2)}, u32[]{:S(2)}) %collective-permute-start.18) | collective-permute-done | bytes 688160 | tf_op jit(solution)/shard_map/ppermute | solution.py:423
  169.9 2.2 collective-permute-done.17.refs_4_
  172.1 0.9 shard_map.74
  173.1 2.7 %collective-permute-start.20 = (f32[72,512]{1,0:T(8,128)S(1)}, f32[72,512]{1,0:T(8,128)S(1)}, u32[]{:S(2)}, u32[]{:S(2)}) collective-permute-start(f32[72,512]{1,0:T(8,128)S(1)} %get-tuple-element.96.refs_0_), channel_id=1, source_target_pairs={{0,96},{1,97},{2,98},{3,99},{4,100},{5,101},{6,102},{7,103},{8,104... | collective-permute-start | bytes 442376 | tf_op jit(solution)/shard_map/ppermute | solution.py:423
  175.8 1.1 collective-permute-start.23
  176.9 3.4 %collective-permute-done.19.refs_1_.refs_2_ = f32[72,512]{1,0:T(8,128)S(1)} collective-permute-done((f32[72,512]{1,0:T(8,128)S(1)}, f32[72,512]{1,0:T(8,128)S(1)}, u32[]{:S(2)}, u32[]{:S(2)}) %collective-permute-start.19) | collective-permute-done | bytes 147488 | tf_op jit(solution)/shard_map/ppermute | solution.py:423
  180.2 0.8 shard_map.75
  181.1 1.2 collective-permute-start.28
  182.3 0.9 collective-permute-start.24
  183.2 1.8 collective-permute-start.26
  185.0 0.9 collective-permute-start.27
  185.9 1.0 shard_map.76.refs_0_.refs_1_
  186.9 0.8 collective-permute-done.24.refs_3_
  188.3 0.7 collective-permute-start.29
  189.6 0.9 collective-permute-done.27.refs_6_
  190.6 0.9 shard_map.78.refs_0_.refs_2_
  191.8 3.8 %shard_map.79 = f32[512,512]{1,0:T(8,128)S(1)} custom-call(s32[32]{0:T(128)S(1)} %copy-done.20, s32[3]{0:T(128)S(1)} %copy-done.18, f32[128,512]{1,0:T(8,128)S(1)} %shard_map.78.refs_0_.refs_2_, f32[192,512]{1,0:T(8,128)S(1)} %shard_map.76.refs_0_.refs_1_, f32[128,512]{1,0:T(8,128)S(1)} %shard_map.78.refs_0_.refs_2_, ...), custom_call_target="tpu_custom_call" | custom-call | bytes 3690000 | tf_op jit(solution)/shard_map/pallas_call | solution.py:118
  196.0 3.2 %collective-permute-start.31 = (f32[512,512]{1,0:T(8,128)S(1)}, f32[512,512]{1,0:T(8,128)S(1)}, u32[]{:S(2)}, u32[]{:S(2)}) collective-permute-start(f32[512,512]{1,0:T(8,128)S(1)} %shard_map.79), channel_id=1, source_target_pairs={{0,18},{1,19},{2,16},{3,17},{4,22},{5,23},{6,20},{7,21},{8,26},{9,... | collective-permute-start | bytes 3145736 | tf_op jit(solution)/shard_map/ppermute | solution.py:423
  199.2 12.5 %collective-permute-done.30 = f32[512,512]{1,0:T(8,128)S(1)} collective-permute-done((f32[512,512]{1,0:T(8,128)S(1)}, f32[512,512]{1,0:T(8,128)S(1)}, u32[]{:S(2)}, u32[]{:S(2)}) %collective-permute-start.30) | collective-permute-done | bytes 1048608 | tf_op jit(solution)/shard_map/ppermute | solution.py:423
  211.8 9.6 %collective-permute-start.32 = (f32[512,512]{1,0:T(8,128)S(1)}, f32[512,512]{1,0:T(8,128)S(1)}, u32[]{:S(2)}, u32[]{:S(2)}) collective-permute-start(f32[512,512]{1,0:T(8,128)S(1)} %collective-permute-done.30), channel_id=1, source_target_pairs={{0,1},{1,0},{2,3},{3,2},{4,5},{5,4},{6,7},{7,6},{8,9},{9,8},{10,11... | collective-permute-start | bytes 3145736 | tf_op jit(solution)/shard_map/ppermute | solution.py:423
  221.4 1.9 collective-permute-start.33
  224.1 1.6 collective-permute-done.33
  226.2 2.3 bitcast_dynamic-update-slice_fusion
  (93 shorter events, 6.7 us)
Async XLA Ops:
  12.3 37.3 %collective-permute-start = (f32[4,192,512]{2,1,0:T(8,128)}, f32[4,192,512]{2,1,0:T(8,128)S(1)}, u32[]{:S(2)}, u32[]{:S(2)}) collective-permute-start(f32[4,192,512]{2,1,0:T(8,128)} %get-tuple-element.62), channel_id=1, source_target_pairs={{0,32},{1,33},{2,34},{3,35},{4,36},{5,37},{6,38},{7,39},{8,40},{9,... | collective-permute-start | bytes 4718600 | tf_op jit(solution)/shard_map/ppermute | solution.py:423
  14.4 35.6 %collective-permute-start.1 = (f32[4,192,512]{2,1,0:T(8,128)}, f32[4,192,512]{2,1,0:T(8,128)S(1)}, u32[]{:S(2)}, u32[]{:S(2)}) collective-permute-start(f32[4,192,512]{2,1,0:T(8,128)} %get-tuple-element.63), channel_id=1, source_target_pairs={{0,96},{1,97},{2,98},{3,99},{4,100},{5,101},{6,102},{7,103},{8,104... | collective-permute-start | bytes 4718600 | tf_op jit(solution)/shard_map/ppermute | solution.py:423
  15.7 36.6 %collective-permute-start.2 = (f32[4,192,512]{2,1,0:T(8,128)}, f32[4,192,512]{2,1,0:T(8,128)}, u32[]{:S(2)}, u32[]{:S(2)}) collective-permute-start(f32[4,192,512]{2,1,0:T(8,128)} %get-tuple-element.64), channel_id=1, source_target_pairs={{0,4},{1,5},{2,6},{3,7},{4,8},{5,9},{6,10},{7,11},{8,12},{9,13},{1... | collective-permute-start | bytes 4718600 | tf_op jit(solution)/shard_map/ppermute | solution.py:423
  16.9 36.7 %collective-permute-start.3 = (f32[4,192,512]{2,1,0:T(8,128)}, f32[4,192,512]{2,1,0:T(8,128)}, u32[]{:S(2)}, u32[]{:S(2)}) collective-permute-start(f32[4,192,512]{2,1,0:T(8,128)} %get-tuple-element.59.refs_0_), channel_id=1, source_target_pairs={{0,12},{1,13},{2,14},{3,15},{4,0},{5,1},{6,2},{7,3},{8,4},{9,5},{1... | collective-permute-start | bytes 4718600 | tf_op jit(solution)/shard_map/ppermute | solution.py:423
  26.8 95.5 %collective-permute-start.9 = (f32[16,128,512]{2,1,0:T(8,128)}, f32[16,128,512]{2,1,0:T(8,128)}, u32[]{:S(2)}, u32[]{:S(2)}) collective-permute-start(f32[16,128,512]{2,1,0:T(8,128)} %shard_map.56.refs_0_), channel_id=1, source_target_pairs={{0,16},{1,17},{2,18},{3,19},{4,20},{5,21},{6,22},{7,23},{8,24},{9,... | collective-permute-start | bytes 12582920 | tf_op jit(solution)/shard_map/ppermute | solution.py:423
  28.4 35.2 %slice-start = ((s8[6291456]{0:T(1024)(128)(4,1)}), s8[4194304]{0:T(1024)(128)(4,1)S(1)}, s32[]{:S(2)}) async-start(s8[6291456]{0:T(1024)(128)(4,1)} %bitcast.29), calls=%async_computation | async-start | bytes 8388608
  49.6 5.8 %copy-start.22 = (f32[4,192,512]{2,1,0:T(8,128)}, f32[4,192,512]{2,1,0:T(8,128)S(1)}, u32[]{:S(2)}) copy-start(f32[4,192,512]{2,1,0:T(8,128)S(1)} %collective-permute-done.refs_1_) | copy-start | bytes 4718596
  49.6 35.8 %collective-permute-start.6 = (f32[4,192,512]{2,1,0:T(8,128)}, f32[4,192,512]{2,1,0:T(8,128)}, u32[]{:S(2)}, u32[]{:S(2)}) collective-permute-start(f32[4,192,512]{2,1,0:T(8,128)} %get-tuple-element.74), channel_id=1, source_target_pairs={{0,32},{1,33},{2,34},{3,35},{4,36},{5,37},{6,38},{7,39},{8,40},{9,... | collective-permute-start | bytes 4718600 | tf_op jit(solution)/shard_map/ppermute | solution.py:423
  50.0 5.4 %copy-start.23 = (f32[4,192,512]{2,1,0:T(8,128)}, f32[4,192,512]{2,1,0:T(8,128)S(1)}, u32[]{:S(2)}) copy-start(f32[4,192,512]{2,1,0:T(8,128)S(1)} %collective-permute-done.1.refs_2_) | copy-start | bytes 4718596
  50.0 35.5 %collective-permute-start.7 = (f32[4,192,512]{2,1,0:T(8,128)}, f32[4,192,512]{2,1,0:T(8,128)}, u32[]{:S(2)}, u32[]{:S(2)}) collective-permute-start(f32[4,192,512]{2,1,0:T(8,128)} %get-tuple-element.75), channel_id=1, source_target_pairs={{0,96},{1,97},{2,98},{3,99},{4,100},{5,101},{6,102},{7,103},{8,104... | collective-permute-start | bytes 4718600 | tf_op jit(solution)/shard_map/ppermute | solution.py:423
  52.3 35.9 %collective-permute-start.4 = (f32[4,192,512]{2,1,0:T(8,128)}, f32[4,192,512]{2,1,0:T(8,128)}, u32[]{:S(2)}, u32[]{:S(2)}) collective-permute-start(f32[4,192,512]{2,1,0:T(8,128)} %get-tuple-element.70), channel_id=1, source_target_pairs={{0,4},{1,5},{2,6},{3,7},{4,8},{5,9},{6,10},{7,11},{8,12},{9,13},{1... | collective-permute-start | bytes 4718600 | tf_op jit(solution)/shard_map/ppermute | solution.py:423
  53.6 34.6 %collective-permute-start.5 = (f32[4,192,512]{2,1,0:T(8,128)}, f32[4,192,512]{2,1,0:T(8,128)}, u32[]{:S(2)}, u32[]{:S(2)}) collective-permute-start(f32[4,192,512]{2,1,0:T(8,128)} %get-tuple-element.71), channel_id=1, source_target_pairs={{0,12},{1,13},{2,14},{3,15},{4,0},{5,1},{6,2},{7,3},{8,4},{9,5},{1... | collective-permute-start | bytes 4718600 | tf_op jit(solution)/shard_map/ppermute | solution.py:423
  55.4 8.2 %slice-start.1 = ((s8[6291456]{0:T(1024)(128)(4,1)}), s8[2097152]{0:T(1024)(128)(4,1)S(1)}, s32[]{:S(2)}) async-start(s8[6291456]{0:T(1024)(128)(4,1)} %bitcast.29), calls=%async_computation.1 | async-start | bytes 4194304
  55.4 8.2 %copy-start.17 = (s32[3]{0:T(128)S(1)}, s32[3]{0:T(128)}, u32[]{:S(2)}) copy-start(s32[3]{0:T(128)} %pad_add_fusion.where) | copy-start | bytes 40
  55.4 8.2 %copy-start.19 = (s32[32]{0:T(128)S(1)}, s32[32]{0:T(128)}, u32[]{:S(2)}) copy-start(s32[32]{0:T(128)} %table.45) | copy-start | bytes 388
  63.6 3.4 %copy-start.2 = (f32[8,512,512]{2,1,0:T(8,128)S(1)}, f32[8,512,512]{2,1,0:T(8,128)}, u32[]{:S(2)}) copy-start(f32[8,512,512]{2,1,0:T(8,128)} %refs_2_.14) | copy-start | bytes 25165828
  67.0 1.4 copy-start.11
  68.4 4.8 %copy-start.9 = (f32[4,512,512]{2,1,0:T(8,128)S(1)}, f32[4,512,512]{2,1,0:T(8,128)}, u32[]{:S(2)}) copy-start(f32[4,512,512]{2,1,0:T(8,128)} %refs_2_.15) | copy-start | bytes 12582916
  73.2 3.4 %copy-start.3 = (f32[8,512,512]{2,1,0:T(8,128)S(1)}, f32[8,512,512]{2,1,0:T(8,128)}, u32[]{:S(2)}) copy-start(f32[8,512,512]{2,1,0:T(8,128)} %refs_2_.14) | copy-start | bytes 25165828
  77.4 0.8 copy-start.13
  78.3 0.8 copy-start.15
  85.5 33.7 %collective-permute-start.10 = (f32[4,192,512]{2,1,0:T(8,128)}, f32[4,192,512]{2,1,0:T(8,128)}, u32[]{:S(2)}, u32[]{:S(2)}) collective-permute-start(f32[4,192,512]{2,1,0:T(8,128)} %get-tuple-element.77.refs_4_), channel_id=1, source_target_pairs={{0,96},{1,97},{2,98},{3,99},{4,100},{5,101},{6,102},{7,103},{8,104... | collective-permute-start | bytes 4718600 | tf_op jit(solution)/shard_map/ppermute | solution.py:423
  87.9 34.4 %collective-permute-start.8 = (f32[4,192,512]{2,1,0:T(8,128)}, f32[4,192,512]{2,1,0:T(8,128)}, u32[]{:S(2)}, u32[]{:S(2)}) collective-permute-start(f32[4,192,512]{2,1,0:T(8,128)} %get-tuple-element.81), channel_id=1, source_target_pairs={{0,32},{1,33},{2,34},{3,35},{4,36},{5,37},{6,38},{7,39},{8,40},{9,... | collective-permute-start | bytes 4718600 | tf_op jit(solution)/shard_map/ppermute | solution.py:423
  88.2 15.6 %slice-start.2 = ((s8[6291456]{0:T(1024)(128)(4,1)}), s8[2097152]{0:T(1024)(128)(4,1)S(1)}, s32[]{:S(2)}) async-start(s8[6291456]{0:T(1024)(128)(4,1)} %bitcast.31), calls=%async_computation.2 | async-start | bytes 4194304
  88.2 41.1 %collective-permute-start.11 = (f32[4,192,512]{2,1,0:T(8,128)}, f32[4,192,512]{2,1,0:T(8,128)}, u32[]{:S(2)}, u32[]{:S(2)}) collective-permute-start(f32[4,192,512]{2,1,0:T(8,128)} %get-tuple-element.85), channel_id=1, source_target_pairs={{0,4},{1,5},{2,6},{3,7},{4,8},{5,9},{6,10},{7,11},{8,12},{9,13},{1... | collective-permute-start | bytes 4718600 | tf_op jit(solution)/shard_map/ppermute | solution.py:423
  89.3 14.6 %slice-start.3 = ((s8[6291456]{0:T(1024)(128)(4,1)}), s8[4194304]{0:T(1024)(128)(4,1)S(1)}, s32[]{:S(2)}) async-start(s8[6291456]{0:T(1024)(128)(4,1)} %bitcast.31), calls=%async_computation.3 | async-start | bytes 8388608
  89.3 14.6 %copy-start.18 = (s32[3]{0:T(128)S(1)}, s32[3]{0:T(128)}, u32[]{:S(2)}) copy-start(s32[3]{0:T(128)} %pad_add_fusion.where) | copy-start | bytes 40
  89.3 14.6 %copy-start.20 = (s32[32]{0:T(128)S(1)}, s32[32]{0:T(128)}, u32[]{:S(2)}) copy-start(s32[32]{0:T(128)} %table.45) | copy-start | bytes 388
  89.3 40.0 %collective-permute-start.12 = (f32[4,192,512]{2,1,0:T(8,128)}, f32[4,192,512]{2,1,0:T(8,128)}, u32[]{:S(2)}, u32[]{:S(2)}) collective-permute-start(f32[4,192,512]{2,1,0:T(8,128)} %get-tuple-element.78.refs_0_), channel_id=1, source_target_pairs={{0,12},{1,13},{2,14},{3,15},{4,0},{5,1},{6,2},{7,3},{8,4},{9,5},{1... | collective-permute-start | bytes 4718600 | tf_op jit(solution)/shard_map/ppermute | solution.py:423
  103.9 2.2 copy-start
  106.1 3.4 %copy-start.4 = (f32[8,512,512]{2,1,0:T(8,128)S(1)}, f32[8,512,512]{2,1,0:T(8,128)}, u32[]{:S(2)}) copy-start(f32[8,512,512]{2,1,0:T(8,128)} %refs_2_.14) | copy-start | bytes 25165828
  109.5 4.8 %copy-start.10 = (f32[4,512,512]{2,1,0:T(8,128)S(1)}, f32[4,512,512]{2,1,0:T(8,128)}, u32[]{:S(2)}) copy-start(f32[4,512,512]{2,1,0:T(8,128)} %refs_2_.15) | copy-start | bytes 12582916
  109.5 4.8 %copy-start.12 = (bf16[768,2048]{1,0:T(8,128)(2,1)S(1)}, bf16[768,2048]{1,0:T(8,128)(2,1)}, u32[]{:S(2)}) copy-start(bf16[768,2048]{1,0:T(8,128)(2,1)} %refs_1_.9) | copy-start | bytes 9437188
  114.3 7.9 %copy-start.1 = (f32[16,128,512]{2,1,0:T(8,128)S(1)}, f32[16,128,512]{2,1,0:T(8,128)}, u32[]{:S(2)}) copy-start(f32[16,128,512]{2,1,0:T(8,128)} %get-tuple-element.79.refs_0_) | copy-start | bytes 12582916
  114.3 7.9 %copy-start.5 = (f32[4,192,512]{2,1,0:T(8,128)S(1)}, f32[4,192,512]{2,1,0:T(8,128)}, u32[]{:S(2)}) copy-start(f32[4,192,512]{2,1,0:T(8,128)} %get-tuple-element.80.refs_4_.refs_16_.refs_12_) | copy-start | bytes 4718596
  114.3 7.9 %copy-start.6 = (f32[4,192,512]{2,1,0:T(8,128)S(1)}, f32[4,192,512]{2,1,0:T(8,128)}, u32[]{:S(2)}) copy-start(f32[4,192,512]{2,1,0:T(8,128)} %get-tuple-element.82.refs_8_.refs_12_.refs_16_) | copy-start | bytes 4718596
  122.2 7.1 %copy-start.7 = (f32[4,192,512]{2,1,0:T(8,128)S(1)}, f32[4,192,512]{2,1,0:T(8,128)}, u32[]{:S(2)}) copy-start(f32[4,192,512]{2,1,0:T(8,128)} %get-tuple-element.84.refs_4_.refs_16_.refs_12_) | copy-start | bytes 4718596
  122.3 7.1 %copy-start.8 = (f32[4,192,512]{2,1,0:T(8,128)S(1)}, f32[4,192,512]{2,1,0:T(8,128)}, u32[]{:S(2)}) copy-start(f32[4,192,512]{2,1,0:T(8,128)} %get-tuple-element.86.refs_8_.refs_12_.refs_16_) | copy-start | bytes 4718596
  126.1 30.1 %collective-permute-start.13 = (f32[2,336,512]{2,1,0:T(8,128)}, f32[2,336,512]{2,1,0:T(8,128)S(1)}, u32[]{:S(2)}, u32[]{:S(2)}) collective-permute-start(f32[2,336,512]{2,1,0:T(8,128)} %get-tuple-element.90), channel_id=1, source_target_pairs={{0,4},{1,5},{2,6},{3,7},{4,8},{5,9},{6,10},{7,11},{8,12},{9,13},{1... | collective-permute-start | bytes 4128776 | tf_op jit(solution)/shard_map/ppermute | solution.py:423
  127.4 29.4 %collective-permute-start.14 = (f32[2,336,512]{2,1,0:T(8,128)S(1)}, f32[2,336,512]{2,1,0:T(8,128)S(1)}, u32[]{:S(2)}, u32[]{:S(2)}) collective-permute-start(f32[2,336,512]{2,1,0:T(8,128)S(1)} %get-tuple-element.83.refs_0_), channel_id=1, source_target_pairs={{0,12},{1,13},{2,14},{3,15},{4,0},{5,1},{6,2},{7,3},{8,4},{9,5},{1... | collective-permute-start | bytes 4128776 | tf_op jit(solution)/shard_map/ppermute | solution.py:423
  131.8 27.4 %collective-permute-start.15 = (f32[2,320,512]{2,1,0:T(8,128)S(1)}, f32[2,320,512]{2,1,0:T(8,128)S(1)}, u32[]{:S(2)}, u32[]{:S(2)}) collective-permute-start(f32[2,320,512]{2,1,0:T(8,128)S(1)} %get-tuple-element.93), channel_id=1, source_target_pairs={{0,32},{1,33},{2,34},{3,35},{4,36},{5,37},{6,38},{7,39},{8,40},{9,... | collective-permute-start | bytes 3932168 | tf_op jit(solution)/shard_map/ppermute | solution.py:423
  131.9 28.0 %collective-permute-start.16 = (f32[2,320,512]{2,1,0:T(8,128)S(1)}, f32[2,320,512]{2,1,0:T(8,128)S(1)}, u32[]{:S(2)}, u32[]{:S(2)}) collective-permute-start(f32[2,320,512]{2,1,0:T(8,128)S(1)} %get-tuple-element.87.refs_0_), channel_id=1, source_target_pairs={{0,96},{1,97},{2,98},{3,99},{4,100},{5,101},{6,102},{7,103},{8,104... | collective-permute-start | bytes 3932168 | tf_op jit(solution)/shard_map/ppermute | solution.py:423
  157.4 12.5 %collective-permute-start.18 = (f32[336,512]{1,0:T(8,128)S(1)}, f32[336,512]{1,0:T(8,128)S(1)}, u32[]{:S(2)}, u32[]{:S(2)}) collective-permute-start(f32[336,512]{1,0:T(8,128)S(1)} %shard_map.71.refs_0_), channel_id=1, source_target_pairs={{0,12},{1,13},{2,14},{3,15},{4,0},{5,1},{6,2},{7,3},{8,4},{9,5},{1... | collective-permute-start | bytes 2064392 | tf_op jit(solution)/shard_map/ppermute | solution.py:423
  159.1 13.1 %collective-permute-start.17 = (f32[336,512]{1,0:T(8,128)S(1)}, f32[336,512]{1,0:T(8,128)S(1)}, u32[]{:S(2)}, u32[]{:S(2)}) collective-permute-start(f32[336,512]{1,0:T(8,128)S(1)} %shard_map.70.refs_0_), channel_id=1, source_target_pairs={{0,4},{1,5},{2,6},{3,7},{4,8},{5,9},{6,10},{7,11},{8,12},{9,13},{1... | collective-permute-start | bytes 2064392 | tf_op jit(solution)/shard_map/ppermute | solution.py:423
  160.5 16.3 %collective-permute-start.22 = (f32[320,512]{1,0:T(8,128)S(1)}, f32[320,512]{1,0:T(8,128)S(1)}, u32[]{:S(2)}, u32[]{:S(2)}) collective-permute-start(f32[320,512]{1,0:T(8,128)S(1)} %shard_map.73.refs_0_), channel_id=1, source_target_pairs={{0,96},{1,97},{2,98},{3,99},{4,100},{5,101},{6,102},{7,103},{8,104... | collective-permute-start | bytes 1966088 | tf_op jit(solution)/shard_map/ppermute | solution.py:423
  162.4 14.5 %collective-permute-start.21 = (f32[320,512]{1,0:T(8,128)S(1)}, f32[320,512]{1,0:T(8,128)S(1)}, u32[]{:S(2)}, u32[]{:S(2)}) collective-permute-start(f32[320,512]{1,0:T(8,128)S(1)} %shard_map.72.refs_0_), channel_id=1, source_target_pairs={{0,32},{1,33},{2,34},{3,35},{4,36},{5,37},{6,38},{7,39},{8,40},{9,... | collective-permute-start | bytes 1966088 | tf_op jit(solution)/shard_map/ppermute | solution.py:423
  173.0 7.2 %collective-permute-start.19 = (f32[72,512]{1,0:T(8,128)S(1)}, f32[72,512]{1,0:T(8,128)S(1)}, u32[]{:S(2)}, u32[]{:S(2)}) collective-permute-start(f32[72,512]{1,0:T(8,128)S(1)} %get-tuple-element.97), channel_id=1, source_target_pairs={{0,32},{1,33},{2,34},{3,35},{4,36},{5,37},{6,38},{7,39},{8,40},{9,... | collective-permute-start | bytes 442376 | tf_op jit(solution)/shard_map/ppermute | solution.py:423
  173.1 7.1 %collective-permute-start.20 = (f32[72,512]{1,0:T(8,128)S(1)}, f32[72,512]{1,0:T(8,128)S(1)}, u32[]{:S(2)}, u32[]{:S(2)}) collective-permute-start(f32[72,512]{1,0:T(8,128)S(1)} %get-tuple-element.96.refs_0_), channel_id=1, source_target_pairs={{0,96},{1,97},{2,98},{3,99},{4,100},{5,101},{6,102},{7,103},{8,104... | collective-permute-start | bytes 442376 | tf_op jit(solution)/shard_map/ppermute | solution.py:423
  175.8 9.2 %collective-permute-start.23 = (f32[192,512]{1,0:T(8,128)S(1)}, f32[192,512]{1,0:T(8,128)S(1)}, u32[]{:S(2)}, u32[]{:S(2)}) collective-permute-start(f32[192,512]{1,0:T(8,128)S(1)} %get-tuple-element.102), channel_id=1, source_target_pairs={{0,16},{1,17},{2,18},{3,19},{4,20},{5,21},{6,22},{7,23},{8,24},{9,... | collective-permute-start | bytes 1179656 | tf_op jit(solution)/shard_map/ppermute | solution.py:423
  181.1 10.7 %collective-permute-start.28 = (f32[192,512]{1,0:T(8,128)S(1)}, f32[192,512]{1,0:T(8,128)S(1)}, u32[]{:S(2)}, u32[]{:S(2)}) collective-permute-start(f32[192,512]{1,0:T(8,128)S(1)} %get-tuple-element.111), channel_id=1, source_target_pairs={{0,16},{1,17},{2,18},{3,19},{4,20},{5,21},{6,22},{7,23},{8,24},{9,... | collective-permute-start | bytes 1179656 | tf_op jit(solution)/shard_map/ppermute | solution.py:423
  182.3 5.5 %collective-permute-start.24 = (f32[72,512]{1,0:T(8,128)S(1)}, f32[72,512]{1,0:T(8,128)S(1)}, u32[]{:S(2)}, u32[]{:S(2)}) collective-permute-start(f32[72,512]{1,0:T(8,128)S(1)} %get-tuple-element.104), channel_id=1, source_target_pairs={{0,64},{1,65},{2,66},{3,67},{4,68},{5,69},{6,70},{7,71},{8,72},{9,... | collective-permute-start | bytes 442376 | tf_op jit(solution)/shard_map/ppermute | solution.py:423
  183.2 6.4 %collective-permute-start.25 = (f32[64,512]{1,0:T(8,128)S(1)}, f32[64,512]{1,0:T(8,128)S(1)}, u32[]{:S(2)}, u32[]{:S(2)}) collective-permute-start(f32[64,512]{1,0:T(8,128)S(1)} %get-tuple-element.107), channel_id=1, source_target_pairs={{0,4},{1,5},{2,6},{3,7},{4,8},{5,9},{6,10},{7,11},{8,12},{9,13},{1... | collective-permute-start | bytes 393224 | tf_op jit(solution)/shard_map/ppermute | solution.py:423
  183.2 6.4 %collective-permute-start.26 = (f32[64,512]{1,0:T(8,128)S(1)}, f32[64,512]{1,0:T(8,128)S(1)}, u32[]{:S(2)}, u32[]{:S(2)}) collective-permute-start(f32[64,512]{1,0:T(8,128)S(1)} %get-tuple-element.108), channel_id=1, source_target_pairs={{0,8},{1,9},{2,10},{3,11},{4,12},{5,13},{6,14},{7,15},{8,0},{9,1},... | collective-permute-start | bytes 393224 | tf_op jit(solution)/shard_map/ppermute | solution.py:423
  185.0 5.5 %collective-permute-start.27 = (f32[64,512]{1,0:T(8,128)S(1)}, f32[64,512]{1,0:T(8,128)S(1)}, u32[]{:S(2)}, u32[]{:S(2)}) collective-permute-start(f32[64,512]{1,0:T(8,128)S(1)} %get-tuple-element.98.refs_0_), channel_id=1, source_target_pairs={{0,12},{1,13},{2,14},{3,15},{4,0},{5,1},{6,2},{7,3},{8,4},{9,5},{1... | collective-permute-start | bytes 393224 | tf_op jit(solution)/shard_map/ppermute | solution.py:423
  186.9 4.9 %copy-start.14 = (bf16[512,512]{1,0:T(8,128)(2,1)S(1)}, bf16[512,512]{1,0:T(8,128)(2,1)}, u32[]{:S(2)}) copy-start(bf16[512,512]{1,0:T(8,128)(2,1)} %copy-done.13) | copy-start | bytes 1572868
  186.9 4.9 %copy-start.16 = (bf16[512,512]{1,0:T(8,128)(2,1)S(1)}, bf16[512,512]{1,0:T(8,128)(2,1)}, u32[]{:S(2)}) copy-start(bf16[512,512]{1,0:T(8,128)(2,1)} %copy-done.15) | copy-start | bytes 1572868
  188.3 3.4 %collective-permute-start.29 = (f32[8,512]{1,0:T(8,128)S(1)}, f32[8,512]{1,0:T(8,128)S(1)}, u32[]{:S(2)}, u32[]{:S(2)}) collective-permute-start(f32[8,512]{1,0:T(8,128)S(1)} %get-tuple-element.105.refs_0_.refs_5_), channel_id=1, source_target_pairs={{0,16},{1,17},{2,18},{3,19},{4,20},{5,21},{6,22},{7,23},{8,24},{9,... | collective-permute-start | bytes 49160 | tf_op jit(solution)/shard_map/ppermute | solution.py:423
  195.6 16.2 %collective-permute-start.30 = (f32[512,512]{1,0:T(8,128)S(1)}, f32[512,512]{1,0:T(8,128)S(1)}, u32[]{:S(2)}, u32[]{:S(2)}) collective-permute-start(f32[512,512]{1,0:T(8,128)S(1)} %shard_map.79), channel_id=1, source_target_pairs={{0,16},{1,17},{2,18},{3,19},{4,20},{5,21},{6,22},{7,23},{8,24},{9,... | collective-permute-start | bytes 3145736 | tf_op jit(solution)/shard_map/ppermute | solution.py:423
  196.0 25.4 %collective-permute-start.31 = (f32[512,512]{1,0:T(8,128)S(1)}, f32[512,512]{1,0:T(8,128)S(1)}, u32[]{:S(2)}, u32[]{:S(2)}) collective-permute-start(f32[512,512]{1,0:T(8,128)S(1)} %shard_map.79), channel_id=1, source_target_pairs={{0,18},{1,19},{2,16},{3,17},{4,22},{5,23},{6,20},{7,21},{8,26},{9,... | collective-permute-start | bytes 3145736 | tf_op jit(solution)/shard_map/ppermute | solution.py:423
  211.8 12.3 %collective-permute-start.32 = (f32[512,512]{1,0:T(8,128)S(1)}, f32[512,512]{1,0:T(8,128)S(1)}, u32[]{:S(2)}, u32[]{:S(2)}) collective-permute-start(f32[512,512]{1,0:T(8,128)S(1)} %collective-permute-done.30), channel_id=1, source_target_pairs={{0,1},{1,0},{2,3},{3,2},{4,5},{5,4},{6,7},{7,6},{8,9},{9,8},{10,11... | collective-permute-start | bytes 3145736 | tf_op jit(solution)/shard_map/ppermute | solution.py:423
  221.4 4.4 %collective-permute-start.33 = (f32[512,512]{1,0:T(8,128)S(1)}, f32[512,512]{1,0:T(8,128)}, u32[]{:S(2)}, u32[]{:S(2)}) collective-permute-start(f32[512,512]{1,0:T(8,128)S(1)} %collective-permute-done.31), channel_id=1, source_target_pairs={{0,1},{1,0},{2,3},{3,2},{4,5},{5,4},{6,7},{7,6},{8,9},{9,8},{10,11... | collective-permute-start | bytes 3145736 | tf_op jit(solution)/shard_map/ppermute | solution.py:423
  224.1 2.0 copy-start.21

commit v6 on v5

--- a/solution.py
+++ b/solution.py
@@ -232,11 +232,33 @@
 TERMS = ((1, 0, (0,)), (3, 1, (1,)), (0, 0, (2, 0)), (0, 1, (2, 1)))
 
 
+def sum_rows_body(table, where, first_in, second_in, sums_out, out):
+    for y in range(4):
+        for u in range(4):
+            rows = []
+            for z in (1 - where[1], where[1]):
+                block = table[u * 8 + z * 4 + y]
+                a = block >> 2
+                rows.append(jnp.where(a < 4, first_in[a & 3], second_in[a & 3]))
+                rows.append(sums_out[block & 3])
+            rows.append(jnp.zeros((EXTRA - 4, BLK), jnp.float32))
+            out[y, u] = jnp.concatenate(rows, axis=0)
+
+
+def sum_rows(order, sums):
+    ins = [(s, whole(s)) for s in sums]
+    return order(sum_rows_body, 1, ins, [full(4, 4, EXTRA, BLK)])[0]
+
+
 def turn_body(jobs, table, where, *refs):
-    sums, refs = refs[:3], refs[3:]
-    ins, outs = refs[: 4 * len(jobs)], refs[4 * len(jobs) :]
-    for n, (stream, r, half, place) in enumerate(jobs):
-        base, more, got, term = ins[4 * n : 4 * n + 4]
+    refs = list(refs)
+    ins = []
+    for stream, *_ in jobs:
+        n = 5 if stream == "x" else 4
+        ins.append(refs[:n])
+        refs = refs[n:]
+    outs = refs
+    for (stream, r, half, place), (base, more, got, term, *sums) in zip(jobs, ins):
         out = outs[place[0]].at[place[1]] if len(place) == 2 else outs[place[0]]
         out[:ROWS_A, :] = base[0] + more[0]
         rows = (half_rows(stream) - ROWS_A) // 2
@@ -244,23 +266,13 @@
             at = (0, v) if stream == "y" else (v, 0)
             low = ROWS_A + v * rows
             out[low : low + ROWS_C, :] = got[at] + term[at]
-            if stream == "y":
-                continue
-            first_in, second_in, sums_out = sums
-            parts = []
-            for sub in (1, 0):
-                block = table[spot(where, "y", r, sub, 2 * half + v)]
-                a = block >> 2
-                parts.append(jnp.where(a < 4, first_in[a & 3], second_in[a & 3]))
-                parts.append(sums_out[block & 3])
-            parts.append(jnp.zeros((EXTRA - 4, BLK), jnp.float32))
-            out[low + ROWS_C : low + rows, :] = jnp.concatenate(parts, axis=0)
+            if stream == "x":
+                out[low + ROWS_C : low + rows, :] = sums[0][0, v]
 
 
 def turn(order, streams, pieces, halves, got, terms, sums):
     once = dict(pipeline_mode=pl.Buffered(1))
-    ins = [(s, whole(s)) for s in sums]
-    jobs, outs = [], []
+    ins, jobs, outs = [], [], []
     for stream in streams:
         for r, half, place in pieces:
             jobs.append((stream, r, half, (place[0] + len(outs), *place[1:])))
@@ -275,6 +287,9 @@
             ins += [(a, spec((1, ROWS_A, BLK), here, **once)) for a in halves[stream][half]]
             for a in (got, terms):
                 ins.append((a.reshape(4, 4, 2 * ROWS_C, BLK), spec(shape, side, **once)))
+            if stream == "x":
+                at = lambda i, t, w, r=r, h=half: ((w[2] + r) & 3, h, 0, 0)
+                ins.append((sums, spec((1, 2, EXTRA, BLK), at, **once)))
         rows = half_rows(stream)
         if pieces is TERMS:
             outs += [full(rows, BLK)] * 2 + [full(2, rows, BLK)]
@@ -432,14 +447,17 @@
     made = products(order, turned, latents, SETS_B + SETS_T)
     got_b = both(*made[:2], "x") + both(*made[2:4], "y")
     sets_t = relay(order, got_a, made[4:])
-    sums = [square_sums(order, latents, eig_in, 0, 4)]
+    sums = [
+        square_sums(order, latents, eig_in, 0, 4),
+        square_sums(order, latents, eig_in, 4, 4),
+    ]
     basis_in, basis_out = bases(order, eig_in, eig_out)
     got_t = both(*order.gate(sets_t[:2], got_b[:2]), "x")
     got_t += both(*order.gate(sets_t[2:], got_b[2:]), "y")
     got_b = [got_b[n] for n in (1, 0, 3, 2)]
     *own, terms_c = products(order, turned, latents, SETS_OWN + SETS_KEEP, got_b)
-    sums.append(square_sums(order, latents, eig_in, 4, 4))
     sums.append(square_sums(order, out_grads, eig_out, 0, 4))
+    sums = sum_rows(order, sums)
 
     halves = {
         stream: ((own[n], got_t[n]), (own[n + 1], got_t[n + 1]))

time: 229 us -> 229 us (level)
  local copies, waits for them, and re-layouts: 18.8 us -> 21.1 us
    unnamed x56 -> x58, local copies, waits for them, and re-layouts: 15.8 us -> 18.1 us
    pallas_call x23 -> x24, Pallas kernels: 90 us -> 89.3 us  [__call__(): pl.pallas_call(inner, out_shape=shapes, grid_spec=pltpu.PrefetchScalarGri...]
where the time goes in v6:
time: 229 us; the launch traced here: 228 us
  Pallas kernels  89.3 us (39%)
  waiting for transfers between devices  65.3 us (29%)
  starting transfers between devices  50.9 us (22%)
  local copies, waits for them, and re-layouts  21.1 us (9%)
    pallas_call x24, Pallas kernels, __call__(): pl.pallas_call(inner, out_shape=shapes, grid_spec=pltpu.PrefetchScalarGri...  89.3 us
    ppermute x34, waiting for transfers between devices, on_device(): send = lambda value, pairs: lax.ppermute(value, AXES, pairs)  65.3 us
    ppermute x34, starting transfers between devices, on_device(): send = lambda value, pairs: lax.ppermute(value, AXES, pairs)  50.9 us
    unnamed x58, local copies, waits for them, and re-layouts  18.1 us
  transfers between devices with their start and end apart: 34, of which 15 were waited for; matrix products, arithmetic and copies ran while one was open for 0% of the time, Pallas kernels for 33%

profile of v6, /device:TPU:1, one launch (start us, length us, event | category | flops | bytes accessed | tf_op | source)
XLA Modules:
  0.0 227.7 jit_solution(6477141605452085951)
XLA Ops:
  0.6 11.2 %shard_map.55 = (bf16[2048,768]{1,0:T(8,128)(2,1)}, f32[4,192,512]{2,1,0:T(8,128)}, f32[4,192,512]{2,1,0:T(8,128)}, f32[4,192,512]{2,1,0:T(8,128)}, f32[4,192,512]{2,1,0:T(8,128)}) custom-call(s32[32]{0:T(128)} %table.47, s32[3]{0:T(128)} %pad_add_fusion.where, bf16[768,2048]{1,0:T(8,128)(2,1)} %refs_1_.9, bf16[768,4096]{1,0:T(8,128)(2,1)} %refs_2_.14, ...), custom_call_target="tpu_custom_call" | custom-call | bytes 3690000 | tf_op jit(solution)/shard_map/pallas_call | solution.py:118
  11.8 2.1 collective-permute-start
  13.9 1.5 collective-permute-start.1
  15.4 1.3 collective-permute-start.2
  16.7 1.4 collective-permute-start.3
  18.1 8.2 %shard_map.56.refs_0_ = f32[16,128,512]{2,1,0:T(8,128)} custom-call(s32[32]{0:T(128)} %table.47, s32[3]{0:T(128)} %pad_add_fusion.where, f32[4,192,512]{2,1,0:T(8,128)} %get-tuple-element.59.refs_0_, bf16[2048,768]{1,0:T(8,128)(2,1)} %get-tuple-element.60.refs_1_, bf16[768,4096]{1,0:T(8,128)(2,1)} %refs_2_.14), custom_call_target="tpu_custom_call" | custom-call | bytes 3690000 | tf_op jit(solution)/shard_map/pallas_call | solution.py:118
  26.4 1.6 collective-permute-start.9
  28.0 12.4 %shard_map.57 = (f32[4,192,512]{2,1,0:T(8,128)}, f32[4,192,512]{2,1,0:T(8,128)}, f32[4,192,512]{2,1,0:T(8,128)}, f32[4,192,512]{2,1,0:T(8,128)}, f32[4,192,512]{...) custom-call(s32[32]{0:T(128)} %table.47, s32[3]{0:T(128)} %pad_add_fusion.where, ...), custom_call_target="tpu_custom_call" | custom-call | bytes 3690000 | tf_op jit(solution)/shard_map/pallas_call | solution.py:118
  40.4 9.2 %collective-permute-done.refs_1_ = f32[4,192,512]{2,1,0:T(8,128)S(1)} collective-permute-done((f32[4,192,512]{2,1,0:T(8,128)}, f32[4,192,512]{2,1,0:T(8,128)S(1)}, u32[]{:S(2)}, u32[]{:S(2)}) %collective-permute-start) | collective-permute-done | bytes 1572896 | tf_op jit(solution)/shard_map/ppermute | solution.py:438
  49.6 2.7 %collective-permute-start.7 = (f32[4,192,512]{2,1,0:T(8,128)}, f32[4,192,512]{2,1,0:T(8,128)}, u32[]{:S(2)}, u32[]{:S(2)}) collective-permute-start(f32[4,192,512]{2,1,0:T(8,128)} %get-tuple-element.75), channel_id=1, source_target_pairs={{0,96},{1,97},{2,98},{3,99},{4,100},{5,101},{6,102},{7,103},{8,104... | collective-permute-start | bytes 4718600 | tf_op jit(solution)/shard_map/ppermute | solution.py:438
  52.3 1.1 collective-permute-start.4
  53.4 1.6 collective-permute-start.5
  55.0 8.1 %shard_map.58 = (f32[4,192,512]{2,1,0:T(8,128)}, f32[4,192,512]{2,1,0:T(8,128)}, f32[4,192,512]{2,1,0:T(8,128)}, f32[4,192,512]{2,1,0:T(8,128)}) custom-call(s32[32]{0:T(128)} %table.47, s32[3]{0:T(128)} %pad_add_fusion.where, f32[4,192,512]{2,1,0:T(8,128)} %get-tuple-element.61.refs_0_.refs_8_, f32[4,192,512]{2,1,0:T(8,128)} %copy-done.25, ...), custom_call_target="tpu_custom_call" | custom-call | bytes 3690000 | tf_op jit(solution)/shard_map/pallas_call | solution.py:118
  63.2 3.4 %copy-done.2 = f32[8,512,512]{2,1,0:T(8,128)S(1)} copy-done((f32[8,512,512]{2,1,0:T(8,128)S(1)}, f32[8,512,512]{2,1,0:T(8,128)}, u32[]{:S(2)}) %copy-start.2) | copy-done | bytes 8388632
  66.6 1.4 copy-done.10
  68.0 4.9 %shard_map.59.refs_0_.refs_1_ = f32[4,1,512]{2,1,0:T(1,128)S(1)} custom-call(s32[32]{0:T(128)S(1)} %copy-done.22, s32[3]{0:T(128)S(1)} %copy-done.20, f32[4,192,512]{2,1,0:T(8,128)S(1)} %copy-done.10, bf16[768,4096]{1,0:T(8,128)(2,1)S(1)} %bitcast.30, f32[8,512,512]{2,1,0:T(8,128)S(1)} %copy-done.2), custom_call_target="tpu_custom_call" | custom-call | bytes 3690000 | tf_op jit(solution)/shard_map/pallas_call | solution.py:118
  72.8 3.4 %copy-done.3 = f32[8,512,512]{2,1,0:T(8,128)S(1)} copy-done((f32[8,512,512]{2,1,0:T(8,128)S(1)}, f32[8,512,512]{2,1,0:T(8,128)}, u32[]{:S(2)}) %copy-start.3) | copy-done | bytes 8388632
  76.2 4.9 %shard_map.60.refs_0_.refs_2_ = f32[4,1,512]{2,1,0:T(1,128)S(1)} custom-call(s32[32]{0:T(128)S(1)} %copy-done.22, s32[3]{0:T(128)S(1)} %copy-done.20, f32[4,1,512]{2,1,0:T(1,128)S(1)} %shard_map.59.refs_0_.refs_1_, bf16[768,4096]{1,0:T(8,128)(2,1)S(1)} %bitcast.30, f32[8,512,512]{2,1,0:T(8,128)S(1)} %copy-done.3), custom_call_target="tpu_custom_call" | custom-call | bytes 3690000 | tf_op jit(solution)/shard_map/pallas_call | solution.py:118
  81.1 0.9 shard_map.61
  82.8 0.8 copy-done.14
  83.6 0.8 copy-done.16
  84.4 0.8 copy-done.18
  85.7 2.4 %collective-permute-start.10 = (f32[4,192,512]{2,1,0:T(8,128)}, f32[4,192,512]{2,1,0:T(8,128)S(1)}, u32[]{:S(2)}, u32[]{:S(2)}) collective-permute-start(f32[4,192,512]{2,1,0:T(8,128)} %get-tuple-element.77.refs_4_), channel_id=1, source_target_pairs={{0,96},{1,97},{2,98},{3,99},{4,100},{5,101},{6,102},{7,103},{8,104... | collective-permute-start | bytes 4718600 | tf_op jit(solution)/shard_map/ppermute | solution.py:438
  88.1 0.9 collective-permute-start.11
  89.1 2.0 collective-permute-start.12
  91.0 12.5 %shard_map.64 = (f32[4,192,512]{2,1,0:T(8,128)}, f32[4,192,512]{2,1,0:T(8,128)}, f32[4,192,512]{2,1,0:T(8,128)}, f32[4,192,512]{2,1,0:T(8,128)}, f32[16,128,512]{2,1,0:T(8,128)}) custom-call(s32[32]{0:T(128)} %table.47, s32[3]{0:T(128)} %pad_add_fusion.where, f32[4,192,512]{2,1,0:T(8,128)} %get-tuple-element.78.refs_0_, ...), custom_call_target="tpu_custom_call" | custom-call | bytes 3690000 | tf_op jit(solution)/shard_map/pallas_call | solution.py:118
  103.6 2.2 copy-done
  105.7 2.2 copy-done.9
  107.9 1.9 copy-done.11
  109.8 4.9 %shard_map.65.refs_0_.refs_3_ = f32[4,1,512]{2,1,0:T(1,128)S(1)} custom-call(s32[32]{0:T(128)S(1)} %copy-done.23, s32[3]{0:T(128)S(1)} %copy-done.21, f32[16,128,512]{2,1,0:T(8,128)S(1)} %copy-done, bf16[768,2048]{1,0:T(8,128)(2,1)S(1)} %copy-done.11, f32[4,512,512]{2,1,0:T(8,128)S(1)} %copy-done.9), custom_call_target="tpu_custom_call" | custom-call | bytes 3690000 | tf_op jit(solution)/shard_map/pallas_call | solution.py:118
  115.4 4.2 %collective-permute-done.10.refs_7_.refs_12_.refs_17_ = f32[4,192,512]{2,1,0:T(8,128)S(1)} collective-permute-done((f32[4,192,512]{2,1,0:T(8,128)}, f32[4,192,512]{2,1,0:T(8,128)S(1)}, u32[]{:S(2)}, u32[]{:S(2)}) %collective-permute-start.10) | collective-permute-done | bytes 1572896 | tf_op jit(solution)/shard_map/ppermute | solution.py:438
  119.6 3.0 %collective-permute-done.8.refs_2_.refs_17_.refs_12_ = f32[4,192,512]{2,1,0:T(8,128)S(1)} collective-permute-done((f32[4,192,512]{2,1,0:T(8,128)}, f32[4,192,512]{2,1,0:T(8,128)S(1)}, u32[]{:S(2)}, u32[]{:S(2)}) %collective-permute-start.8) | collective-permute-done | bytes 1572896 | tf_op jit(solution)/shard_map/ppermute | solution.py:438
  122.7 3.3 %shard_map.67 = (f32[2,336,512]{2,1,0:T(8,128)}, f32[2,336,512]{2,1,0:T(8,128)S(1)}) custom-call(s32[32]{0:T(128)S(1)} %copy-done.23, s32[3]{0:T(128)S(1)} %copy-done.21, f32[4,4,8,512]{3,2,1,0:T(8,128)S(1)} %shard_map.66.refs_0_.refs_5_.refs_10_.refs_15_.refs_20_, f32[4,192,512]{2,1,0:T(8,128)S(1)} %copy-done.6, ...), custom_call_target="tpu_custom_call" | custom-call | bytes 3690000 | tf_op jit(solution)/shard_map/pallas_call | solution.py:118
  126.6 2.0 collective-permute-start.14
  128.7 3.0 %shard_map.68 = (f32[2,320,512]{2,1,0:T(8,128)}, f32[2,320,512]{2,1,0:T(8,128)S(1)}) custom-call(s32[32]{0:T(128)S(1)} %copy-done.23, s32[3]{0:T(128)S(1)} %copy-done.21, f32[2,336,512]{2,1,0:T(8,128)S(1)} %get-tuple-element.83.refs_0_, f32[4,192,512]{2,1,0:T(8,128)S(1)} %copy-done.4, f32[4,192,512]{2,1,0:T(8,128)S(1)} %collective-permute-done.11.refs_2_.refs_14_.refs_10_, ...), custom_call_target="tpu_custom_call" | custom-call | bytes 3690000 | tf_op jit(solution)/shard_map/pallas_call | solution.py:118
  131.7 2.7 %collective-permute-start.16 = (f32[2,320,512]{2,1,0:T(8,128)S(1)}, f32[2,320,512]{2,1,0:T(8,128)S(1)}, u32[]{:S(2)}, u32[]{:S(2)}) collective-permute-start(f32[2,320,512]{2,1,0:T(8,128)S(1)} %get-tuple-element.87.refs_0_), channel_id=1, source_target_pairs={{0,96},{1,97},{2,98},{3,99},{4,100},{5,101},{6,102},{7,103},{8,104... | collective-permute-start | bytes 3932168 | tf_op jit(solution)/shard_map/ppermute | solution.py:438
  134.4 2.0 shard_map.69
  136.4 2.0 shard_map.70
  138.4 16.9 %collective-permute-done.13.refs_1_.refs_2_ = f32[2,336,512]{2,1,0:T(8,128)S(1)} collective-permute-done((f32[2,336,512]{2,1,0:T(8,128)}, f32[2,336,512]{2,1,0:T(8,128)S(1)}, u32[]{:S(2)}, u32[]{:S(2)}) %collective-permute-start.13) | collective-permute-done | bytes 1376288 | tf_op jit(solution)/shard_map/ppermute | solution.py:438
  156.6 1.6 collective-permute-start.18
  158.3 0.9 collective-permute-done.15.refs_1_.refs_4_
  160.4 1.6 collective-permute-start.22
  162.0 7.0 %collective-permute-done.18.refs_5_ = f32[336,512]{1,0:T(8,128)S(1)} collective-permute-done((f32[336,512]{1,0:T(8,128)S(1)}, f32[336,512]{1,0:T(8,128)S(1)}, u32[]{:S(2)}, u32[]{:S(2)}) %collective-permute-start.18) | collective-permute-done | bytes 688160 | tf_op jit(solution)/shard_map/ppermute | solution.py:438
  169.0 2.2 collective-permute-done.17.refs_4_
  171.2 0.9 shard_map.75
  172.2 2.7 %collective-permute-start.20 = (f32[72,512]{1,0:T(8,128)S(1)}, f32[72,512]{1,0:T(8,128)S(1)}, u32[]{:S(2)}, u32[]{:S(2)}) collective-permute-start(f32[72,512]{1,0:T(8,128)S(1)} %get-tuple-element.96.refs_0_), channel_id=1, source_target_pairs={{0,96},{1,97},{2,98},{3,99},{4,100},{5,101},{6,102},{7,103},{8,104... | collective-permute-start | bytes 442376 | tf_op jit(solution)/shard_map/ppermute | solution.py:438
  174.8 1.4 collective-permute-start.23
  176.2 3.1 %collective-permute-done.19.refs_1_.refs_2_ = f32[72,512]{1,0:T(8,128)S(1)} collective-permute-done((f32[72,512]{1,0:T(8,128)S(1)}, f32[72,512]{1,0:T(8,128)S(1)}, u32[]{:S(2)}, u32[]{:S(2)}) %collective-permute-start.19) | collective-permute-done | bytes 147488 | tf_op jit(solution)/shard_map/ppermute | solution.py:438
  179.3 0.8 shard_map.76
  180.2 1.5 collective-permute-start.28
  181.6 1.2 collective-permute-start.24
  182.8 1.5 collective-permute-start.26
  184.3 1.2 collective-permute-start.27
  185.5 1.0 shard_map.77.refs_0_.refs_1_
  188.1 1.1 collective-permute-done.25.refs_4_
  189.2 0.9 collective-permute-done.27.refs_6_
  190.1 0.9 shard_map.79.refs_0_.refs_2_
  191.1 3.8 %shard_map.80 = f32[512,512]{1,0:T(8,128)S(1)} custom-call(s32[32]{0:T(128)S(1)} %copy-done.23, s32[3]{0:T(128)S(1)} %copy-done.21, f32[128,512]{1,0:T(8,128)S(1)} %shard_map.79.refs_0_.refs_2_, f32[192,512]{1,0:T(8,128)S(1)} %shard_map.77.refs_0_.refs_1_, f32[128,512]{1,0:T(8,128)S(1)} %shard_map.79.refs_0_.refs_2_, ...), custom_call_target="tpu_custom_call" | custom-call | bytes 3690000 | tf_op jit(solution)/shard_map/pallas_call | solution.py:118
  195.2 3.4 %collective-permute-start.31 = (f32[512,512]{1,0:T(8,128)S(1)}, f32[512,512]{1,0:T(8,128)S(1)}, u32[]{:S(2)}, u32[]{:S(2)}) collective-permute-start(f32[512,512]{1,0:T(8,128)S(1)} %shard_map.80), channel_id=1, source_target_pairs={{0,18},{1,19},{2,16},{3,17},{4,22},{5,23},{6,20},{7,21},{8,26},{9,... | collective-permute-start | bytes 3145736 | tf_op jit(solution)/shard_map/ppermute | solution.py:438
  198.6 13.9 %collective-permute-done.30 = f32[512,512]{1,0:T(8,128)S(1)} collective-permute-done((f32[512,512]{1,0:T(8,128)S(1)}, f32[512,512]{1,0:T(8,128)S(1)}, u32[]{:S(2)}, u32[]{:S(2)}) %collective-permute-start.30) | collective-permute-done | bytes 1048608 | tf_op jit(solution)/shard_map/ppermute | solution.py:438
  212.4 8.3 %collective-permute-start.32 = (f32[512,512]{1,0:T(8,128)S(1)}, f32[512,512]{1,0:T(8,128)S(1)}, u32[]{:S(2)}, u32[]{:S(2)}) collective-permute-start(f32[512,512]{1,0:T(8,128)S(1)} %collective-permute-done.30), channel_id=1, source_target_pairs={{0,1},{1,0},{2,3},{3,2},{4,5},{5,4},{6,7},{7,6},{8,9},{9,8},{10,11... | collective-permute-start | bytes 3145736 | tf_op jit(solution)/shard_map/ppermute | solution.py:438
  220.7 1.9 collective-permute-start.33
  223.5 1.6 collective-permute-done.33
  225.5 2.3 bitcast_dynamic-update-slice_fusion
  (95 shorter events, 8.9 us)
Async XLA Ops:
  11.8 37.8 %collective-permute-start = (f32[4,192,512]{2,1,0:T(8,128)}, f32[4,192,512]{2,1,0:T(8,128)S(1)}, u32[]{:S(2)}, u32[]{:S(2)}) collective-permute-start(f32[4,192,512]{2,1,0:T(8,128)} %get-tuple-element.62), channel_id=1, source_target_pairs={{0,32},{1,33},{2,34},{3,35},{4,36},{5,37},{6,38},{7,39},{8,40},{9,... | collective-permute-start | bytes 4718600 | tf_op jit(solution)/shard_map/ppermute | solution.py:438
  13.9 35.7 %collective-permute-start.1 = (f32[4,192,512]{2,1,0:T(8,128)}, f32[4,192,512]{2,1,0:T(8,128)S(1)}, u32[]{:S(2)}, u32[]{:S(2)}) collective-permute-start(f32[4,192,512]{2,1,0:T(8,128)} %get-tuple-element.63), channel_id=1, source_target_pairs={{0,96},{1,97},{2,98},{3,99},{4,100},{5,101},{6,102},{7,103},{8,104... | collective-permute-start | bytes 4718600 | tf_op jit(solution)/shard_map/ppermute | solution.py:438
  15.4 36.9 %collective-permute-start.2 = (f32[4,192,512]{2,1,0:T(8,128)}, f32[4,192,512]{2,1,0:T(8,128)}, u32[]{:S(2)}, u32[]{:S(2)}) collective-permute-start(f32[4,192,512]{2,1,0:T(8,128)} %get-tuple-element.64), channel_id=1, source_target_pairs={{0,4},{1,5},{2,6},{3,7},{4,8},{5,9},{6,10},{7,11},{8,12},{9,13},{1... | collective-permute-start | bytes 4718600 | tf_op jit(solution)/shard_map/ppermute | solution.py:438
  16.7 36.7 %collective-permute-start.3 = (f32[4,192,512]{2,1,0:T(8,128)}, f32[4,192,512]{2,1,0:T(8,128)}, u32[]{:S(2)}, u32[]{:S(2)}) collective-permute-start(f32[4,192,512]{2,1,0:T(8,128)} %get-tuple-element.59.refs_0_), channel_id=1, source_target_pairs={{0,12},{1,13},{2,14},{3,15},{4,0},{5,1},{6,2},{7,3},{8,4},{9,5},{1... | collective-permute-start | bytes 4718600 | tf_op jit(solution)/shard_map/ppermute | solution.py:438
  26.4 96.3 %collective-permute-start.9 = (f32[16,128,512]{2,1,0:T(8,128)}, f32[16,128,512]{2,1,0:T(8,128)}, u32[]{:S(2)}, u32[]{:S(2)}) collective-permute-start(f32[16,128,512]{2,1,0:T(8,128)} %shard_map.56.refs_0_), channel_id=1, source_target_pairs={{0,16},{1,17},{2,18},{3,19},{4,20},{5,21},{6,22},{7,23},{8,24},{9,... | collective-permute-start | bytes 12582920 | tf_op jit(solution)/shard_map/ppermute | solution.py:438
  28.0 35.1 %slice-start = ((s8[6291456]{0:T(1024)(128)(4,1)}), s8[4194304]{0:T(1024)(128)(4,1)S(1)}, s32[]{:S(2)}) async-start(s8[6291456]{0:T(1024)(128)(4,1)} %bitcast.29), calls=%async_computation | async-start | bytes 8388608
  49.6 5.4 %copy-start.25 = (f32[4,192,512]{2,1,0:T(8,128)}, f32[4,192,512]{2,1,0:T(8,128)S(1)}, u32[]{:S(2)}) copy-start(f32[4,192,512]{2,1,0:T(8,128)S(1)} %collective-permute-done.refs_1_) | copy-start | bytes 4718596
  49.6 36.1 %collective-permute-start.6 = (f32[4,192,512]{2,1,0:T(8,128)}, f32[4,192,512]{2,1,0:T(8,128)}, u32[]{:S(2)}, u32[]{:S(2)}) collective-permute-start(f32[4,192,512]{2,1,0:T(8,128)} %get-tuple-element.74), channel_id=1, source_target_pairs={{0,32},{1,33},{2,34},{3,35},{4,36},{5,37},{6,38},{7,39},{8,40},{9,... | collective-permute-start | bytes 4718600 | tf_op jit(solution)/shard_map/ppermute | solution.py:438
  49.6 5.4 %copy-start.26 = (f32[4,192,512]{2,1,0:T(8,128)}, f32[4,192,512]{2,1,0:T(8,128)S(1)}, u32[]{:S(2)}) copy-start(f32[4,192,512]{2,1,0:T(8,128)S(1)} %collective-permute-done.1.refs_2_) | copy-start | bytes 4718596
  49.6 36.1 %collective-permute-start.7 = (f32[4,192,512]{2,1,0:T(8,128)}, f32[4,192,512]{2,1,0:T(8,128)}, u32[]{:S(2)}, u32[]{:S(2)}) collective-permute-start(f32[4,192,512]{2,1,0:T(8,128)} %get-tuple-element.75), channel_id=1, source_target_pairs={{0,96},{1,97},{2,98},{3,99},{4,100},{5,101},{6,102},{7,103},{8,104... | collective-permute-start | bytes 4718600 | tf_op jit(solution)/shard_map/ppermute | solution.py:438
  52.3 35.8 %collective-permute-start.4 = (f32[4,192,512]{2,1,0:T(8,128)}, f32[4,192,512]{2,1,0:T(8,128)}, u32[]{:S(2)}, u32[]{:S(2)}) collective-permute-start(f32[4,192,512]{2,1,0:T(8,128)} %get-tuple-element.70), channel_id=1, source_target_pairs={{0,4},{1,5},{2,6},{3,7},{4,8},{5,9},{6,10},{7,11},{8,12},{9,13},{1... | collective-permute-start | bytes 4718600 | tf_op jit(solution)/shard_map/ppermute | solution.py:438
  53.4 34.8 %collective-permute-start.5 = (f32[4,192,512]{2,1,0:T(8,128)}, f32[4,192,512]{2,1,0:T(8,128)}, u32[]{:S(2)}, u32[]{:S(2)}) collective-permute-start(f32[4,192,512]{2,1,0:T(8,128)} %get-tuple-element.71), channel_id=1, source_target_pairs={{0,12},{1,13},{2,14},{3,15},{4,0},{5,1},{6,2},{7,3},{8,4},{9,5},{1... | collective-permute-start | bytes 4718600 | tf_op jit(solution)/shard_map/ppermute | solution.py:438
  55.0 8.1 %slice-start.1 = ((s8[6291456]{0:T(1024)(128)(4,1)}), s8[2097152]{0:T(1024)(128)(4,1)S(1)}, s32[]{:S(2)}) async-start(s8[6291456]{0:T(1024)(128)(4,1)} %bitcast.29), calls=%async_computation.1 | async-start | bytes 4194304
  55.0 8.1 %copy-start.20 = (s32[3]{0:T(128)S(1)}, s32[3]{0:T(128)}, u32[]{:S(2)}) copy-start(s32[3]{0:T(128)} %pad_add_fusion.where) | copy-start | bytes 40
  55.0 8.2 %copy-start.22 = (s32[32]{0:T(128)S(1)}, s32[32]{0:T(128)}, u32[]{:S(2)}) copy-start(s32[32]{0:T(128)} %table.47) | copy-start | bytes 388
  63.2 3.4 %copy-start.2 = (f32[8,512,512]{2,1,0:T(8,128)S(1)}, f32[8,512,512]{2,1,0:T(8,128)}, u32[]{:S(2)}) copy-start(f32[8,512,512]{2,1,0:T(8,128)} %refs_1_.8) | copy-start | bytes 25165828
  66.6 1.4 copy-start.10
  72.8 3.4 %copy-start.3 = (f32[8,512,512]{2,1,0:T(8,128)S(1)}, f32[8,512,512]{2,1,0:T(8,128)}, u32[]{:S(2)}) copy-start(f32[8,512,512]{2,1,0:T(8,128)} %refs_1_.8) | copy-start | bytes 25165828
  76.2 4.9 %copy-start.8 = (f32[4,512,512]{2,1,0:T(8,128)S(1)}, f32[4,512,512]{2,1,0:T(8,128)}, u32[]{:S(2)}) copy-start(f32[4,512,512]{2,1,0:T(8,128)} %refs_2_.15) | copy-start | bytes 12582916
  82.0 0.8 copy-start.12
  82.8 0.8 copy-start.14
  83.6 0.8 copy-start.16
  84.4 0.8 copy-start.18
  85.7 33.9 %collective-permute-start.10 = (f32[4,192,512]{2,1,0:T(8,128)}, f32[4,192,512]{2,1,0:T(8,128)S(1)}, u32[]{:S(2)}, u32[]{:S(2)}) collective-permute-start(f32[4,192,512]{2,1,0:T(8,128)} %get-tuple-element.77.refs_4_), channel_id=1, source_target_pairs={{0,96},{1,97},{2,98},{3,99},{4,100},{5,101},{6,102},{7,103},{8,104... | collective-permute-start | bytes 4718600 | tf_op jit(solution)/shard_map/ppermute | solution.py:438
  88.1 34.5 %collective-permute-start.8 = (f32[4,192,512]{2,1,0:T(8,128)}, f32[4,192,512]{2,1,0:T(8,128)S(1)}, u32[]{:S(2)}, u32[]{:S(2)}) collective-permute-start(f32[4,192,512]{2,1,0:T(8,128)} %get-tuple-element.81), channel_id=1, source_target_pairs={{0,32},{1,33},{2,34},{3,35},{4,36},{5,37},{6,38},{7,39},{8,40},{9,... | collective-permute-start | bytes 4718600 | tf_op jit(solution)/shard_map/ppermute | solution.py:438
  88.1 40.5 %collective-permute-start.11 = (f32[4,192,512]{2,1,0:T(8,128)}, f32[4,192,512]{2,1,0:T(8,128)S(1)}, u32[]{:S(2)}, u32[]{:S(2)}) collective-permute-start(f32[4,192,512]{2,1,0:T(8,128)} %get-tuple-element.85), channel_id=1, source_target_pairs={{0,4},{1,5},{2,6},{3,7},{4,8},{5,9},{6,10},{7,11},{8,12},{9,13},{1... | collective-permute-start | bytes 4718600 | tf_op jit(solution)/shard_map/ppermute | solution.py:438
  89.1 14.5 %copy-start.21 = (s32[3]{0:T(128)S(1)}, s32[3]{0:T(128)}, u32[]{:S(2)}) copy-start(s32[3]{0:T(128)} %pad_add_fusion.where) | copy-start | bytes 40
  89.1 14.5 %copy-start.23 = (s32[32]{0:T(128)S(1)}, s32[32]{0:T(128)}, u32[]{:S(2)}) copy-start(s32[32]{0:T(128)} %table.47) | copy-start | bytes 388
  89.1 39.6 %collective-permute-start.12 = (f32[4,192,512]{2,1,0:T(8,128)}, f32[4,192,512]{2,1,0:T(8,128)S(1)}, u32[]{:S(2)}, u32[]{:S(2)}) collective-permute-start(f32[4,192,512]{2,1,0:T(8,128)} %get-tuple-element.78.refs_0_), channel_id=1, source_target_pairs={{0,12},{1,13},{2,14},{3,15},{4,0},{5,1},{6,2},{7,3},{8,4},{9,5},{1... | collective-permute-start | bytes 4718600 | tf_op jit(solution)/shard_map/ppermute | solution.py:438
  103.6 2.2 copy-start
  105.7 2.2 copy-start.9
  107.9 1.9 copy-start.11
  109.8 12.8 %copy-start.1 = (f32[16,128,512]{2,1,0:T(8,128)S(1)}, f32[16,128,512]{2,1,0:T(8,128)}, u32[]{:S(2)}) copy-start(f32[16,128,512]{2,1,0:T(8,128)} %get-tuple-element.79.refs_0_) | copy-start | bytes 12582916
  109.8 12.8 %copy-start.6 = (f32[4,192,512]{2,1,0:T(8,128)S(1)}, f32[4,192,512]{2,1,0:T(8,128)}, u32[]{:S(2)}) copy-start(f32[4,192,512]{2,1,0:T(8,128)} %get-tuple-element.80.refs_1_.refs_16_.refs_11_) | copy-start | bytes 4718596
  109.8 12.8 %copy-start.7 = (f32[4,192,512]{2,1,0:T(8,128)S(1)}, f32[4,192,512]{2,1,0:T(8,128)}, u32[]{:S(2)}) copy-start(f32[4,192,512]{2,1,0:T(8,128)} %get-tuple-element.82.refs_6_.refs_11_.refs_16_) | copy-start | bytes 4718596
  122.7 6.0 %copy-start.4 = (f32[4,192,512]{2,1,0:T(8,128)S(1)}, f32[4,192,512]{2,1,0:T(8,128)}, u32[]{:S(2)}) copy-start(f32[4,192,512]{2,1,0:T(8,128)} %get-tuple-element.84.refs_1_.refs_13_.refs_9_) | copy-start | bytes 4718596
  122.7 6.0 %copy-start.5 = (f32[4,192,512]{2,1,0:T(8,128)S(1)}, f32[4,192,512]{2,1,0:T(8,128)}, u32[]{:S(2)}) copy-start(f32[4,192,512]{2,1,0:T(8,128)} %get-tuple-element.86.refs_5_.refs_9_.refs_13_) | copy-start | bytes 4718596
  126.0 29.4 %collective-permute-start.13 = (f32[2,336,512]{2,1,0:T(8,128)}, f32[2,336,512]{2,1,0:T(8,128)S(1)}, u32[]{:S(2)}, u32[]{:S(2)}) collective-permute-start(f32[2,336,512]{2,1,0:T(8,128)} %get-tuple-element.90), channel_id=1, source_target_pairs={{0,4},{1,5},{2,6},{3,7},{4,8},{5,9},{6,10},{7,11},{8,12},{9,13},{1... | collective-permute-start | bytes 4128776 | tf_op jit(solution)/shard_map/ppermute | solution.py:438
  126.6 29.4 %collective-permute-start.14 = (f32[2,336,512]{2,1,0:T(8,128)S(1)}, f32[2,336,512]{2,1,0:T(8,128)S(1)}, u32[]{:S(2)}, u32[]{:S(2)}) collective-permute-start(f32[2,336,512]{2,1,0:T(8,128)S(1)} %get-tuple-element.83.refs_0_), channel_id=1, source_target_pairs={{0,12},{1,13},{2,14},{3,15},{4,0},{5,1},{6,2},{7,3},{8,4},{9,5},{1... | collective-permute-start | bytes 4128776 | tf_op jit(solution)/shard_map/ppermute | solution.py:438
  131.7 27.4 %collective-permute-start.15 = (f32[2,320,512]{2,1,0:T(8,128)}, f32[2,320,512]{2,1,0:T(8,128)S(1)}, u32[]{:S(2)}, u32[]{:S(2)}) collective-permute-start(f32[2,320,512]{2,1,0:T(8,128)} %get-tuple-element.93), channel_id=1, source_target_pairs={{0,32},{1,33},{2,34},{3,35},{4,36},{5,37},{6,38},{7,39},{8,40},{9,... | collective-permute-start | bytes 3932168 | tf_op jit(solution)/shard_map/ppermute | solution.py:438
  131.7 28.0 %collective-permute-start.16 = (f32[2,320,512]{2,1,0:T(8,128)S(1)}, f32[2,320,512]{2,1,0:T(8,128)S(1)}, u32[]{:S(2)}, u32[]{:S(2)}) collective-permute-start(f32[2,320,512]{2,1,0:T(8,128)S(1)} %get-tuple-element.87.refs_0_), channel_id=1, source_target_pairs={{0,96},{1,97},{2,98},{3,99},{4,100},{5,101},{6,102},{7,103},{8,104... | collective-permute-start | bytes 3932168 | tf_op jit(solution)/shard_map/ppermute | solution.py:438
  156.6 12.4 %collective-permute-start.18 = (f32[336,512]{1,0:T(8,128)S(1)}, f32[336,512]{1,0:T(8,128)S(1)}, u32[]{:S(2)}, u32[]{:S(2)}) collective-permute-start(f32[336,512]{1,0:T(8,128)S(1)} %shard_map.72.refs_0_), channel_id=1, source_target_pairs={{0,12},{1,13},{2,14},{3,15},{4,0},{5,1},{6,2},{7,3},{8,4},{9,5},{1... | collective-permute-start | bytes 2064392 | tf_op jit(solution)/shard_map/ppermute | solution.py:438
  158.3 13.0 %collective-permute-start.17 = (f32[336,512]{1,0:T(8,128)S(1)}, f32[336,512]{1,0:T(8,128)S(1)}, u32[]{:S(2)}, u32[]{:S(2)}) collective-permute-start(f32[336,512]{1,0:T(8,128)S(1)} %shard_map.71.refs_0_), channel_id=1, source_target_pairs={{0,4},{1,5},{2,6},{3,7},{4,8},{5,9},{6,10},{7,11},{8,12},{9,13},{1... | collective-permute-start | bytes 2064392 | tf_op jit(solution)/shard_map/ppermute | solution.py:438
  160.4 15.8 %collective-permute-start.22 = (f32[320,512]{1,0:T(8,128)S(1)}, f32[320,512]{1,0:T(8,128)S(1)}, u32[]{:S(2)}, u32[]{:S(2)}) collective-permute-start(f32[320,512]{1,0:T(8,128)S(1)} %shard_map.74.refs_0_), channel_id=1, source_target_pairs={{0,96},{1,97},{2,98},{3,99},{4,100},{5,101},{6,102},{7,103},{8,104... | collective-permute-start | bytes 1966088 | tf_op jit(solution)/shard_map/ppermute | solution.py:438
  162.0 14.2 %collective-permute-start.21 = (f32[320,512]{1,0:T(8,128)S(1)}, f32[320,512]{1,0:T(8,128)S(1)}, u32[]{:S(2)}, u32[]{:S(2)}) collective-permute-start(f32[320,512]{1,0:T(8,128)S(1)} %shard_map.73.refs_0_), channel_id=1, source_target_pairs={{0,32},{1,33},{2,34},{3,35},{4,36},{5,37},{6,38},{7,39},{8,40},{9,... | collective-permute-start | bytes 1966088 | tf_op jit(solution)/shard_map/ppermute | solution.py:438
  172.1 7.2 %collective-permute-start.19 = (f32[72,512]{1,0:T(8,128)S(1)}, f32[72,512]{1,0:T(8,128)S(1)}, u32[]{:S(2)}, u32[]{:S(2)}) collective-permute-start(f32[72,512]{1,0:T(8,128)S(1)} %get-tuple-element.97), channel_id=1, source_target_pairs={{0,32},{1,33},{2,34},{3,35},{4,36},{5,37},{6,38},{7,39},{8,40},{9,... | collective-permute-start | bytes 442376 | tf_op jit(solution)/shard_map/ppermute | solution.py:438
  172.2 7.1 %collective-permute-start.20 = (f32[72,512]{1,0:T(8,128)S(1)}, f32[72,512]{1,0:T(8,128)S(1)}, u32[]{:S(2)}, u32[]{:S(2)}) collective-permute-start(f32[72,512]{1,0:T(8,128)S(1)} %get-tuple-element.96.refs_0_), channel_id=1, source_target_pairs={{0,96},{1,97},{2,98},{3,99},{4,100},{5,101},{6,102},{7,103},{8,104... | collective-permute-start | bytes 442376 | tf_op jit(solution)/shard_map/ppermute | solution.py:438
  174.8 10.6 %copy-start.13 = (bf16[512,512]{1,0:T(8,128)(2,1)S(1)}, bf16[512,512]{1,0:T(8,128)(2,1)}, u32[]{:S(2)}) copy-start(bf16[512,512]{1,0:T(8,128)(2,1)} %copy-done.12) | copy-start | bytes 1572868
  174.8 10.6 %copy-start.15 = (bf16[512,512]{1,0:T(8,128)(2,1)S(1)}, bf16[512,512]{1,0:T(8,128)(2,1)}, u32[]{:S(2)}) copy-start(bf16[512,512]{1,0:T(8,128)(2,1)} %copy-done.14) | copy-start | bytes 1572868
  174.8 9.4 %collective-permute-start.23 = (f32[192,512]{1,0:T(8,128)S(1)}, f32[192,512]{1,0:T(8,128)S(1)}, u32[]{:S(2)}, u32[]{:S(2)}) collective-permute-start(f32[192,512]{1,0:T(8,128)S(1)} %get-tuple-element.102), channel_id=1, source_target_pairs={{0,16},{1,17},{2,18},{3,19},{4,20},{5,21},{6,22},{7,23},{8,24},{9,... | collective-permute-start | bytes 1179656 | tf_op jit(solution)/shard_map/ppermute | solution.py:438
  180.2 11.0 %collective-permute-start.28 = (f32[192,512]{1,0:T(8,128)S(1)}, f32[192,512]{1,0:T(8,128)S(1)}, u32[]{:S(2)}, u32[]{:S(2)}) collective-permute-start(f32[192,512]{1,0:T(8,128)S(1)} %get-tuple-element.111), channel_id=1, source_target_pairs={{0,16},{1,17},{2,18},{3,19},{4,20},{5,21},{6,22},{7,23},{8,24},{9,... | collective-permute-start | bytes 1179656 | tf_op jit(solution)/shard_map/ppermute | solution.py:438
  181.6 5.5 %collective-permute-start.24 = (f32[72,512]{1,0:T(8,128)S(1)}, f32[72,512]{1,0:T(8,128)S(1)}, u32[]{:S(2)}, u32[]{:S(2)}) collective-permute-start(f32[72,512]{1,0:T(8,128)S(1)} %get-tuple-element.104), channel_id=1, source_target_pairs={{0,64},{1,65},{2,66},{3,67},{4,68},{5,69},{6,70},{7,71},{8,72},{9,... | collective-permute-start | bytes 442376 | tf_op jit(solution)/shard_map/ppermute | solution.py:438
  182.8 6.4 %collective-permute-start.25 = (f32[64,512]{1,0:T(8,128)S(1)}, f32[64,512]{1,0:T(8,128)S(1)}, u32[]{:S(2)}, u32[]{:S(2)}) collective-permute-start(f32[64,512]{1,0:T(8,128)S(1)} %get-tuple-element.107), channel_id=1, source_target_pairs={{0,4},{1,5},{2,6},{3,7},{4,8},{5,9},{6,10},{7,11},{8,12},{9,13},{1... | collective-permute-start | bytes 393224 | tf_op jit(solution)/shard_map/ppermute | solution.py:438
  182.8 6.4 %collective-permute-start.26 = (f32[64,512]{1,0:T(8,128)S(1)}, f32[64,512]{1,0:T(8,128)S(1)}, u32[]{:S(2)}, u32[]{:S(2)}) collective-permute-start(f32[64,512]{1,0:T(8,128)S(1)} %get-tuple-element.108), channel_id=1, source_target_pairs={{0,8},{1,9},{2,10},{3,11},{4,12},{5,13},{6,14},{7,15},{8,0},{9,1},... | collective-permute-start | bytes 393224 | tf_op jit(solution)/shard_map/ppermute | solution.py:438
  184.3 5.9 %collective-permute-start.27 = (f32[64,512]{1,0:T(8,128)S(1)}, f32[64,512]{1,0:T(8,128)S(1)}, u32[]{:S(2)}, u32[]{:S(2)}) collective-permute-start(f32[64,512]{1,0:T(8,128)S(1)} %get-tuple-element.98.refs_0_), channel_id=1, source_target_pairs={{0,12},{1,13},{2,14},{3,15},{4,0},{5,1},{6,2},{7,3},{8,4},{9,5},{1... | collective-permute-start | bytes 393224 | tf_op jit(solution)/shard_map/ppermute | solution.py:438
  186.5 4.6 %copy-start.17 = (bf16[512,512]{1,0:T(8,128)(2,1)S(1)}, bf16[512,512]{1,0:T(8,128)(2,1)}, u32[]{:S(2)}) copy-start(bf16[512,512]{1,0:T(8,128)(2,1)} %copy-done.16) | copy-start | bytes 1572868
  186.5 4.6 %copy-start.19 = (bf16[512,512]{1,0:T(8,128)(2,1)S(1)}, bf16[512,512]{1,0:T(8,128)(2,1)}, u32[]{:S(2)}) copy-start(bf16[512,512]{1,0:T(8,128)(2,1)} %copy-done.18) | copy-start | bytes 1572868
  187.7 3.4 %collective-permute-start.29 = (f32[8,512]{1,0:T(8,128)S(1)}, f32[8,512]{1,0:T(8,128)S(1)}, u32[]{:S(2)}, u32[]{:S(2)}) collective-permute-start(f32[8,512]{1,0:T(8,128)S(1)} %get-tuple-element.105.refs_0_.refs_5_), channel_id=1, source_target_pairs={{0,16},{1,17},{2,18},{3,19},{4,20},{5,21},{6,22},{7,23},{8,24},{9,... | collective-permute-start | bytes 49160 | tf_op jit(solution)/shard_map/ppermute | solution.py:438
  194.9 17.5 %collective-permute-start.30 = (f32[512,512]{1,0:T(8,128)S(1)}, f32[512,512]{1,0:T(8,128)S(1)}, u32[]{:S(2)}, u32[]{:S(2)}) collective-permute-start(f32[512,512]{1,0:T(8,128)S(1)} %shard_map.80), channel_id=1, source_target_pairs={{0,16},{1,17},{2,18},{3,19},{4,20},{5,21},{6,22},{7,23},{8,24},{9,... | collective-permute-start | bytes 3145736 | tf_op jit(solution)/shard_map/ppermute | solution.py:438
  195.2 25.6 %collective-permute-start.31 = (f32[512,512]{1,0:T(8,128)S(1)}, f32[512,512]{1,0:T(8,128)S(1)}, u32[]{:S(2)}, u32[]{:S(2)}) collective-permute-start(f32[512,512]{1,0:T(8,128)S(1)} %shard_map.80), channel_id=1, source_target_pairs={{0,18},{1,19},{2,16},{3,17},{4,22},{5,23},{6,20},{7,21},{8,26},{9,... | collective-permute-start | bytes 3145736 | tf_op jit(solution)/shard_map/ppermute | solution.py:438
  212.4 10.9 %collective-permute-start.32 = (f32[512,512]{1,0:T(8,128)S(1)}, f32[512,512]{1,0:T(8,128)S(1)}, u32[]{:S(2)}, u32[]{:S(2)}) collective-permute-start(f32[512,512]{1,0:T(8,128)S(1)} %collective-permute-done.30), channel_id=1, source_target_pairs={{0,1},{1,0},{2,3},{3,2},{4,5},{5,4},{6,7},{7,6},{8,9},{9,8},{10,11... | collective-permute-start | bytes 3145736 | tf_op jit(solution)/shard_map/ppermute | solution.py:438
  220.7 4.3 %collective-permute-start.33 = (f32[512,512]{1,0:T(8,128)S(1)}, f32[512,512]{1,0:T(8,128)}, u32[]{:S(2)}, u32[]{:S(2)}) collective-permute-start(f32[512,512]{1,0:T(8,128)S(1)} %collective-permute-done.31), channel_id=1, source_target_pairs={{0,1},{1,0},{2,3},{3,2},{4,5},{5,4},{6,7},{7,6},{8,9},{9,8},{10,11... | collective-permute-start | bytes 3145736 | tf_op jit(solution)/shard_map/ppermute | solution.py:438
  223.5 2.0 copy-start.24

commit v7 on v6

--- a/solution.py
+++ b/solution.py
@@ -298,14 +298,16 @@
     return order(functools.partial(turn_body, jobs), 1, ins, outs, vmem=TURN)
 
 
-def relay_half_body(table, where, message, term, out):
-    out[...] = message[0] + term[...]
-
-
-def relay_half(order, message, term):
-    rows = message.shape[1]
-    ins = [(message, spec((1, rows, BLK), lambda i, t, w: (0, 0, 0))), (term, whole(term))]
-    return order(relay_half_body, 1, ins, [full(rows, BLK)])[0]
+def relay_half_body(table, where, *refs):
+    for message, term, out in zip(refs[:2], refs[2:4], refs[4:]):
+        out[...] = message[0] + term[...]
+
+
+def relay_half(order, messages, terms):
+    rows = messages[0].shape[1]
+    half = spec((1, rows, BLK), lambda i, t, w: (0, 0, 0))
+    ins = [(m, half) for m in messages] + [(a, whole(a)) for a in terms]
+    return order(relay_half_body, 1, ins, [full(rows, BLK)] * 2)
 
 
 def end_body(stream, table, where, own, forth, back, more_forth, more_back, *outs):
@@ -470,7 +472,7 @@
     *parts_y, mine_y = turn(order, "y", TERMS, *rest)
 
     def follow(stream, messages, parts):
-        more = [relay_half(order, m, p) for m, p in zip(messages, parts)]
+        more = relay_half(order, messages, parts)
         return both(*more, "y" if stream == "x" else "x")
 
     more_x = follow("x", msgs_x, parts_x)

time: 229 us -> 228 us (level)
  waiting for transfers between devices: 65.3 us -> 57.9 us
  starting transfers between devices: 50.9 us -> 57.3 us
    ppermute x34, waiting for transfers between devices: 65.3 us -> 57.9 us  [on_device(): send = lambda value, pairs: lax.ppermute(value, AXES, pairs)]
    ppermute x34, starting transfers between devices: 50.9 us -> 57.3 us  [on_device(): send = lambda value, pairs: lax.ppermute(value, AXES, pairs)]
    pallas_call x24 -> x22, Pallas kernels: 89.3 us -> 88.8 us  [__call__(): pl.pallas_call(inner, out_shape=shapes, grid_spec=pltpu.PrefetchScalarGri...]
  transfers between devices with their start and end apart: 34 -> 34, of which waited for: 15 -> 14; matrix products, arithmetic and copies ran while one was open for 0% -> 0% of each run, Pallas kernels for 33% -> 32%
where the time goes in v7:
time: 228 us; the launch traced here: 227 us
  Pallas kernels  88.8 us (39%)
  waiting for transfers between devices  57.9 us (25%)
  starting transfers between devices  57.3 us (25%)
  local copies, waits for them, and re-layouts  22.3 us (10%)
    pallas_call x22, Pallas kernels, __call__(): pl.pallas_call(inner, out_shape=shapes, grid_spec=pltpu.PrefetchScalarGri...  88.8 us
    ppermute x34, waiting for transfers between devices, on_device(): send = lambda value, pairs: lax.ppermute(value, AXES, pairs)  57.9 us
    ppermute x34, starting transfers between devices, on_device(): send = lambda value, pairs: lax.ppermute(value, AXES, pairs)  57.3 us
    unnamed x58, local copies, waits for them, and re-layouts  19.3 us
  transfers between devices with their start and end apart: 34, of which 14 were waited for; matrix products, arithmetic and copies ran while one was open for 0% of the time, Pallas kernels for 32%

profile of v7, /device:TPU:1, one launch (start us, length us, event | category | flops | bytes accessed | tf_op | source)
XLA Modules:
  0.0 227.2 jit_solution(14772078955559326675)
XLA Ops:
  0.7 12.0 %shard_map.55 = (bf16[2048,768]{1,0:T(8,128)(2,1)}, f32[4,192,512]{2,1,0:T(8,128)}, f32[4,192,512]{2,1,0:T(8,128)}, f32[4,192,512]{2,1,0:T(8,128)}, f32[4,192,512]{2,1,0:T(8,128)}) custom-call(s32[32]{0:T(128)} %table.43, s32[3]{0:T(128)} %pad_add_fusion.where, bf16[768,2048]{1,0:T(8,128)(2,1)} %refs_1_.9, bf16[768,4096]{1,0:T(8,128)(2,1)} %refs_2_.14, ...), custom_call_target="tpu_custom_call" | custom-call | bytes 3690000 | tf_op jit(solution)/shard_map/pallas_call | solution.py:118
  12.6 2.0 collective-permute-start
  14.6 1.1 collective-permute-start.1
  15.8 1.7 collective-permute-start.2
  17.4 1.4 collective-permute-start.3
  18.9 8.2 %shard_map.56.refs_0_ = f32[16,128,512]{2,1,0:T(8,128)} custom-call(s32[32]{0:T(128)} %table.43, s32[3]{0:T(128)} %pad_add_fusion.where, f32[4,192,512]{2,1,0:T(8,128)} %get-tuple-element.63.refs_0_, bf16[2048,768]{1,0:T(8,128)(2,1)} %get-tuple-element.64.refs_1_, bf16[768,4096]{1,0:T(8,128)(2,1)} %refs_2_.14), custom_call_target="tpu_custom_call" | custom-call | bytes 3690000 | tf_op jit(solution)/shard_map/pallas_call | solution.py:118
  27.1 1.6 collective-permute-start.9
  28.7 12.3 %shard_map.57 = (f32[4,192,512]{2,1,0:T(8,128)}, f32[4,192,512]{2,1,0:T(8,128)}, f32[4,192,512]{2,1,0:T(8,128)}, f32[4,192,512]{2,1,0:T(8,128)}, f32[4,192,512]{...) custom-call(s32[32]{0:T(128)} %table.43, s32[3]{0:T(128)} %pad_add_fusion.where, ...), custom_call_target="tpu_custom_call" | custom-call | bytes 3690000 | tf_op jit(solution)/shard_map/pallas_call | solution.py:118
  41.0 8.4 %collective-permute-done.refs_1_ = f32[4,192,512]{2,1,0:T(8,128)S(1)} collective-permute-done((f32[4,192,512]{2,1,0:T(8,128)}, f32[4,192,512]{2,1,0:T(8,128)S(1)}, u32[]{:S(2)}, u32[]{:S(2)}) %collective-permute-start) | collective-permute-done | bytes 1572896 | tf_op jit(solution)/shard_map/ppermute | solution.py:440
  49.4 0.8 collective-permute-start.6
  50.2 1.9 collective-permute-start.7
  52.5 1.6 collective-permute-start.4
  54.1 1.6 collective-permute-start.5
  55.7 8.2 %shard_map.58 = (f32[4,192,512]{2,1,0:T(8,128)}, f32[4,192,512]{2,1,0:T(8,128)}, f32[4,192,512]{2,1,0:T(8,128)}, f32[4,192,512]{2,1,0:T(8,128)}) custom-call(s32[32]{0:T(128)} %table.43, s32[3]{0:T(128)} %pad_add_fusion.where, f32[4,192,512]{2,1,0:T(8,128)} %get-tuple-element.65.refs_0_.refs_8_, f32[4,192,512]{2,1,0:T(8,128)} %copy-done.26, ...), custom_call_target="tpu_custom_call" | custom-call | bytes 3690000 | tf_op jit(solution)/shard_map/pallas_call | solution.py:118
  64.0 3.4 %copy-done.2 = f32[8,512,512]{2,1,0:T(8,128)S(1)} copy-done((f32[8,512,512]{2,1,0:T(8,128)S(1)}, f32[8,512,512]{2,1,0:T(8,128)}, u32[]{:S(2)}) %copy-start.2) | copy-done | bytes 8388632
  67.3 1.4 copy-done.10
  68.7 4.8 %shard_map.59.refs_0_.refs_1_ = f32[4,1,512]{2,1,0:T(1,128)S(1)} custom-call(s32[32]{0:T(128)S(1)} %copy-done.22, s32[3]{0:T(128)S(1)} %copy-done.20, f32[4,192,512]{2,1,0:T(8,128)S(1)} %copy-done.10, bf16[768,4096]{1,0:T(8,128)(2,1)S(1)} %bitcast.30, f32[8,512,512]{2,1,0:T(8,128)S(1)} %copy-done.2), custom_call_target="tpu_custom_call" | custom-call | bytes 3690000 | tf_op jit(solution)/shard_map/pallas_call | solution.py:118
  73.6 3.4 %copy-done.3 = f32[8,512,512]{2,1,0:T(8,128)S(1)} copy-done((f32[8,512,512]{2,1,0:T(8,128)S(1)}, f32[8,512,512]{2,1,0:T(8,128)}, u32[]{:S(2)}) %copy-start.3) | copy-done | bytes 8388632
  76.9 4.8 %shard_map.60.refs_0_.refs_2_ = f32[4,1,512]{2,1,0:T(1,128)S(1)} custom-call(s32[32]{0:T(128)S(1)} %copy-done.22, s32[3]{0:T(128)S(1)} %copy-done.20, f32[4,1,512]{2,1,0:T(1,128)S(1)} %shard_map.59.refs_0_.refs_1_, bf16[768,4096]{1,0:T(8,128)(2,1)S(1)} %bitcast.30, f32[8,512,512]{2,1,0:T(8,128)S(1)} %copy-done.3), custom_call_target="tpu_custom_call" | custom-call | bytes 3690000 | tf_op jit(solution)/shard_map/pallas_call | solution.py:118
  81.8 0.8 shard_map.61
  82.6 0.8 copy-done.12
  83.4 0.8 copy-done.14
  84.3 0.8 copy-done.16
  85.1 0.8 copy-done.18
  85.9 1.1 copy-done.24
  87.4 1.1 collective-permute-start.8
  88.7 1.2 collective-permute-start.11
  89.9 2.0 collective-permute-start.12
  91.9 12.5 %shard_map.64 = (f32[4,192,512]{2,1,0:T(8,128)}, f32[4,192,512]{2,1,0:T(8,128)}, f32[4,192,512]{2,1,0:T(8,128)}, f32[4,192,512]{2,1,0:T(8,128)}, f32[16,128,512]{2,1,0:T(8,128)}) custom-call(s32[32]{0:T(128)} %table.43, s32[3]{0:T(128)} %pad_add_fusion.where, f32[4,192,512]{2,1,0:T(8,128)} %get-tuple-element.82.refs_0_, ...), custom_call_target="tpu_custom_call" | custom-call | bytes 3690000 | tf_op jit(solution)/shard_map/pallas_call | solution.py:118
  104.4 2.2 copy-done
  106.5 2.2 copy-done.9
  108.7 1.9 copy-done.11
  110.6 4.8 %shard_map.65.refs_0_.refs_3_ = f32[4,1,512]{2,1,0:T(1,128)S(1)} custom-call(s32[32]{0:T(128)S(1)} %copy-done.23, s32[3]{0:T(128)S(1)} %copy-done.21, f32[16,128,512]{2,1,0:T(8,128)S(1)} %copy-done, bf16[768,2048]{1,0:T(8,128)(2,1)S(1)} %copy-done.11, f32[4,512,512]{2,1,0:T(8,128)S(1)} %copy-done.9), custom_call_target="tpu_custom_call" | custom-call | bytes 3690000 | tf_op jit(solution)/shard_map/pallas_call | solution.py:118
  115.4 0.7 shard_map.66.refs_0_.refs_5_.refs_10_.refs_15_.refs_20_
  116.1 4.7 %collective-permute-done.10.refs_7_.refs_12_.refs_17_ = f32[4,192,512]{2,1,0:T(8,128)S(1)} collective-permute-done((f32[4,192,512]{2,1,0:T(8,128)}, f32[4,192,512]{2,1,0:T(8,128)S(1)}, u32[]{:S(2)}, u32[]{:S(2)}) %collective-permute-start.10) | collective-permute-done | bytes 1572896 | tf_op jit(solution)/shard_map/ppermute | solution.py:440
  121.5 3.3 %shard_map.67 = (f32[2,336,512]{2,1,0:T(8,128)}, f32[2,336,512]{2,1,0:T(8,128)S(1)}) custom-call(s32[32]{0:T(128)S(1)} %copy-done.23, s32[3]{0:T(128)S(1)} %copy-done.21, f32[4,4,8,512]{3,2,1,0:T(8,128)S(1)} %shard_map.66.refs_0_.refs_5_.refs_10_.refs_15_.refs_20_, f32[4,192,512]{2,1,0:T(8,128)S(1)} %copy-done.6, ...), custom_call_target="tpu_custom_call" | custom-call | bytes 3690000 | tf_op jit(solution)/shard_map/pallas_call | solution.py:118
  124.8 2.5 %collective-permute-start.13 = (f32[2,336,512]{2,1,0:T(8,128)}, f32[2,336,512]{2,1,0:T(8,128)S(1)}, u32[]{:S(2)}, u32[]{:S(2)}) collective-permute-start(f32[2,336,512]{2,1,0:T(8,128)} %get-tuple-element.94), channel_id=1, source_target_pairs={{0,4},{1,5},{2,6},{3,7},{4,8},{5,9},{6,10},{7,11},{8,12},{9,13},{1... | collective-permute-start | bytes 4128776 | tf_op jit(solution)/shard_map/ppermute | solution.py:440
  127.3 1.8 collective-permute-start.14
  129.1 3.0 %shard_map.68 = (f32[2,320,512]{2,1,0:T(8,128)}, f32[2,320,512]{2,1,0:T(8,128)S(1)}) custom-call(s32[32]{0:T(128)S(1)} %copy-done.23, s32[3]{0:T(128)S(1)} %copy-done.21, f32[2,336,512]{2,1,0:T(8,128)S(1)} %get-tuple-element.87.refs_0_, f32[4,192,512]{2,1,0:T(8,128)S(1)} %copy-done.4, f32[4,192,512]{2,1,0:T(8,128)S(1)} %collective-permute-done.11.refs_2_.refs_14_.refs_10_, ...), custom_call_target="tpu_custom_call" | custom-call | bytes 3690000 | tf_op jit(solution)/shard_map/pallas_call | solution.py:118
  132.1 2.7 %collective-permute-start.16 = (f32[2,320,512]{2,1,0:T(8,128)S(1)}, f32[2,320,512]{2,1,0:T(8,128)S(1)}, u32[]{:S(2)}, u32[]{:S(2)}) collective-permute-start(f32[2,320,512]{2,1,0:T(8,128)S(1)} %get-tuple-element.91.refs_0_), channel_id=1, source_target_pairs={{0,96},{1,97},{2,98},{3,99},{4,100},{5,101},{6,102},{7,103},{8,104... | collective-permute-start | bytes 3932168 | tf_op jit(solution)/shard_map/ppermute | solution.py:440
  134.8 2.0 shard_map.69
  136.8 2.0 shard_map.70
  138.8 17.1 %collective-permute-done.13.refs_1_.refs_2_ = f32[2,336,512]{2,1,0:T(8,128)S(1)} collective-permute-done((f32[2,336,512]{2,1,0:T(8,128)}, f32[2,336,512]{2,1,0:T(8,128)S(1)}, u32[]{:S(2)}, u32[]{:S(2)}) %collective-permute-start.13) | collective-permute-done | bytes 1376288 | tf_op jit(solution)/shard_map/ppermute | solution.py:440
  156.8 2.5 %collective-permute-start.18 = (f32[336,512]{1,0:T(8,128)S(1)}, f32[336,512]{1,0:T(8,128)S(1)}, u32[]{:S(2)}, u32[]{:S(2)}) collective-permute-start(f32[336,512]{1,0:T(8,128)S(1)} %get-tuple-element.97.refs_0_), channel_id=1, source_target_pairs={{0,12},{1,13},{2,14},{3,15},{4,0},{5,1},{6,2},{7,3},{8,4},{9,5},{1... | collective-permute-start | bytes 2064392 | tf_op jit(solution)/shard_map/ppermute | solution.py:440
  160.5 2.7 %collective-permute-start.22 = (f32[320,512]{1,0:T(8,128)S(1)}, f32[320,512]{1,0:T(8,128)S(1)}, u32[]{:S(2)}, u32[]{:S(2)}) collective-permute-start(f32[320,512]{1,0:T(8,128)S(1)} %get-tuple-element.101.refs_0_), channel_id=1, source_target_pairs={{0,96},{1,97},{2,98},{3,99},{4,100},{5,101},{6,102},{7,103},{8,104... | collective-permute-start | bytes 1966088 | tf_op jit(solution)/shard_map/ppermute | solution.py:440
  163.1 7.2 %collective-permute-done.17.refs_4_ = f32[336,512]{1,0:T(8,128)S(1)} collective-permute-done((f32[336,512]{1,0:T(8,128)S(1)}, f32[336,512]{1,0:T(8,128)S(1)}, u32[]{:S(2)}, u32[]{:S(2)}) %collective-permute-start.17) | collective-permute-done | bytes 688160 | tf_op jit(solution)/shard_map/ppermute | solution.py:440
  170.4 0.9 shard_map.73
  171.4 2.5 %collective-permute-start.20 = (f32[72,512]{1,0:T(8,128)S(1)}, f32[72,512]{1,0:T(8,128)S(1)}, u32[]{:S(2)}, u32[]{:S(2)}) collective-permute-start(f32[72,512]{1,0:T(8,128)S(1)} %get-tuple-element.103.refs_0_), channel_id=1, source_target_pairs={{0,96},{1,97},{2,98},{3,99},{4,100},{5,101},{6,102},{7,103},{8,104... | collective-permute-start | bytes 442376 | tf_op jit(solution)/shard_map/ppermute | solution.py:440
  174.0 1.2 collective-permute-start.23
  175.1 3.3 %collective-permute-done.19.refs_1_.refs_2_ = f32[72,512]{1,0:T(8,128)S(1)} collective-permute-done((f32[72,512]{1,0:T(8,128)S(1)}, f32[72,512]{1,0:T(8,128)S(1)}, u32[]{:S(2)}, u32[]{:S(2)}) %collective-permute-start.19) | collective-permute-done | bytes 147488 | tf_op jit(solution)/shard_map/ppermute | solution.py:440
  178.4 0.8 shard_map.74
  179.3 1.2 collective-permute-start.28
  180.5 1.2 collective-permute-start.24
  181.7 3.6 %collective-permute-start.26 = (f32[64,512]{1,0:T(8,128)S(1)}, f32[64,512]{1,0:T(8,128)S(1)}, u32[]{:S(2)}, u32[]{:S(2)}) collective-permute-start(f32[64,512]{1,0:T(8,128)S(1)} %get-tuple-element.116), channel_id=1, source_target_pairs={{0,8},{1,9},{2,10},{3,11},{4,12},{5,13},{6,14},{7,15},{8,0},{9,1},... | collective-permute-start | bytes 393224 | tf_op jit(solution)/shard_map/ppermute | solution.py:440
  185.4 1.0 shard_map.75.refs_0_.refs_1_
  187.6 1.4 collective-permute-done.26.refs_5_
  189.4 0.9 shard_map.77.refs_0_.refs_2_
  190.5 3.8 %shard_map.78 = f32[512,512]{1,0:T(8,128)S(1)} custom-call(s32[32]{0:T(128)S(1)} %copy-done.23, s32[3]{0:T(128)S(1)} %copy-done.21, f32[128,512]{1,0:T(8,128)S(1)} %shard_map.77.refs_0_.refs_2_, f32[192,512]{1,0:T(8,128)S(1)} %shard_map.75.refs_0_.refs_1_, f32[128,512]{1,0:T(8,128)S(1)} %shard_map.77.refs_0_.refs_2_, ...), custom_call_target="tpu_custom_call" | custom-call | bytes 3690000 | tf_op jit(solution)/shard_map/pallas_call | solution.py:118
  194.6 3.4 %collective-permute-start.31 = (f32[512,512]{1,0:T(8,128)S(1)}, f32[512,512]{1,0:T(8,128)S(1)}, u32[]{:S(2)}, u32[]{:S(2)}) collective-permute-start(f32[512,512]{1,0:T(8,128)S(1)} %shard_map.78), channel_id=1, source_target_pairs={{0,18},{1,19},{2,16},{3,17},{4,22},{5,23},{6,20},{7,21},{8,26},{9,... | collective-permute-start | bytes 3145736 | tf_op jit(solution)/shard_map/ppermute | solution.py:440
  198.1 12.0 %collective-permute-done.30 = f32[512,512]{1,0:T(8,128)S(1)} collective-permute-done((f32[512,512]{1,0:T(8,128)S(1)}, f32[512,512]{1,0:T(8,128)S(1)}, u32[]{:S(2)}, u32[]{:S(2)}) %collective-permute-start.30) | collective-permute-done | bytes 1048608 | tf_op jit(solution)/shard_map/ppermute | solution.py:440
  210.1 10.0 %collective-permute-start.32 = (f32[512,512]{1,0:T(8,128)S(1)}, f32[512,512]{1,0:T(8,128)S(1)}, u32[]{:S(2)}, u32[]{:S(2)}) collective-permute-start(f32[512,512]{1,0:T(8,128)S(1)} %collective-permute-done.30), channel_id=1, source_target_pairs={{0,1},{1,0},{2,3},{3,2},{4,5},{5,4},{6,7},{7,6},{8,9},{9,8},{10,11... | collective-permute-start | bytes 3145736 | tf_op jit(solution)/shard_map/ppermute | solution.py:440
  220.1 2.1 collective-permute-start.33
  223.0 1.6 collective-permute-done.33
  225.0 2.3 bitcast_dynamic-update-slice_fusion
  (93 shorter events, 7.9 us)
Async XLA Ops:
  12.6 36.8 %collective-permute-start = (f32[4,192,512]{2,1,0:T(8,128)}, f32[4,192,512]{2,1,0:T(8,128)S(1)}, u32[]{:S(2)}, u32[]{:S(2)}) collective-permute-start(f32[4,192,512]{2,1,0:T(8,128)} %get-tuple-element.66), channel_id=1, source_target_pairs={{0,32},{1,33},{2,34},{3,35},{4,36},{5,37},{6,38},{7,39},{8,40},{9,... | collective-permute-start | bytes 4718600 | tf_op jit(solution)/shard_map/ppermute | solution.py:440
  14.6 35.6 %collective-permute-start.1 = (f32[4,192,512]{2,1,0:T(8,128)}, f32[4,192,512]{2,1,0:T(8,128)}, u32[]{:S(2)}, u32[]{:S(2)}) collective-permute-start(f32[4,192,512]{2,1,0:T(8,128)} %get-tuple-element.67), channel_id=1, source_target_pairs={{0,96},{1,97},{2,98},{3,99},{4,100},{5,101},{6,102},{7,103},{8,104... | collective-permute-start | bytes 4718600 | tf_op jit(solution)/shard_map/ppermute | solution.py:440
  15.8 36.8 %collective-permute-start.2 = (f32[4,192,512]{2,1,0:T(8,128)}, f32[4,192,512]{2,1,0:T(8,128)}, u32[]{:S(2)}, u32[]{:S(2)}) collective-permute-start(f32[4,192,512]{2,1,0:T(8,128)} %get-tuple-element.68), channel_id=1, source_target_pairs={{0,4},{1,5},{2,6},{3,7},{4,8},{5,9},{6,10},{7,11},{8,12},{9,13},{1... | collective-permute-start | bytes 4718600 | tf_op jit(solution)/shard_map/ppermute | solution.py:440
  17.4 36.7 %collective-permute-start.3 = (f32[4,192,512]{2,1,0:T(8,128)}, f32[4,192,512]{2,1,0:T(8,128)}, u32[]{:S(2)}, u32[]{:S(2)}) collective-permute-start(f32[4,192,512]{2,1,0:T(8,128)} %get-tuple-element.63.refs_0_), channel_id=1, source_target_pairs={{0,12},{1,13},{2,14},{3,15},{4,0},{5,1},{6,2},{7,3},{8,4},{9,5},{1... | collective-permute-start | bytes 4718600 | tf_op jit(solution)/shard_map/ppermute | solution.py:440
  27.1 94.4 %collective-permute-start.9 = (f32[16,128,512]{2,1,0:T(8,128)}, f32[16,128,512]{2,1,0:T(8,128)}, u32[]{:S(2)}, u32[]{:S(2)}) collective-permute-start(f32[16,128,512]{2,1,0:T(8,128)} %shard_map.56.refs_0_), channel_id=1, source_target_pairs={{0,16},{1,17},{2,18},{3,19},{4,20},{5,21},{6,22},{7,23},{8,24},{9,... | collective-permute-start | bytes 12582920 | tf_op jit(solution)/shard_map/ppermute | solution.py:440
  28.7 35.2 %slice-start = ((s8[6291456]{0:T(1024)(128)(4,1)}), s8[4194304]{0:T(1024)(128)(4,1)S(1)}, s32[]{:S(2)}) async-start(s8[6291456]{0:T(1024)(128)(4,1)} %bitcast.29), calls=%async_computation | async-start | bytes 8388608
  49.4 6.3 %copy-start.26 = (f32[4,192,512]{2,1,0:T(8,128)}, f32[4,192,512]{2,1,0:T(8,128)S(1)}, u32[]{:S(2)}) copy-start(f32[4,192,512]{2,1,0:T(8,128)S(1)} %collective-permute-done.refs_1_) | copy-start | bytes 4718596
  49.4 36.5 %collective-permute-start.6 = (f32[4,192,512]{2,1,0:T(8,128)}, f32[4,192,512]{2,1,0:T(8,128)S(1)}, u32[]{:S(2)}, u32[]{:S(2)}) collective-permute-start(f32[4,192,512]{2,1,0:T(8,128)} %get-tuple-element.78), channel_id=1, source_target_pairs={{0,32},{1,33},{2,34},{3,35},{4,36},{5,37},{6,38},{7,39},{8,40},{9,... | collective-permute-start | bytes 4718600 | tf_op jit(solution)/shard_map/ppermute | solution.py:440
  50.2 35.7 %collective-permute-start.7 = (f32[4,192,512]{2,1,0:T(8,128)}, f32[4,192,512]{2,1,0:T(8,128)}, u32[]{:S(2)}, u32[]{:S(2)}) collective-permute-start(f32[4,192,512]{2,1,0:T(8,128)} %get-tuple-element.79), channel_id=1, source_target_pairs={{0,96},{1,97},{2,98},{3,99},{4,100},{5,101},{6,102},{7,103},{8,104... | collective-permute-start | bytes 4718600 | tf_op jit(solution)/shard_map/ppermute | solution.py:440
  52.5 36.2 %collective-permute-start.4 = (f32[4,192,512]{2,1,0:T(8,128)}, f32[4,192,512]{2,1,0:T(8,128)}, u32[]{:S(2)}, u32[]{:S(2)}) collective-permute-start(f32[4,192,512]{2,1,0:T(8,128)} %get-tuple-element.74), channel_id=1, source_target_pairs={{0,4},{1,5},{2,6},{3,7},{4,8},{5,9},{6,10},{7,11},{8,12},{9,13},{1... | collective-permute-start | bytes 4718600 | tf_op jit(solution)/shard_map/ppermute | solution.py:440
  54.1 34.6 %collective-permute-start.5 = (f32[4,192,512]{2,1,0:T(8,128)}, f32[4,192,512]{2,1,0:T(8,128)}, u32[]{:S(2)}, u32[]{:S(2)}) collective-permute-start(f32[4,192,512]{2,1,0:T(8,128)} %get-tuple-element.75), channel_id=1, source_target_pairs={{0,12},{1,13},{2,14},{3,15},{4,0},{5,1},{6,2},{7,3},{8,4},{9,5},{1... | collective-permute-start | bytes 4718600 | tf_op jit(solution)/shard_map/ppermute | solution.py:440
  55.7 8.2 %slice-start.1 = ((s8[6291456]{0:T(1024)(128)(4,1)}), s8[2097152]{0:T(1024)(128)(4,1)S(1)}, s32[]{:S(2)}) async-start(s8[6291456]{0:T(1024)(128)(4,1)} %bitcast.29), calls=%async_computation.1 | async-start | bytes 4194304
  55.7 8.2 %copy-start.20 = (s32[3]{0:T(128)S(1)}, s32[3]{0:T(128)}, u32[]{:S(2)}) copy-start(s32[3]{0:T(128)} %pad_add_fusion.where) | copy-start | bytes 40
  55.7 8.2 %copy-start.22 = (s32[32]{0:T(128)S(1)}, s32[32]{0:T(128)}, u32[]{:S(2)}) copy-start(s32[32]{0:T(128)} %table.43) | copy-start | bytes 388
  63.9 3.4 %copy-start.2 = (f32[8,512,512]{2,1,0:T(8,128)S(1)}, f32[8,512,512]{2,1,0:T(8,128)}, u32[]{:S(2)}) copy-start(f32[8,512,512]{2,1,0:T(8,128)} %refs_1_.8) | copy-start | bytes 25165828
  67.3 1.4 copy-start.10
  73.6 3.4 %copy-start.3 = (f32[8,512,512]{2,1,0:T(8,128)S(1)}, f32[8,512,512]{2,1,0:T(8,128)}, u32[]{:S(2)}) copy-start(f32[8,512,512]{2,1,0:T(8,128)} %refs_1_.8) | copy-start | bytes 25165828
  76.9 4.8 %copy-start.8 = (f32[4,512,512]{2,1,0:T(8,128)S(1)}, f32[4,512,512]{2,1,0:T(8,128)}, u32[]{:S(2)}) copy-start(f32[4,512,512]{2,1,0:T(8,128)} %refs_2_.15) | copy-start | bytes 12582916
  82.6 0.8 copy-start.12
  83.4 0.8 copy-start.14
  84.3 0.8 copy-start.16
  85.1 0.8 copy-start.18
  85.9 1.1 copy-start.24
  87.0 33.8 %collective-permute-start.10 = (f32[4,192,512]{2,1,0:T(8,128)}, f32[4,192,512]{2,1,0:T(8,128)S(1)}, u32[]{:S(2)}, u32[]{:S(2)}) collective-permute-start(f32[4,192,512]{2,1,0:T(8,128)} %get-tuple-element.81.refs_4_), channel_id=1, source_target_pairs={{0,96},{1,97},{2,98},{3,99},{4,100},{5,101},{6,102},{7,103},{8,104... | collective-permute-start | bytes 4718600 | tf_op jit(solution)/shard_map/ppermute | solution.py:440
  87.4 34.0 %collective-permute-start.8 = (f32[4,192,512]{2,1,0:T(8,128)}, f32[4,192,512]{2,1,0:T(8,128)S(1)}, u32[]{:S(2)}, u32[]{:S(2)}) collective-permute-start(f32[4,192,512]{2,1,0:T(8,128)} %get-tuple-element.85), channel_id=1, source_target_pairs={{0,32},{1,33},{2,34},{3,35},{4,36},{5,37},{6,38},{7,39},{8,40},{9,... | collective-permute-start | bytes 4718600 | tf_op jit(solution)/shard_map/ppermute | solution.py:440
  88.7 40.4 %collective-permute-start.11 = (f32[4,192,512]{2,1,0:T(8,128)}, f32[4,192,512]{2,1,0:T(8,128)S(1)}, u32[]{:S(2)}, u32[]{:S(2)}) collective-permute-start(f32[4,192,512]{2,1,0:T(8,128)} %get-tuple-element.89), channel_id=1, source_target_pairs={{0,4},{1,5},{2,6},{3,7},{4,8},{5,9},{6,10},{7,11},{8,12},{9,13},{1... | collective-permute-start | bytes 4718600 | tf_op jit(solution)/shard_map/ppermute | solution.py:440
  89.9 14.5 %copy-start.21 = (s32[3]{0:T(128)S(1)}, s32[3]{0:T(128)}, u32[]{:S(2)}) copy-start(s32[3]{0:T(128)} %pad_add_fusion.where) | copy-start | bytes 40
  89.9 14.5 %copy-start.23 = (s32[32]{0:T(128)S(1)}, s32[32]{0:T(128)}, u32[]{:S(2)}) copy-start(s32[32]{0:T(128)} %table.43) | copy-start | bytes 388
  89.9 39.2 %collective-permute-start.12 = (f32[4,192,512]{2,1,0:T(8,128)}, f32[4,192,512]{2,1,0:T(8,128)S(1)}, u32[]{:S(2)}, u32[]{:S(2)}) collective-permute-start(f32[4,192,512]{2,1,0:T(8,128)} %get-tuple-element.82.refs_0_), channel_id=1, source_target_pairs={{0,12},{1,13},{2,14},{3,15},{4,0},{5,1},{6,2},{7,3},{8,4},{9,5},{1... | collective-permute-start | bytes 4718600 | tf_op jit(solution)/shard_map/ppermute | solution.py:440
  104.4 2.2 copy-start
  106.5 2.2 copy-start.9
  108.7 1.9 copy-start.11
  110.6 10.9 %copy-start.1 = (f32[16,128,512]{2,1,0:T(8,128)S(1)}, f32[16,128,512]{2,1,0:T(8,128)}, u32[]{:S(2)}) copy-start(f32[16,128,512]{2,1,0:T(8,128)} %get-tuple-element.83.refs_0_) | copy-start | bytes 12582916
  110.6 10.9 %copy-start.6 = (f32[4,192,512]{2,1,0:T(8,128)S(1)}, f32[4,192,512]{2,1,0:T(8,128)}, u32[]{:S(2)}) copy-start(f32[4,192,512]{2,1,0:T(8,128)} %get-tuple-element.84.refs_1_.refs_16_.refs_11_) | copy-start | bytes 4718596
  110.6 10.9 %copy-start.7 = (f32[4,192,512]{2,1,0:T(8,128)S(1)}, f32[4,192,512]{2,1,0:T(8,128)}, u32[]{:S(2)}) copy-start(f32[4,192,512]{2,1,0:T(8,128)} %get-tuple-element.86.refs_6_.refs_11_.refs_16_) | copy-start | bytes 4718596
  121.5 7.6 %copy-start.4 = (f32[4,192,512]{2,1,0:T(8,128)S(1)}, f32[4,192,512]{2,1,0:T(8,128)}, u32[]{:S(2)}) copy-start(f32[4,192,512]{2,1,0:T(8,128)} %get-tuple-element.88.refs_1_.refs_13_.refs_9_) | copy-start | bytes 4718596
  121.5 7.6 %copy-start.5 = (f32[4,192,512]{2,1,0:T(8,128)S(1)}, f32[4,192,512]{2,1,0:T(8,128)}, u32[]{:S(2)}) copy-start(f32[4,192,512]{2,1,0:T(8,128)} %get-tuple-element.90.refs_5_.refs_9_.refs_13_) | copy-start | bytes 4718596
  124.8 31.1 %collective-permute-start.13 = (f32[2,336,512]{2,1,0:T(8,128)}, f32[2,336,512]{2,1,0:T(8,128)S(1)}, u32[]{:S(2)}, u32[]{:S(2)}) collective-permute-start(f32[2,336,512]{2,1,0:T(8,128)} %get-tuple-element.94), channel_id=1, source_target_pairs={{0,4},{1,5},{2,6},{3,7},{4,8},{5,9},{6,10},{7,11},{8,12},{9,13},{1... | collective-permute-start | bytes 4128776 | tf_op jit(solution)/shard_map/ppermute | solution.py:440
  127.3 28.6 %collective-permute-start.14 = (f32[2,336,512]{2,1,0:T(8,128)S(1)}, f32[2,336,512]{2,1,0:T(8,128)S(1)}, u32[]{:S(2)}, u32[]{:S(2)}) collective-permute-start(f32[2,336,512]{2,1,0:T(8,128)S(1)} %get-tuple-element.87.refs_0_), channel_id=1, source_target_pairs={{0,12},{1,13},{2,14},{3,15},{4,0},{5,1},{6,2},{7,3},{8,4},{9,5},{1... | collective-permute-start | bytes 4128776 | tf_op jit(solution)/shard_map/ppermute | solution.py:440
  132.1 27.6 %collective-permute-start.15 = (f32[2,320,512]{2,1,0:T(8,128)}, f32[2,320,512]{2,1,0:T(8,128)S(1)}, u32[]{:S(2)}, u32[]{:S(2)}) collective-permute-start(f32[2,320,512]{2,1,0:T(8,128)} %get-tuple-element.98), channel_id=1, source_target_pairs={{0,32},{1,33},{2,34},{3,35},{4,36},{5,37},{6,38},{7,39},{8,40},{9,... | collective-permute-start | bytes 3932168 | tf_op jit(solution)/shard_map/ppermute | solution.py:440
  132.1 27.6 %collective-permute-start.16 = (f32[2,320,512]{2,1,0:T(8,128)S(1)}, f32[2,320,512]{2,1,0:T(8,128)S(1)}, u32[]{:S(2)}, u32[]{:S(2)}) collective-permute-start(f32[2,320,512]{2,1,0:T(8,128)S(1)} %get-tuple-element.91.refs_0_), channel_id=1, source_target_pairs={{0,96},{1,97},{2,98},{3,99},{4,100},{5,101},{6,102},{7,103},{8,104... | collective-permute-start | bytes 3932168 | tf_op jit(solution)/shard_map/ppermute | solution.py:440
  156.6 13.7 %collective-permute-start.17 = (f32[336,512]{1,0:T(8,128)S(1)}, f32[336,512]{1,0:T(8,128)S(1)}, u32[]{:S(2)}, u32[]{:S(2)}) collective-permute-start(f32[336,512]{1,0:T(8,128)S(1)} %get-tuple-element.102), channel_id=1, source_target_pairs={{0,4},{1,5},{2,6},{3,7},{4,8},{5,9},{6,10},{7,11},{8,12},{9,13},{1... | collective-permute-start | bytes 2064392 | tf_op jit(solution)/shard_map/ppermute | solution.py:440
  156.8 13.5 %collective-permute-start.18 = (f32[336,512]{1,0:T(8,128)S(1)}, f32[336,512]{1,0:T(8,128)S(1)}, u32[]{:S(2)}, u32[]{:S(2)}) collective-permute-start(f32[336,512]{1,0:T(8,128)S(1)} %get-tuple-element.97.refs_0_), channel_id=1, source_target_pairs={{0,12},{1,13},{2,14},{3,15},{4,0},{5,1},{6,2},{7,3},{8,4},{9,5},{1... | collective-permute-start | bytes 2064392 | tf_op jit(solution)/shard_map/ppermute | solution.py:440
  160.4 14.8 %collective-permute-start.21 = (f32[320,512]{1,0:T(8,128)S(1)}, f32[320,512]{1,0:T(8,128)S(1)}, u32[]{:S(2)}, u32[]{:S(2)}) collective-permute-start(f32[320,512]{1,0:T(8,128)S(1)} %get-tuple-element.105), channel_id=1, source_target_pairs={{0,32},{1,33},{2,34},{3,35},{4,36},{5,37},{6,38},{7,39},{8,40},{9,... | collective-permute-start | bytes 1966088 | tf_op jit(solution)/shard_map/ppermute | solution.py:440
  160.5 14.7 %collective-permute-start.22 = (f32[320,512]{1,0:T(8,128)S(1)}, f32[320,512]{1,0:T(8,128)S(1)}, u32[]{:S(2)}, u32[]{:S(2)}) collective-permute-start(f32[320,512]{1,0:T(8,128)S(1)} %get-tuple-element.101.refs_0_), channel_id=1, source_target_pairs={{0,96},{1,97},{2,98},{3,99},{4,100},{5,101},{6,102},{7,103},{8,104... | collective-permute-start | bytes 1966088 | tf_op jit(solution)/shard_map/ppermute | solution.py:440
  171.2 7.2 %collective-permute-start.19 = (f32[72,512]{1,0:T(8,128)S(1)}, f32[72,512]{1,0:T(8,128)S(1)}, u32[]{:S(2)}, u32[]{:S(2)}) collective-permute-start(f32[72,512]{1,0:T(8,128)S(1)} %get-tuple-element.104), channel_id=1, source_target_pairs={{0,32},{1,33},{2,34},{3,35},{4,36},{5,37},{6,38},{7,39},{8,40},{9,... | collective-permute-start | bytes 442376 | tf_op jit(solution)/shard_map/ppermute | solution.py:440
  171.4 7.0 %collective-permute-start.20 = (f32[72,512]{1,0:T(8,128)S(1)}, f32[72,512]{1,0:T(8,128)S(1)}, u32[]{:S(2)}, u32[]{:S(2)}) collective-permute-start(f32[72,512]{1,0:T(8,128)S(1)} %get-tuple-element.103.refs_0_), channel_id=1, source_target_pairs={{0,96},{1,97},{2,98},{3,99},{4,100},{5,101},{6,102},{7,103},{8,104... | collective-permute-start | bytes 442376 | tf_op jit(solution)/shard_map/ppermute | solution.py:440
  174.0 11.4 %copy-start.13 = (bf16[512,512]{1,0:T(8,128)(2,1)S(1)}, bf16[512,512]{1,0:T(8,128)(2,1)}, u32[]{:S(2)}) copy-start(bf16[512,512]{1,0:T(8,128)(2,1)} %copy-done.12) | copy-start | bytes 1572868
  174.0 11.4 %copy-start.15 = (bf16[512,512]{1,0:T(8,128)(2,1)S(1)}, bf16[512,512]{1,0:T(8,128)(2,1)}, u32[]{:S(2)}) copy-start(bf16[512,512]{1,0:T(8,128)(2,1)} %copy-done.14) | copy-start | bytes 1572868
  174.0 11.3 %collective-permute-start.23 = (f32[192,512]{1,0:T(8,128)S(1)}, f32[192,512]{1,0:T(8,128)S(1)}, u32[]{:S(2)}, u32[]{:S(2)}) collective-permute-start(f32[192,512]{1,0:T(8,128)S(1)} %get-tuple-element.110), channel_id=1, source_target_pairs={{0,16},{1,17},{2,18},{3,19},{4,20},{5,21},{6,22},{7,23},{8,24},{9,... | collective-permute-start | bytes 1179656 | tf_op jit(solution)/shard_map/ppermute | solution.py:440
  179.3 11.1 %collective-permute-start.28 = (f32[192,512]{1,0:T(8,128)S(1)}, f32[192,512]{1,0:T(8,128)S(1)}, u32[]{:S(2)}, u32[]{:S(2)}) collective-permute-start(f32[192,512]{1,0:T(8,128)S(1)} %get-tuple-element.119), channel_id=1, source_target_pairs={{0,16},{1,17},{2,18},{3,19},{4,20},{5,21},{6,22},{7,23},{8,24},{9,... | collective-permute-start | bytes 1179656 | tf_op jit(solution)/shard_map/ppermute | solution.py:440
  180.5 5.9 %collective-permute-start.24 = (f32[72,512]{1,0:T(8,128)S(1)}, f32[72,512]{1,0:T(8,128)S(1)}, u32[]{:S(2)}, u32[]{:S(2)}) collective-permute-start(f32[72,512]{1,0:T(8,128)S(1)} %get-tuple-element.112), channel_id=1, source_target_pairs={{0,64},{1,65},{2,66},{3,67},{4,68},{5,69},{6,70},{7,71},{8,72},{9,... | collective-permute-start | bytes 442376 | tf_op jit(solution)/shard_map/ppermute | solution.py:440
  181.7 5.9 %collective-permute-start.25 = (f32[64,512]{1,0:T(8,128)S(1)}, f32[64,512]{1,0:T(8,128)S(1)}, u32[]{:S(2)}, u32[]{:S(2)}) collective-permute-start(f32[64,512]{1,0:T(8,128)S(1)} %get-tuple-element.115), channel_id=1, source_target_pairs={{0,4},{1,5},{2,6},{3,7},{4,8},{5,9},{6,10},{7,11},{8,12},{9,13},{1... | collective-permute-start | bytes 393224 | tf_op jit(solution)/shard_map/ppermute | solution.py:440
  181.7 7.3 %collective-permute-start.26 = (f32[64,512]{1,0:T(8,128)S(1)}, f32[64,512]{1,0:T(8,128)S(1)}, u32[]{:S(2)}, u32[]{:S(2)}) collective-permute-start(f32[64,512]{1,0:T(8,128)S(1)} %get-tuple-element.116), channel_id=1, source_target_pairs={{0,8},{1,9},{2,10},{3,11},{4,12},{5,13},{6,14},{7,15},{8,0},{9,1},... | collective-permute-start | bytes 393224 | tf_op jit(solution)/shard_map/ppermute | solution.py:440
  185.3 4.1 %collective-permute-start.27 = (f32[64,512]{1,0:T(8,128)S(1)}, f32[64,512]{1,0:T(8,128)S(1)}, u32[]{:S(2)}, u32[]{:S(2)}) collective-permute-start(f32[64,512]{1,0:T(8,128)S(1)} %get-tuple-element.106.refs_0_), channel_id=1, source_target_pairs={{0,12},{1,13},{2,14},{3,15},{4,0},{5,1},{6,2},{7,3},{8,4},{9,5},{1... | collective-permute-start | bytes 393224 | tf_op jit(solution)/shard_map/ppermute | solution.py:440
  186.4 4.0 %copy-start.17 = (bf16[512,512]{1,0:T(8,128)(2,1)S(1)}, bf16[512,512]{1,0:T(8,128)(2,1)}, u32[]{:S(2)}) copy-start(bf16[512,512]{1,0:T(8,128)(2,1)} %copy-done.16) | copy-start | bytes 1572868
  186.4 4.0 %copy-start.19 = (bf16[512,512]{1,0:T(8,128)(2,1)S(1)}, bf16[512,512]{1,0:T(8,128)(2,1)}, u32[]{:S(2)}) copy-start(bf16[512,512]{1,0:T(8,128)(2,1)} %copy-done.18) | copy-start | bytes 1572868
  187.0 3.4 %collective-permute-start.29 = (f32[8,512]{1,0:T(8,128)S(1)}, f32[8,512]{1,0:T(8,128)S(1)}, u32[]{:S(2)}, u32[]{:S(2)}) collective-permute-start(f32[8,512]{1,0:T(8,128)S(1)} %get-tuple-element.113.refs_0_.refs_5_), channel_id=1, source_target_pairs={{0,16},{1,17},{2,18},{3,19},{4,20},{5,21},{6,22},{7,23},{8,24},{9,... | collective-permute-start | bytes 49160 | tf_op jit(solution)/shard_map/ppermute | solution.py:440
  194.2 15.8 %collective-permute-start.30 = (f32[512,512]{1,0:T(8,128)S(1)}, f32[512,512]{1,0:T(8,128)S(1)}, u32[]{:S(2)}, u32[]{:S(2)}) collective-permute-start(f32[512,512]{1,0:T(8,128)S(1)} %shard_map.78), channel_id=1, source_target_pairs={{0,16},{1,17},{2,18},{3,19},{4,20},{5,21},{6,22},{7,23},{8,24},{9,... | collective-permute-start | bytes 3145736 | tf_op jit(solution)/shard_map/ppermute | solution.py:440
  194.6 25.4 %collective-permute-start.31 = (f32[512,512]{1,0:T(8,128)S(1)}, f32[512,512]{1,0:T(8,128)S(1)}, u32[]{:S(2)}, u32[]{:S(2)}) collective-permute-start(f32[512,512]{1,0:T(8,128)S(1)} %shard_map.78), channel_id=1, source_target_pairs={{0,18},{1,19},{2,16},{3,17},{4,22},{5,23},{6,20},{7,21},{8,26},{9,... | collective-permute-start | bytes 3145736 | tf_op jit(solution)/shard_map/ppermute | solution.py:440
  210.1 12.8 %collective-permute-start.32 = (f32[512,512]{1,0:T(8,128)S(1)}, f32[512,512]{1,0:T(8,128)S(1)}, u32[]{:S(2)}, u32[]{:S(2)}) collective-permute-start(f32[512,512]{1,0:T(8,128)S(1)} %collective-permute-done.30), channel_id=1, source_target_pairs={{0,1},{1,0},{2,3},{3,2},{4,5},{5,4},{6,7},{7,6},{8,9},{9,8},{10,11... | collective-permute-start | bytes 3145736 | tf_op jit(solution)/shard_map/ppermute | solution.py:440
  220.1 4.5 %collective-permute-start.33 = (f32[512,512]{1,0:T(8,128)S(1)}, f32[512,512]{1,0:T(8,128)}, u32[]{:S(2)}, u32[]{:S(2)}) collective-permute-start(f32[512,512]{1,0:T(8,128)S(1)} %collective-permute-done.31), channel_id=1, source_target_pairs={{0,1},{1,0},{2,3},{3,2},{4,5},{5,4},{6,7},{7,6},{8,9},{9,8},{10,11... | collective-permute-start | bytes 3145736 | tf_op jit(solution)/shard_map/ppermute | solution.py:440
  223.0 2.0 copy-start.25
